TPU v7x, 32 devices: a whole 2x2x4 slice. The times are simulated.
32 devices in a mesh: dp: 16 (over z, y, core), shard: 2 (over x).
Axes of the slice: x: 2, y: 2, z: 4, core: 2. Of those that a mesh axis runs over, the one named last changes fastest.
Arguments:
- tokens: bfloat16 [32768, 512], P(('dp', 'shard')), may hold values from -6 to 6
- segment_ids: int32 [32768], P(('dp', 'shard')), may hold values from 0 to 1024, as said below
- row_counts: int32 [32], P(('dp', 'shard')), may hold values from 512 to 1024, as said below
- global_count: int32 [1], replicated, may hold values from 32768 to 65536
- cotangent: float32 [32768, 512], P(('dp', 'shard')), may hold values from -6 to 6
- query_weight: bfloat16 [512, 512], P('shard'), may hold values from -0.25 to 0.25
- key_weight: bfloat16 [512, 512], P('shard'), may hold values from -0.25 to 0.25
- value_weight: bfloat16 [512, 512], P('shard'), may hold values from -0.25 to 0.25
- output_weight: bfloat16 [512, 512], P('shard'), may hold values from -1 to 1
- inner_weight: bfloat16 [512, 2048], P('shard'), may hold values from -0.25 to 0.25
- outer_weight: bfloat16 [2048, 512], P('shard'), may hold values from -0.125 to 0.125
- attn_gain: bfloat16 [512], P('shard'), may hold values from 0.5 to 1.5
- attn_bias: bfloat16 [512], P('shard'), may hold values from -3 to 3
- feed_gain: bfloat16 [512], P('shard'), may hold values from 0.5 to 1.5
- feed_bias: bfloat16 [512], P('shard'), may hold values from -3 to 3
Outputs:
- mixed: bfloat16 [32768, 512], P(('dp', 'shard'))
- input_grad: float32 [32768, 512], P(('dp', 'shard'))
- query_grad: float32 [512, 512], P('shard')
- key_grad: float32 [512, 512], P('shard')
- value_grad: float32 [512, 512], P('shard')
- output_grad: float32 [512, 512], P('shard')
- inner_grad: float32 [512, 2048], P('shard')
- outer_grad: float32 [2048, 512], P('shard')
- attn_gain_grad: float32 [512], P('shard')
- attn_bias_grad: float32 [512], P('shard')
- feed_gain_grad: float32 [512], P('shard')
- feed_bias_grad: float32 [512], P('shard')
Inputs may be any that keep to these rules, and one draw needn't show every extreme that they name: `segment_ids`: within each row of 1024 tokens the ids never fall; a sentence (a run of one id below 1024) holds 1 to 256 tokens and some sentence holds exactly 256; the tokens from the row's count onward carry the id 1024. `row_counts`: some row uses all 1024 tokens and some row exactly half of them. `global_count`: at least the number of tokens in use over all rows.
All inputs are finite; a program needn't handle non-finite values.
Results may differ from a plain program's by a relative error of at most 0.028.
Values may be sent and summed in bfloat16 or wider, within the bound.
No kernel may reach another device: no remote copies, remote signals or barrier semaphores. Data moves between devices by JAX's collectives and lax.ppermute only.
A program may use at most 256 MiB of HBM per device.

v0:
```python
import functools

import jax
import jax.numpy as jnp
from jax import lax
from jax.experimental import pallas as pl
from jax.experimental.pallas import tpu as pltpu
from jax.sharding import PartitionSpec as P

H = 8
B = 256
CHUNK = 256
norm_eps = 1e-05
masked_score = -1e30
bf16 = jnp.bfloat16
f32 = jnp.float32


def nn(left, right):
    return lax.dot_general(left, right, (((1,), (0,)), ((), ())), preferred_element_type=f32)


def nt(left, right):
    return lax.dot_general(left, right, (((1,), (1,)), ((), ())), preferred_element_type=f32)


def band(block, blocks):
    return max(0, block - 1) * B, min(blocks, block + 2) * B


def key_blocks(block, blocks):
    low, high = band(block, blocks)
    for at in range(low, high, B):
        step = (block * B - at) // B + 1
        yield slice(at, at + B), slice(step * B, (step + 1) * B), slice(at - low, at - low + B)


def query_blocks(block, blocks):
    low, high = band(block, blocks)
    first = low - block * B + B
    return slice(low, high), slice(first, first + high - low)


def fill_bias(seg_ref, bias_ref):
    column = seg_ref[...].T[:, 0:1]
    blocks = bias_ref.shape[0] // B
    for block in range(blocks):
        row = seg_ref[0:1, block * B : (block + 1) * B]
        for keys, cols, _ in key_blocks(block, blocks):
            bias_ref[keys, cols] = jnp.where(column[keys] == row, 0.0, masked_score)


def bias_of(bias_ref, block, blocks):
    parts = [bias_ref[keys, cols] for keys, cols, _ in key_blocks(block, blocks)]
    return jnp.concatenate(parts, axis=0)


def attend_head(head, size, qkv_ref, bias_ref, o_ref, lse_ref):
    blocks = qkv_ref.shape[2] // B
    rows = pl.ds(pl.multiple_of(head * size, size), size)
    key = qkv_ref[1, rows, :].T
    for block in range(blocks):
        low, high = band(block, blocks)
        tile = slice(block * B, (block + 1) * B)
        score = nn(key[low:high], qkv_ref[0, rows, tile]) + bias_of(bias_ref, block, blocks)
        top = jnp.max(score, axis=0, keepdims=True)
        weight = jnp.exp(score - top)
        total = jnp.sum(weight, axis=0, keepdims=True)
        mixed = nn(qkv_ref[2, rows, low:high], weight.astype(bf16)) * (1.0 / total)
        o_ref[rows, tile] = mixed.astype(bf16)
        lse_ref[head, :, tile] = jnp.broadcast_to(top + jnp.log(total), (8, B))


def attend_head_back(
    head, out, size, qkv_ref, o_ref, do_ref, lse_ref, bias_ref, prob_ref, ds_ref, dqkv_ref
):
    length = qkv_ref.shape[2]
    blocks = length // B
    scale = size**-0.5
    rows = pl.ds(pl.multiple_of(head * size, size), size)
    outs = pl.ds(pl.multiple_of(out * size, size), size)
    key_t = qkv_ref[1, rows, :]
    key = key_t.T
    value = qkv_ref[2, rows, :].T
    do_t = do_ref[rows, :]
    delta = jnp.sum(do_t.astype(f32) * o_ref[rows, :].astype(f32), axis=0, keepdims=True)
    for block in range(blocks):
        low, high = band(block, blocks)
        tile = slice(block * B, (block + 1) * B)
        score = nn(key[low:high], qkv_ref[0, rows, tile]) + bias_of(bias_ref, block, blocks)
        prob = jnp.exp(score - lse_ref[head, 0:1, tile])
        prob_low = prob.astype(bf16)
        dprob = nn(value[low:high], do_t[:, tile])
        dscore = (prob * (dprob - delta[:, tile])).astype(bf16)
        for keys, cols, part in key_blocks(block, blocks):
            prob_ref[keys, cols] = prob_low[part]
            ds_ref[keys, cols] = dscore[part]
        dq = nn(key_t[:, low:high], dscore) * scale
        dqkv_ref[0, outs, tile] = dq.astype(bf16)
    query = qkv_ref[0, rows, :].T
    do = do_t.T
    for block in range(blocks):
        tile = slice(block * B, (block + 1) * B)
        queries, cols = query_blocks(block, blocks)
        dv = nn(prob_ref[tile, cols], do[queries])
        dqkv_ref[2, outs, tile] = dv.astype(bf16).T
        dk = nn(ds_ref[tile, cols], query[queries])
        dqkv_ref[1, outs, tile] = dk.astype(bf16).T


def normalize(values):
    center = values - jnp.mean(values, axis=0, keepdims=True)
    spread = jnp.mean(center * center, axis=0, keepdims=True)
    scale = lax.rsqrt(spread + norm_eps)
    return center * scale, scale


def normalize_back(dn, n, scale):
    mean_one = jnp.mean(dn, axis=0, keepdims=True)
    mean_two = jnp.mean(dn * n, axis=0, keepdims=True)
    return (dn - mean_one - n * mean_two) * scale


def gelu_pair(u):
    c0 = 0.7978845608028654
    c1 = c0 * 0.044715
    square = u * u
    t = jnp.tanh(u * (c0 + c1 * square))
    half = 0.5 * u
    cdf = 0.5 + 0.5 * t
    z = u * cdf
    slope = cdf + half * (1.0 - t * t) * (c0 + (3.0 * c1) * square)
    return z, slope


def lanes_sum(values):
    return values[:, :128] + values[:, 128:]


def turn_kernel(x_ref, x_t_ref):
    x_t_ref[...] = x_ref[...].T


def attend_kernel(first, size, x_ref, w_ref, seg_ref, *refs):
    if first:
        w_t_ref = refs[0]
        w_t_ref[...] = w_ref[...].T
        refs = refs[1:]
    else:
        w_t_ref = w_ref
    qkv_ref, o_ref, lse_ref, bias_ref = refs
    rows = o_ref.shape[0]
    fill_bias(seg_ref, bias_ref)
    for at in range(0, x_ref.shape[1], B):
        cols = slice(at, at + B)
        query = nn(w_t_ref[:rows, :], x_ref[:, cols]).astype(bf16)
        qkv_ref[0, :, cols] = query * jnp.asarray(size**-0.5, bf16)
        qkv_ref[1, :, cols] = nn(w_t_ref[rows : 2 * rows, :], x_ref[:, cols]).astype(bf16)
        qkv_ref[2, :, cols] = nn(w_t_ref[2 * rows :, :], x_ref[:, cols]).astype(bf16)

    def two_heads(pair, carry):
        for one in range(2):
            attend_head(2 * pair + one, size, qkv_ref, bias_ref, o_ref, lse_ref)
        return carry

    lax.fori_loop(0, rows // size // 2, two_heads, 0)


def join_heads(oa_ref, ob_ref, o_ref):
    rows = oa_ref.shape[0]
    o_ref[:rows, :] = oa_ref[...]
    o_ref[rows:, :] = ob_ref[...]


def z_copy(z_ref, z_hbm_ref, sem_ref, step):
    slot = step % 2
    there = z_hbm_ref.at[:, step * B : (step + 1) * B]
    return pltpu.make_async_copy(z_ref.at[slot], there, sem_ref.at[slot])


def feed_in_kernel(
    oa_ref,
    ob_ref,
    x_ref,
    wop_ref,
    wi_ref,
    o_ref,
    wo_t_ref,
    wi_t_ref,
    y_ref,
    n1_ref,
    stat_ref,
    yr_ref,
    z_hbm_ref,
    slope_ref,
    z_ref,
    sem_ref,
):
    width, hidden = wi_ref.shape
    join_heads(oa_ref, ob_ref, o_ref)
    wo_t_ref[...] = wop_ref[:, :width].T
    wi_t_ref[...] = wi_ref[...].T
    params = wop_ref[:, width:].astype(f32)
    gain_one, bias_one = params[:, 0:1], params[:, 1:2]
    copies = []
    for at in range(0, x_ref.shape[1], B):
        cols = slice(at, at + B)
        step = at // B
        copies.append(z_copy(z_ref, z_hbm_ref, sem_ref, step))
        if step > 1:
            copies[step - 2].wait()
        h = x_ref[:, cols].astype(f32) + nn(wo_t_ref[...], o_ref[:, cols])
        n1, s1 = normalize(h)
        n1_ref[:, cols] = n1.astype(bf16)
        stat_ref[:, cols] = jnp.broadcast_to(s1, (8, B))
        y = n1 * gain_one + bias_one
        yr_ref[:, cols] = y.astype(bf16)
        y_ref[:, cols] = y
        for f in range(0, hidden, CHUNK):
            u = nn(wi_t_ref[f : f + CHUNK, :], yr_ref[:, cols])
            z, slope = gelu_pair(u)
            z_ref[step % 2, f : f + CHUNK, :] = z.astype(bf16)
            slope_ref[f : f + CHUNK, cols] = slope.astype(bf16)
        copies[step].start()
    for copy in copies[-2:]:
        copy.wait()


def feed_out_kernel(
    y_ref, z_hbm_ref, wop_ref, wu_ref, wu_t_ref, next_ref, x2_ref, n2_ref, stat_ref, z_ref, sem_ref
):
    width = wu_ref.shape[1]
    length = y_ref.shape[1]

    def fetch(step):
        slot = step % 2
        there = z_hbm_ref.at[:, step * B : (step + 1) * B]
        return pltpu.make_async_copy(there, z_ref.at[slot], sem_ref.at[slot])

    copies = [fetch(step) for step in range(length // B)]
    copies[0].start()
    wu_t_ref[...] = wu_ref[...].T
    params = wop_ref[:, width:].astype(f32)
    gain_two, bias_two = params[:, 2:3], params[:, 3:4]
    for at in range(0, y_ref.shape[1], B):
        cols = slice(at, at + B)
        step = at // B
        if step + 1 < len(copies):
            copies[step + 1].start()
        copies[step].wait()
        h2 = y_ref[:, cols] + nn(wu_t_ref[...], z_ref[step % 2])
        n2, s2 = normalize(h2)
        n2_ref[:, cols] = n2.astype(bf16)
        stat_ref[:, cols] = jnp.broadcast_to(s2, (8, B))
        out = n2 * gain_two + bias_two
        next_ref[:, cols] = out
        x2_ref[:, cols] = out.astype(bf16)


def feed_last_kernel(
    oa_ref,
    ob_ref,
    x_ref,
    wop_ref,
    wi_ref,
    wu_ref,
    wo_t_ref,
    wi_t_ref,
    wu_t_ref,
    cot_ref,
    scale_ref,
    o_ref,
    mixed_ref,
    z_hbm_ref,
    du_ref,
    yr_ref,
    dfr_ref,
    dar_ref,
    dh_ref,
    do_ref,
    acc_ref,
    n1_ref,
    z_ref,
    sem_ref,
):
    width, hidden = wi_ref.shape
    join_heads(oa_ref, ob_ref, o_ref)
    params = wop_ref[:, width:].astype(f32)
    gain_one, bias_one = params[:, 0:1], params[:, 1:2]
    gain_two, bias_two = params[:, 2:3], params[:, 3:4]
    acc_ref[...] = jnp.zeros_like(acc_ref)

    copies = []
    for at in range(0, x_ref.shape[1], B):
        cols = slice(at, at + B)
        step = at // B
        slot = step % 2
        copies.append(z_copy(z_ref, z_hbm_ref, sem_ref, step))
        if step > 1:
            copies[step - 2].wait()
        h = x_ref[:, cols] + nn(wo_t_ref[...], o_ref[:, cols])
        n1, s1 = normalize(h)
        n1_ref[slot] = n1
        y = n1 * gain_one + bias_one
        yr_ref[:, cols] = y.astype(bf16)
        dh_ref[:, cols] = y
        for f in range(0, hidden, CHUNK):
            u = nn(wi_t_ref[f : f + CHUNK, :], yr_ref[:, cols])
            z, slope = gelu_pair(u)
            z_ref[slot, f : f + CHUNK, :] = z.astype(bf16)
            du_ref[f : f + CHUNK, cols] = slope.astype(bf16)
        copies[step].start()
        h2 = dh_ref[:, cols] + nn(wu_t_ref[...], z_ref[slot])
        n2, s2 = normalize(h2)
        out = n2 * gain_two + bias_two
        mixed_ref[cols, :] = out.astype(bf16).T
        grad = cot_ref[cols, :].T * scale_ref[0:1, cols]
        acc_ref[2] += lanes_sum(grad * n2)
        acc_ref[3] += lanes_sum(grad)
        dh2 = normalize_back(grad * gain_two, n2, s2)
        dh_ref[:, cols] = dh2
        dfr_ref[:, cols] = dh2.astype(bf16)
        for f in range(0, hidden, CHUNK):
            dz = nn(wu_ref[f : f + CHUNK, :], dfr_ref[:, cols])
            slope = du_ref[f : f + CHUNK, cols].astype(f32)
            du_ref[f : f + CHUNK, cols] = (dz * slope).astype(bf16)
        dy = dh_ref[:, cols] + nn(wi_ref[...], du_ref[:, cols])
        acc_ref[0] += lanes_sum(dy * n1_ref[slot])
        acc_ref[1] += lanes_sum(dy)
        dh = normalize_back(dy * gain_one, n1_ref[slot], s1)
        dh_ref[:, cols] = dh
        dar_ref[:, cols] = dh.astype(bf16)
        do_ref[:, cols] = nn(wop_ref[:, :width], dar_ref[:, cols]).astype(bf16)
    for copy in copies[-2:]:
        copy.wait()


def feed_back_kernel(
    g_ref,
    n1_ref,
    n2_ref,
    stat1_ref,
    stat2_ref,
    slope_ref,
    wop_ref,
    wi_ref,
    wu_ref,
    acc_in_ref,
    dh_ref,
    do_ref,
    du_ref,
    dfr_ref,
    dar_ref,
    acc_ref,
):
    width, hidden = wi_ref.shape
    params = wop_ref[:, width:].astype(f32)
    gain_one, gain_two = params[:, 0:1], params[:, 2:3]
    acc_ref[...] = acc_in_ref[...]
    for at in range(0, g_ref.shape[1], B):
        cols = slice(at, at + B)
        grad = g_ref[:, cols]
        n2 = n2_ref[:, cols].astype(f32)
        acc_ref[2] += lanes_sum(grad * n2)
        acc_ref[3] += lanes_sum(grad)
        dh2 = normalize_back(grad * gain_two, n2, stat2_ref[0:1, cols])
        dh_ref[:, cols] = dh2
        dfr_ref[:, cols] = dh2.astype(bf16)
        for f in range(0, hidden, CHUNK):
            dz = nn(wu_ref[f : f + CHUNK, :], dfr_ref[:, cols])
            slope = slope_ref[f : f + CHUNK, cols].astype(f32)
            du_ref[f : f + CHUNK, cols] = (dz * slope).astype(bf16)
        dy = dh_ref[:, cols] + nn(wi_ref[...], du_ref[:, cols])
        n1 = n1_ref[:, cols].astype(f32)
        acc_ref[0] += lanes_sum(dy * n1)
        acc_ref[1] += lanes_sum(dy)
        dh = normalize_back(dy * gain_one, n1, stat1_ref[0:1, cols])
        dh_ref[:, cols] = dh
        dar_ref[:, cols] = dh.astype(bf16)
        do_ref[:, cols] = nn(wop_ref[:, :width], dar_ref[:, cols]).astype(bf16)


def place(value, first, unit, core, keep_ref, send_ref, cols):
    for at in range(0, value.shape[0], unit):
        block = (first + at) // unit
        rows = slice(block // 2 * unit, block // 2 * unit + unit)
        part = value[at : at + unit]

        @pl.when(core == block % 2)
        def _():
            keep_ref[rows, cols] = part

        @pl.when(core != block % 2)
        def _():
            send_ref[rows, cols] = part


def outer_grad_kernel(
    shards,
    core_ref,
    z1_hbm_ref,
    z2_hbm_ref,
    dfr1_ref,
    dfr2_ref,
    keep_ref,
    send_ref,
    z1_ref,
    z2_ref,
    sem_ref,
):
    core = core_ref[0]
    hidden, width = z1_hbm_ref.shape[0], dfr1_ref.shape[0]
    unit = width // shards // 2
    groups = hidden // width
    per_group = hidden // shards // groups

    def fetch(step, which, hbm_ref, vmem_ref):
        slot = step % 2
        there = hbm_ref.at[step * 256 : (step + 1) * 256]
        return pltpu.make_async_copy(there, vmem_ref.at[slot], sem_ref.at[which, slot])

    copies = [
        (fetch(step, 0, z1_hbm_ref, z1_ref), fetch(step, 1, z2_hbm_ref, z2_ref))
        for step in range(hidden // 256)
    ]
    for copy in copies[0]:
        copy.start()
    for step in range(hidden // 256):
        first = step * 256
        if step + 1 < len(copies):
            for copy in copies[step + 1]:
                copy.start()
        for copy in copies[step]:
            copy.wait()
        slot = step % 2
        dwu = nt(z1_ref[slot], dfr1_ref[...]) + nt(z2_ref[slot], dfr2_ref[...])
        dwu = dwu.astype(bf16)
        for at in range(0, 256, per_group):
            block = (first + at) // per_group
            shard, group = block // groups, block % groups
            cols = slice(group * width, (group + 1) * width)
            rows = dwu[at : at + per_group]
            place(rows, shard * per_group, unit, core, keep_ref, send_ref, cols)


def inner_grad_kernel(
    shards,
    core_ref,
    yr1_ref,
    yr2_ref,
    du1_ref,
    du2_ref,
    o1_ref,
    o2_ref,
    dar1_ref,
    dar2_ref,
    acc_ref,
    keep_ref,
    send_ref,
):
    core = core_ref[0]
    width, hidden = yr1_ref.shape[0], du1_ref.shape[0]
    unit = width // shards // 2
    for first in range(0, hidden, CHUNK):
        part = slice(first, first + CHUNK)
        dwi_t = nt(du1_ref[part, :], yr1_ref[...]) + nt(du2_ref[part, :], yr2_ref[...])
        place(dwi_t.astype(bf16).T, 0, unit, core, keep_ref, send_ref, part)
    for first in range(0, width, CHUNK):
        part = slice(first, first + CHUNK)
        cols = slice(hidden + first, hidden + first + CHUNK)
        dwo = nt(o1_ref[...], dar1_ref[part, :]) + nt(o2_ref[...], dar2_ref[part, :])
        place(dwo.astype(bf16), 0, unit, core, keep_ref, send_ref, cols)
    lane = lax.broadcasted_iota(jnp.int32, (width, 128), 1)
    dpar = jnp.zeros((width, 128), f32)
    for i in range(4):
        dpar = jnp.where(lane == i, jnp.sum(acc_ref[i], axis=1, keepdims=True), dpar)
    last = slice(hidden + width, hidden + width + 128)
    place(dpar.astype(bf16), 0, unit, core, keep_ref, send_ref, last)


def attend_back_kernel(first, size, qkv_ref, o_ref, do_ref, lse_ref, seg_ref, dqkv_ref, *refs):
    bias_ref, prob_ref, ds_ref = refs
    rows = dqkv_ref.shape[1]
    fill_bias(seg_ref, bias_ref)
    here = slice(first, first + rows)

    def two_heads(pair, carry):
        for one in range(2):
            head = 2 * pair + one
            attend_head_back(
                head,
                head,
                size,
                qkv_ref,
                o_ref.at[here],
                do_ref.at[here],
                lse_ref,
                bias_ref,
                prob_ref.at[one],
                ds_ref.at[one],
                dqkv_ref,
            )
        return carry

    lax.fori_loop(0, rows // size // 2, two_heads, 0)


def attend_part_kernel(
    p, size, shards, qkv_ref, o_ref, do_ref, lse_ref, seg_ref, *refs
):
    grads = p % 2 == 1
    if grads:
        core_ref, x1_ref, x2_ref, before_ref, second_ref = refs[:5]
        dqkv_ref, keep_ref, send_ref, bias_ref, prob_ref, ds_ref = refs[5:]
    else:
        dqkv_ref, bias_ref, prob_ref, ds_ref = refs
    fill_bias(seg_ref, bias_ref)
    rows = qkv_ref.shape[1]
    here = slice(p // 2 * rows, (p // 2 + 1) * rows)
    for one in range(2):
        attend_head_back(
            p % 2 * 2 + one,
            one,
            size,
            qkv_ref,
            o_ref.at[here],
            do_ref.at[here],
            lse_ref,
            bias_ref,
            prob_ref.at[one],
            ds_ref.at[one],
            dqkv_ref,
        )
    if not grads:
        return
    core = core_ref[0]
    unit = x1_ref.shape[0] // shards // 2
    for i in range(3):
        joined = jnp.concatenate([before_ref[i], dqkv_ref[i]], axis=0)
        dw = nt(x1_ref[...], joined) + nt(x2_ref[...], second_ref[i])
        place(dw.astype(bf16), 0, unit, core, keep_ref, send_ref, slice(i * rows, (i + 1) * rows))


def input_kernel(turned, wa_ref, wb_ref, dh_ref, *refs):
    parts, grad_ref, join_ref = refs[:-2], refs[-2], refs[-1]
    length = dh_ref.shape[1]
    at = 0
    each = len(parts) // 2
    for group in range(2):
        for i in range(3):
            for part in parts[group * each : (group + 1) * each]:
                rows = part.shape[1]
                join_ref[at : at + rows, :] = part[i]
                at += rows
    half = at // 2
    for at in range(0, length, B):
        cols = slice(at, at + B)
        grad = dh_ref[:, cols] + nn(wa_ref[...], join_ref[:half, cols])
        grad += nn(wb_ref[...], join_ref[half:, cols])
        if turned:
            grad_ref[cols, :] = grad.T
        else:
            grad_ref[:, cols] = grad


VM = pl.BlockSpec(memory_space=pltpu.VMEM)
SM = pl.BlockSpec(memory_space=pltpu.SMEM)
HB = pl.BlockSpec(memory_space=pltpu.HBM)


def call(kernel, outs, scratch, args, specs=None, cost=10, limit=8, far=(), alias={}):
    return pl.pallas_call(
        kernel,
        out_shape=[jax.ShapeDtypeStruct(shape, dtype) for shape, dtype in outs],
        in_specs=specs if specs else [VM] * len(args),
        out_specs=[HB if i in far else VM for i in range(len(outs))],
        scratch_shapes=[pltpu.VMEM(*one) if isinstance(one, tuple) else one for one in scratch],
        input_output_aliases=alias,
        cost_estimate=pl.CostEstimate(
            flops=cost * 1000000000, bytes_accessed=cost * 3000000, transcendentals=0
        ),
        compiler_params=pltpu.CompilerParams(vmem_limit_bytes=limit * 2**20),
    )(*args)


def flip(value, axis, bit):
    count = lax.axis_size(axis)
    return lax.ppermute(value, axis, [(i, i ^ bit) for i in range(count)])


def bit_of(axis, bit):
    return lax.rem(lax.div(lax.axis_index(axis), bit), 2)


def bits_of(axis):
    count = lax.axis_size(axis)
    found = []
    bit = count // 2
    while bit:
        found.append((axis, bit))
        bit //= 2
    return found


def both(bit, mine, other, dim):
    low = jnp.concatenate([mine, other], axis=dim)
    high = jnp.concatenate([other, mine], axis=dim)
    return jnp.where(bit == 0, low, high)


def my_half(block):
    rows = block.shape[0] // 2
    return lax.dynamic_slice_in_dim(block, bit_of("dp", 1) * rows, rows, axis=0)[None]


def my_quarter(block):
    rows = block.shape[0] // 4
    place = 2 * bit_of("dp", 1) + bit_of("dp", 2)
    return lax.dynamic_slice_in_dim(block, place * rows, rows, axis=0)[None]


def over_shards(mine):
    for axis, bit in reversed(bits_of("shard")):
        mine = both(bit_of(axis, bit), mine, flip(mine, axis, bit), 0)
    return mine


def over_cores(mine):
    full = both(bit_of("dp", 1), mine, flip(mine, "dp", 1), 1)
    return full.reshape(-1, mine.shape[-1])


class Sum:
    def __init__(self, keep, send):
        self.labels = bits_of("shard") + bits_of("dp")[:-1]
        self.cols = keep.shape[1]
        self.unit = keep.shape[0] // 2 ** len(self.labels)
        self.keep = keep
        self.sent = send
        self.came = [flip(send, "dp", 1)]
        self.value = None
        self.left = list(self.labels)

    def after(self, other):
        if self.value is None:
            self.keep = tie(self.keep, other)
        else:
            self.value = tie(self.value, other)

    def settle(self):
        if self.value is not None:
            return
        total = self.keep.astype(f32)
        for came in self.came:
            total += came.astype(f32)
        self.value = total.astype(bf16).reshape((2,) * len(self.left) + (self.unit, self.cols))

    def halve(self, axis, bit):
        self.settle()
        dim = self.left.index((axis, bit))
        me = bit_of(axis, bit)
        self.sent = lax.dynamic_index_in_dim(self.value, 1 - me, dim, keepdims=False)
        self.keep = lax.dynamic_index_in_dim(self.value, me, dim, keepdims=False)
        self.came = [flip(self.sent, axis, bit)]
        self.left.remove((axis, bit))
        self.value = None

    def masks(self):
        count = len(self.last)
        for k in range(1, 2**count):
            bits = (bit for i, (_, bit) in enumerate(self.last) if k >> (count - 1 - i) & 1)
            yield k, sum(bits)

    def scatter(self):
        self.settle()
        self.last = list(self.left)
        value = self.value.reshape(-1, self.unit, self.cols)
        me = 0
        for axis, bit in self.last:
            me = 2 * me + bit_of(axis, bit)
        self.keep = lax.dynamic_index_in_dim(value, me, 0, keepdims=False)
        self.came = []
        for k, mask in self.masks():
            send = lax.dynamic_index_in_dim(value, lax.bitwise_xor(me, k), 0, keepdims=False)
            self.came.append(flip(send, "dp", mask))
        self.left = []
        self.value = None

    def collect(self):
        self.settle()
        pieces = [self.value]
        for _, mask in self.masks():
            pieces.append(flip(self.value, "dp", mask))
        for axis, bit in reversed(self.last):
            me = bit_of(axis, bit)
            pairs = zip(pieces[::2], pieces[1::2])
            pieces = [both(me, low[None], high[None], 0) for low, high in pairs]
        self.value = pieces[0]
        self.left = list(self.last)

    def double(self, axis, bit):
        order = [label for label in self.labels if label in self.left or label == (axis, bit)]
        dim = order.index((axis, bit))
        mine = jnp.expand_dims(self.value, dim)
        self.value = both(bit_of(axis, bit), mine, flip(mine, axis, bit), dim)
        self.left = order

    def finish(self):
        self.value = self.value.reshape(-1, self.cols)
        self.other = flip(self.value, "dp", 1)

    def columns(self, first, last):
        mine, other = self.value[:, first:last], self.other[:, first:last]
        return both(bit_of("dp", 1), mine, other, 0).astype(f32)


def join(*sums):
    for one in sums:
        one.settle()
    joined = object.__new__(Sum)
    joined.labels, joined.unit, joined.left = sums[0].labels, sums[0].unit, sums[0].left
    joined.last = getattr(sums[0], "last", None)
    joined.cols = sum(one.cols for one in sums)
    joined.value = jnp.concatenate([one.value for one in sums], axis=-1)
    return joined


def tie_all(*values):
    return lax.optimization_barrier(values)[:-1]


def tie(value, *others):
    return lax.optimization_barrier((value,) + others)[0]


def compute(tokens, seg_rows, scale_rows, cotangent, blocks):
    wa_half, wb_half, wop_half, wi_half, wu_part = blocks
    length, width = tokens.shape
    hidden = wi_half.shape[2]
    size = width // H
    rows = width // 2
    shards = lax.axis_size("shard")
    core = bit_of("dp", 1).reshape(1)
    tall = ((width, length), bf16)
    tall32 = ((width, length), f32)
    wide = ((hidden, length), bf16)
    bias = ((length, 3 * B), f32)
    pair = ((2, length, 3 * B), bf16)
    z_tiles = [((2, hidden, B), bf16), pltpu.SemaphoreType.DMA((2,))]
    heads = [((3, rows, length), bf16), ((rows, length), bf16), ((H // 2, 8, length), f32)]

    wa_mine = over_shards(wa_half)
    wa = over_cores(wa_mine)
    wb_mine, wop_mine, wi_mine, wu_mine = (
        over_shards(tie(part, wa_mine)) for part in (wb_half, wop_half, wi_half, wu_part)
    )
    (x1,) = call(turn_kernel, [tall], [], (tokens,), None, 1)
    first_attend = functools.partial(attend_kernel, True, size)
    turned = [((3 * rows, width), bf16)]
    wa_t, qkv1a, o1a, lse1a = call(first_attend, turned + heads, [bias], (x1, wa, seg_rows), limit=8)
    wb_mine, wop_mine, wi_mine, wu_mine = tie_all(wb_mine, wop_mine, wi_mine, wu_mine, o1a)
    wb = over_cores(wb_mine)
    wi, wop = over_cores(wi_mine), over_cores(wop_mine)
    wu_mine = both(bit_of("dp", 2), wu_mine, flip(wu_mine, "dp", 2), 1)
    seg_b = tie(seg_rows, wi_mine, wop_mine)
    wb_t, qkv1b, o1b, lse1b = call(first_attend, turned + heads, [bias], (x1, wb, seg_b), limit=8)
    o1, wo_t, wi_t, y1, n11, stat11, yr1, z1, slope1 = call(
        feed_in_kernel,
        [tall, ((width, width), bf16), ((hidden, width), bf16), tall32, tall]
        + [((8, length), f32), tall, wide, wide],
        z_tiles,
        (tie(o1a, wu_mine), o1b, x1, wop, wi),
        far=(7,),
    )
    wu = over_cores(wu_mine)
    wu_t, next1, x2, n21, stat12 = call(
        feed_out_kernel,
        [((width, hidden), bf16), tall32, tall, tall, ((8, length), f32)],
        z_tiles,
        (y1, z1, wop, wu),
        [VM, HB, VM, VM],
    )
    attend = functools.partial(attend_kernel, False, size)
    qkv2a, o2a, lse2a = call(attend, heads, [bias], (x2, wa_t, seg_rows), limit=8)
    qkv2b, o2b, lse2b = call(attend, heads, [bias], (x2, wb_t, seg_rows), limit=8)
    o2, mixed, z2, du2, yr2, dfr2, dar2, dh2, do2, acc = call(
        feed_last_kernel,
        [tall, ((length, width), bf16), wide, wide, tall, tall, tall, tall32, tall]
        + [((4, width, 128), f32)],
        [((2, width, B), f32)] + z_tiles,
        (o2a, o2b, next1, wop, wi, wu, wo_t, wi_t, wu_t, cotangent, scale_rows),
        limit=12,
        far=(2,),
    )
    back = [bias, pair, pair]
    dqkv2 = []
    for group, (qkv, lse) in enumerate(((qkv2a, lse2a), (qkv2b, lse2b))):
        kernel = functools.partial(attend_back_kernel, group * rows, size)
        dqkv2 += call(kernel, heads[:1], back, (qkv, o2, do2, lse, seg_rows), limit=14)
    joined = [((3 * width, length), bf16)]
    (grad1,) = call(
        functools.partial(input_kernel, False), [tall32], joined, (wa, wb, dh2, *dqkv2), None, 3, 8
    )
    dh1, do1, du1, dfr1, dar1, acc = call(
        feed_back_kernel,
        [tall32, tall, wide, tall, tall, ((4, width, 128), f32)],
        [],
        (grad1, n11, n21, stat11, stat12, slope1, wop, wi, wu, acc),
        alias={5: 2, 9: 5},
    )
    half = width // 2
    keep_i, send_i = call(
        functools.partial(inner_grad_kernel, shards),
        [((half, hidden + width + 128), bf16)] * 2,
        [],
        (core, yr1, yr2, du1, du2, o1, o2, dar1, dar2, acc),
        [SM] + [VM] * 9,
    )
    inner = Sum(keep_i, send_i)
    keep_u, send_u = call(
        functools.partial(outer_grad_kernel, shards),
        [((half, hidden), bf16)] * 2,
        [((2, 256, length), bf16)] * 2 + [pltpu.SemaphoreType.DMA((2, 2))],
        (tie(core, send_i), z1, z2, dfr1, dfr2),
        [SM, HB, HB, VM, VM],
    )
    parts = []

    def part(p, seg):
        qkv, lse = ((qkv1a, lse1a), (qkv1b, lse1b))[p // 2]
        args = (qkv, o1, do1, lse, seg)
        specs = [VM] * 5
        outs = [((3, 2 * size, length), bf16)]
        if p % 2:
            args += (core, x1, x2, parts[-1], dqkv2[p // 2])
            specs += [SM] + [VM] * 4
            outs += [((half, 3 * rows), bf16)] * 2
        kernel = functools.partial(attend_part_kernel, p, size, shards)
        results = call(kernel, outs, back, args, specs, 15, 14)
        parts.append(results[0])
        return results[1:]

    y_bit = bits_of("dp")[-2]
    x_bits = bits_of("shard")
    inner.after(send_u)
    for label in x_bits:
        inner.halve(*label)
    outer = Sum(keep_u, tie(send_u, inner.sent))
    part(0, tie(seg_rows, inner.sent))
    outer.after(parts[0])
    outer.halve(*y_bit)
    first = Sum(*part(1, tie(seg_rows, outer.sent)))
    inner.after(parts[1])
    inner.halve(*y_bit)
    outer.after(parts[1])
    for label in x_bits:
        outer.halve(*label)
    part(2, tie(seg_rows, inner.sent, outer.sent, first.sent))
    for one in (first, inner, outer):
        one.after(parts[2])
    for label in x_bits:
        first.halve(*label)
    inner.scatter()
    outer.scatter()
    second = Sum(*part(3, tie(seg_rows, inner.keep, outer.keep, first.sent)))
    for one in (first, inner, outer):
        one.after(second.sent)
    feed = join(inner, outer)
    (input_grad,) = call(
        functools.partial(input_kernel, True),
        [((length, width), f32)],
        joined,
        (wa, wb, tie(dh1, second.sent, feed.value), *parts),
        None,
        5,
        10,
    )
    feed.collect()
    for label in x_bits:
        second.halve(*label)
    heads = join(first, second)
    heads.halve(*y_bit)
    feed.after(heads.sent)
    feed.double(*y_bit)
    heads.scatter()
    heads.settle()
    feed.after(heads.value)
    heads.collect()
    feed.finish()
    heads.double(*y_bit)
    heads.finish()
    return mixed, input_grad, feed, heads


def body(
    tokens,
    segment_ids,
    row_counts,
    global_count,
    cotangent,
    query_weight,
    key_weight,
    value_weight,
    output_weight,
    inner_weight,
    outer_weight,
    attn_gain,
    attn_bias,
    feed_gain,
    feed_bias,
):
    length, width = tokens.shape
    hidden = inner_weight.shape[1]
    half = width // 2
    qkv = [my_half(w) for w in (query_weight, key_weight, value_weight)]
    stacked = jnp.stack([attn_gain, attn_bias, feed_gain, feed_bias], axis=1)
    stacked = jnp.pad(stacked, ((0, 0), (0, 124)))
    blocks = (
        jnp.concatenate([w[..., :half] for w in qkv], axis=-1),
        jnp.concatenate([w[..., half:] for w in qkv], axis=-1),
        my_half(jnp.concatenate([output_weight, stacked], axis=1)),
        my_half(inner_weight),
        my_quarter(outer_weight),
    )
    seg_rows = jnp.broadcast_to(segment_ids.astype(f32)[None], (8, length))
    valid = (jnp.arange(length) < row_counts[0]).astype(f32)
    tokens_total = lax.axis_size("dp") * lax.axis_size("shard") * length
    factor = jnp.float32(tokens_total) / global_count[0].astype(f32)
    scale_rows = jnp.broadcast_to((valid * factor)[None], (8, length))
    mixed, input_grad, feed, heads = compute(tokens, seg_rows, scale_rows, cotangent, blocks)
    dqkv = (
        jnp.concatenate([heads.columns(c, c + half) for c in (at, at + 3 * half)], axis=1)
        for at in range(0, 3 * half, half)
    )
    outer = hidden + width + 128
    dwu = [feed.columns(at, at + width) for at in range(outer, outer + hidden, width)]
    dpar = feed.columns(hidden + width, outer)
    return (
        mixed,
        input_grad,
        *dqkv,
        feed.columns(hidden, hidden + width),
        feed.columns(0, hidden),
        jnp.concatenate(dwu, axis=0),
        dpar[:, 0],
        dpar[:, 1],
        dpar[:, 2],
        dpar[:, 3],
    )


def solution(mesh):
    rows = P(("dp", "shard"))
    rows_two = P(("dp", "shard"), None)
    two = P("shard", None)
    one = P("shard")
    in_specs = (rows_two, rows, rows, P(), rows_two) + (two,) * 6 + (one,) * 4
    out_specs = (rows_two, rows_two) + (two,) * 6 + (one,) * 4
    return jax.shard_map(body, mesh=mesh, in_specs=in_specs, out_specs=out_specs, check_vma=False)
```

profile of v0, /device:TPU:0, one launch (start us, length us, event | category | flops | bytes accessed | tf_op | source)
XLA Modules:
  0.0 290.3 jit_solution(11738380629720794226)
XLA Ops:
  5.4 2.9 %collective-permute-start = (bf16[1,128,768]{2,1,0:T(8,128)(2,1)}, bf16[1,128,768]{2,1,0:T(8,128)(2,1)}, u32[]{:S(2)}, u32[]{:S(2)}) collective-permute-start(bf16[1,128,768]{2,1,0:T(8,128)(2,1)} %pad_maximum_fusion), channel_id=1, source_target_pairs={{0,1},{1,0},{2,3},{3,2},{4,5},{5,4},{6,7},{7,6},{8,9},{9,8},{10,11... | collective-permute-start | bytes 589832 | tf_op jit(solution)/shard_map/ppermute | solution.py:588
  22.2 3.0 %collective-permute-done.2 = bf16[1,128,768]{2,1,0:T(8,128)(2,1)} collective-permute-done((bf16[1,128,768]{2,1,0:T(8,128)(2,1)}, bf16[1,128,768]{2,1,0:T(8,128)(2,1)}, u32[]{:S(2)}, u32[]{:S(2)}) %collective-permute-start.2) | collective-permute-done | bytes 196640 | tf_op jit(solution)/shard_map/ppermute | solution.py:588
  25.2 2.0 maximum_select_fusion.12
  27.2 3.6 %collective-permute-done.5 = bf16[1,256,512]{2,1,0:T(8,128)(2,1)} collective-permute-done((bf16[1,256,512]{2,1,0:T(8,128)(2,1)S(1)}, bf16[1,256,512]{2,1,0:T(8,128)(2,1)}, u32[]{:S(2)}, u32[]{:S(2)}) %collective-permute-start.5) | collective-permute-done | bytes 262176 | tf_op jit(solution)/shard_map/ppermute | solution.py:588
  34.1 9.0 %shard_map.239 = (bf16[768,512]{1,0:T(8,128)(2,1)S(1)}, bf16[3,256,1024]{2,1,0:T(8,128)(2,1)S(1)}, bf16[256,1024]{1,0:T(8,128)(2,1)S(1)}, f32[4,8,1024]{2,1,0:T(8,128)S(1)}) custom-call(bf16[512,1024]{1,0:T(8,128)(2,1)S(1)} %shard_map.238.x_ref.refs_1_, bf16[512,768]{1,0:T(8,128)(2,1)S(1)} %bitcast.107, f32[8,1024]{1,0:T(8,128)S(1)} %broadcast_in_dim.21.seg_ref), custom_call_target="tpu_custom_call" | custom-call | flops 10000000000 | bytes 30000000 | tf_op jit(solution)/shard_map/pallas_call | solution.py:572
  52.7 8.7 %shard_map.240 = (bf16[768,512]{1,0:T(8,128)(2,1)S(1)}, bf16[3,256,1024]{2,1,0:T(8,128)(2,1)S(1)}, bf16[256,1024]{1,0:T(8,128)(2,1)S(1)}, f32[4,8,1024]{2,1,0:T(8,128)S(1)}) custom-call(bf16[512,1024]{1,0:T(8,128)(2,1)S(1)} %shard_map.238.x_ref.refs_1_, bf16[512,768]{1,0:T(8,128)(2,1)S(1)} %bitcast.110, f32[8,1024]{1,0:T(8,128)S(1)} %broadcast_in_dim.21.seg_ref), custom_call_target="tpu_custom_call" | custom-call | flops 10000000000 | bytes 30000000 | tf_op jit(solution)/shard_map/pallas_call | solution.py:572
  64.8 10.2 %shard_map.241 = (bf16[512,1024]{1,0:T(8,128)(2,1)S(1)}, bf16[512,512]{1,0:T(8,128)(2,1)S(1)}, bf16[2048,512]{1,0:T(8,128)(2,1)S(1)}, f32[512,1024]{1,0:T(8,128)...) custom-call(bf16[256,1024]{1,0:T(8,128)(2,1)S(1)} %copy-done.33, ...), custom_call_target="tpu_custom_call" | custom-call | flops 10000000000 | bytes 30000000 | tf_op jit(solution)/shard_map/pallas_call | solution.py:572
  77.1 7.4 %shard_map.242 = (bf16[512,2048]{1,0:T(8,128)(2,1)S(1)}, f32[512,1024]{1,0:T(8,128)S(1)}, bf16[512,1024]{1,0:T(8,128)(2,1)S(1)}, bf16[512,1024]{1,0:T(8,128)(2,1)S(1)}, f32[8,1024]{1,0:T(8,128)S(1)}) custom-call(f32[512,1024]{1,0:T(8,128)S(1)} %get-tuple-element.107.y_ref, bf16[2048,1024]{1,0:T(8,128)(2,1)S(1)} %get-tuple-element.108.z_hbm_ref.z1_hbm_ref, ...), custom_call_target="tpu_custom_call" | custom-call | flops 10000000000 | bytes 30000000 | tf_op jit(solution)/shard_map/pallas_call | solution.py:572
  84.5 8.9 %shard_map.244 = (bf16[3,256,1024]{2,1,0:T(8,128)(2,1)S(1)}, bf16[256,1024]{1,0:T(8,128)(2,1)S(1)}, f32[4,8,1024]{2,1,0:T(8,128)S(1)}) custom-call(bf16[512,1024]{1,0:T(8,128)(2,1)S(1)} %get-tuple-element.109.x_ref.refs_2_, bf16[768,512]{1,0:T(8,128)(2,1)S(1)} %get-tuple-element.112.w_ref, f32[8,1024]{1,0:T(8,128)S(1)} %broadcast_in_dim.21.seg_ref), custom_call_target="tpu_custom_call" | custom-call | flops 10000000000 | bytes 30000000 | tf_op jit(solution)/shard_map/pallas_call | solution.py:572
  93.5 8.7 %shard_map.243 = (bf16[3,256,1024]{2,1,0:T(8,128)(2,1)S(1)}, bf16[256,1024]{1,0:T(8,128)(2,1)S(1)}, f32[4,8,1024]{2,1,0:T(8,128)S(1)}) custom-call(bf16[512,1024]{1,0:T(8,128)(2,1)S(1)} %get-tuple-element.109.x_ref.refs_2_, bf16[768,512]{1,0:T(8,128)(2,1)S(1)} %copy-done.31, f32[8,1024]{1,0:T(8,128)S(1)} %broadcast_in_dim.21.seg_ref), custom_call_target="tpu_custom_call" | custom-call | flops 10000000000 | bytes 30000000 | tf_op jit(solution)/shard_map/pallas_call | solution.py:572
  102.2 26.2 %shard_map.245 = (bf16[512,1024]{1,0:T(8,128)(2,1)S(1)}, bf16[1024,512]{1,0:T(8,128)(2,1)}, bf16[2048,1024]{1,0:T(8,128)(2,1)S(1)}, bf16[2048,1024]{1,0:T(8,128)...) custom-call(bf16[256,1024]{1,0:T(8,128)(2,1)S(1)} %get-tuple-element, ...), custom_call_target="tpu_custom_call" | custom-call | flops 10000000000 | bytes 30000000 | tf_op jit(solution)/shard_map/pallas_call | solution.py:572
  128.5 8.7 %shard_map.247.refs_1_.refs_4_ = bf16[3,256,1024]{2,1,0:T(8,128)(2,1)S(1)} custom-call(bf16[3,256,1024]{2,1,0:T(8,128)(2,1)S(1)} %get-tuple-element.124.qkv_ref, bf16[512,1024]{1,0:T(8,128)(2,1)S(1)} %get-tuple-element.121.o_ref.o2_ref, bf16[512,1024]{1,0:T(8,128)(2,1)S(1)} %get-tuple-element.122.do_ref, f32[4,8,1024]{2,1,0:T(8,128)S(1)} %get-tuple-element.125.lse_ref, ...), custom_call_target="tpu_custom_call" | custom-call | flops 10000000000 | bytes 30000000 | tf_op jit(solution)/shard_map/pallas_call | solution.py:572
  137.2 8.8 %shard_map.246.refs_0_.refs_4_ = bf16[3,256,1024]{2,1,0:T(8,128)(2,1)S(1)} custom-call(bf16[3,256,1024]{2,1,0:T(8,128)(2,1)S(1)} %get-tuple-element.120.qkv_ref, bf16[512,1024]{1,0:T(8,128)(2,1)S(1)} %get-tuple-element.121.o_ref.o2_ref, bf16[512,1024]{1,0:T(8,128)(2,1)S(1)} %get-tuple-element.122.do_ref, f32[4,8,1024]{2,1,0:T(8,128)S(1)} %get-tuple-element.123.lse_ref, ...), custom_call_target="tpu_custom_call" | custom-call | flops 10000000000 | bytes 30000000 | tf_op jit(solution)/shard_map/pallas_call | solution.py:572
  147.8 9.7 %shard_map.249 = (f32[512,1024]{1,0:T(8,128)S(1)}, bf16[512,1024]{1,0:T(8,128)(2,1)S(1)}, bf16[2048,1024]{1,0:T(8,128)(2,1)S(1)}, bf16[512,1024]{1,0:T(8,128)(2,...) custom-call(f32[512,1024]{1,0:T(8,128)S(1)} %shard_map.248.g_ref, ...), custom_call_target="tpu_custom_call", output_to_operand_aliasing={{2}: (5, {}), {5}: (9, {})} | custom-call | flops 10000000000 | bytes 30000000 | tf_op jit(solution)/shard_map/pallas_call | solution.py:572
  158.9 10.9 %shard_map.250 = (bf16[256,2688]{1,0:T(8,128)(2,1)S(1)}, bf16[256,2688]{1,0:T(8,128)(2,1)}) custom-call(s32[1]{0:T(128)} %bitcast.13.core_ref.refs_0_, bf16[512,1024]{1,0:T(8,128)(2,1)S(1)} %get-tuple-element.137.yr1_ref, bf16[512,1024]{1,0:T(8,128)(2,1)S(1)} %get-tuple-element.138.yr2_ref, bf16[2048,1024]{1,0:T(8,128)(2,1)S(1)} %get-tuple-element.139.du1_ref, ...), custom_call_target="tpu_custom_call" | custom-call | flops 10000000000 | bytes 30000000 | tf_op jit(solution)/shard_map/pallas_call | solution.py:572
  170.0 2.2 copy-done.13
  172.2 2.2 copy-done.15
  176.9 7.2 %shard_map.251 = (bf16[256,2048]{1,0:T(8,128)(2,1)S(1)}, bf16[256,2048]{1,0:T(8,128)(2,1)S(1)}) custom-call(s32[1]{0:T(128)} %bitcast.13.core_ref.refs_0_, bf16[2048,1024]{1,0:T(8,128)(2,1)S(1)} %copy-done.15, bf16[2048,1024]{1,0:T(8,128)(2,1)S(1)} %copy-done.13, bf16[512,1024]{1,0:T(8,128)(2,1)S(1)} %copy-done.23, bf16[512,1024]{1,0:T(8,128)(2,1)S(1)} %copy-done.19), custom_call_target="tpu_custom_call" | custom-call | flops 10000000000 | bytes 30000000 | tf_op jit(solution)/shard_map/pallas_call | solution.py:572
  187.9 4.3 %shard_map.252.refs_3_.refs_0_ = bf16[3,128,1024]{2,1,0:T(8,128)(2,1)S(1)} custom-call(bf16[3,256,1024]{2,1,0:T(8,128)(2,1)S(1)} %copy-done.29, bf16[512,1024]{1,0:T(8,128)(2,1)S(1)} %copy-done.17, bf16[512,1024]{1,0:T(8,128)(2,1)S(1)} %copy-done.21, f32[4,8,1024]{2,1,0:T(8,128)S(1)} %copy-done.37, f32[8,1024]{1,0:T(8,128)S(1)} %broadcast_in_dim.21.seg_ref), custom_call_target="tpu_custom_call" | custom-call | flops 15000000512 | bytes 45000000 | tf_op jit(solution)/shard_map/pallas_call | solution.py:572
  194.2 8.3 %shard_map.253 = (bf16[3,128,1024]{2,1,0:T(8,128)(2,1)S(1)}, bf16[256,768]{1,0:T(8,128)(2,1)S(1)}, bf16[256,768]{1,0:T(8,128)(2,1)S(1)}) custom-call(bf16[3,256,1024]{2,1,0:T(8,128)(2,1)S(1)} %copy-done.29, bf16[512,1024]{1,0:T(8,128)(2,1)S(1)} %copy-done.17, bf16[512,1024]{1,0:T(8,128)(2,1)S(1)} %copy-done.21, f32[4,8,1024]{2,1,0:T(8,128)S(1)} %copy-done.37, ...), custom_call_target="tpu_custom_call" | custom-call | flops 15000000512 | bytes 45000000 | tf_op jit(solution)/shard_map/pallas_call | solution.py:572
  205.1 2.4 collective-permute-done.14
  208.8 4.3 %shard_map.254.refs_3_.refs_2_ = bf16[3,128,1024]{2,1,0:T(8,128)(2,1)S(1)} custom-call(bf16[3,256,1024]{2,1,0:T(8,128)(2,1)S(1)} %copy-done.27, bf16[512,1024]{1,0:T(8,128)(2,1)S(1)} %copy-done.17, bf16[512,1024]{1,0:T(8,128)(2,1)S(1)} %copy-done.21, f32[4,8,1024]{2,1,0:T(8,128)S(1)} %copy-done.35, f32[8,1024]{1,0:T(8,128)S(1)} %broadcast_in_dim.21.seg_ref), custom_call_target="tpu_custom_call" | custom-call | flops 15000000512 | bytes 45000000 | tf_op jit(solution)/shard_map/pallas_call | solution.py:572
  216.2 2.6 collective-permute-start.19
  220.4 8.3 %shard_map.255 = (bf16[3,128,1024]{2,1,0:T(8,128)(2,1)S(1)}, bf16[256,768]{1,0:T(8,128)(2,1)S(1)}, bf16[256,768]{1,0:T(8,128)(2,1)S(1)}) custom-call(bf16[3,256,1024]{2,1,0:T(8,128)(2,1)S(1)} %copy-done.27, bf16[512,1024]{1,0:T(8,128)(2,1)S(1)} %copy-done.17, bf16[512,1024]{1,0:T(8,128)(2,1)S(1)} %copy-done.21, f32[4,8,1024]{2,1,0:T(8,128)S(1)} %copy-done.35, ...), custom_call_target="tpu_custom_call" | custom-call | flops 15000000512 | bytes 45000000 | tf_op jit(solution)/shard_map/pallas_call | solution.py:572
  229.6 3.5 %collective-permute-start.22 = (bf16[16,2048]{1,0:T(8,128)(2,1)S(1)}, bf16[16,2048]{1,0:T(8,128)(2,1)S(1)}, u32[]{:S(2)}, u32[]{:S(2)}) collective-permute-start(bf16[16,2048]{1,0:T(8,128)(2,1)S(1)} %get-tuple-element.220), channel_id=1, source_target_pairs={{0,16},{2,18},{4,20},{6,22},{8,24},{10,26},{12,28},{14,30},{16,0},... | collective-permute-start | bytes 196616 | tf_op jit(solution)/shard_map/ppermute | solution.py:588
  233.4 3.8 %collective-permute-done.22 = bf16[16,2048]{1,0:T(8,128)(2,1)S(1)} collective-permute-done((bf16[16,2048]{1,0:T(8,128)(2,1)S(1)}, bf16[16,2048]{1,0:T(8,128)(2,1)S(1)}, u32[]{:S(2)}, u32[]{:S(2)}) %collective-permute-start.22) | collective-permute-done | bytes 65568 | tf_op jit(solution)/shard_map/ppermute | solution.py:588
  247.7 3.2 %collective-permute-done.27 = bf16[2,2,16,1536]{3,2,1,0:T(8,128)(2,1)S(1)} collective-permute-done((bf16[2,2,16,1536]{3,2,1,0:T(8,128)(2,1)S(1)}, bf16[2,2,16,1536]{3,2,1,0:T(8,128)(2,1)S(1)}, u32[]{:S(2)}, u32[]{:S(2)}) %collective-permute-start.27) | collective-permute-done | bytes 196640 | tf_op jit(solution)/shard_map/ppermute | solution.py:588
  256.1 4.8 %collective-permute-done.29 = bf16[16,1536]{1,0:T(8,128)(2,1)S(1)} collective-permute-done((bf16[16,1536]{1,0:T(8,128)(2,1)S(1)}, bf16[16,1536]{1,0:T(8,128)(2,1)S(1)}, u32[]{:S(2)}, u32[]{:S(2)}) %collective-permute-start.29) | collective-permute-done | bytes 49184 | tf_op jit(solution)/shard_map/ppermute | solution.py:588
  267.0 2.2 collective-permute-done.32
  269.2 2.1 collective-permute-done.33
  272.1 3.3 %shard_map.256 = f32[1024,512]{1,0:T(8,128)} custom-call(bf16[512,768]{1,0:T(8,128)(2,1)S(1)} %bitcast.109, bf16[512,768]{1,0:T(8,128)(2,1)S(1)} %bitcast.112, f32[512,1024]{1,0:T(8,128)S(1)} %copy-done.11, bf16[3,128,1024]{2,1,0:T(8,128)(2,1)S(1)} %shard_map.252.refs_3_.refs_0_, bf16[3,128,1024]{2,1,0:T(8,128)(2,1)S(1)} %get-tuple-element.159.refs_1_, ...), custom_call_target="tpu_custom_call" | custom-call | flops 5000000000 | bytes 15000000 | tf_op jit(solution)/shard_map/pallas_call | solution.py:572
  275.5 4.6 %collective-permute-done.34 = bf16[2,2,1,16,1536]{4,3,2,1,0:T(8,128)(2,1)S(1)} collective-permute-done((bf16[2,2,1,16,1536]{4,3,2,1,0:T(8,128)(2,1)S(1)}, bf16[2,2,1,16,1536]{4,3,2,1,0:T(8,128)(2,1)S(1)}, u32[]{:S(2)}, u32[]{:S(2)}) %collective-permute-start.34) | collective-permute-done | bytes 196640 | tf_op jit(solution)/shard_map/ppermute | solution.py:588
  (257 shorter events, 88.6 us)
Async XLA Ops:
  5.4 8.2 %collective-permute-start = (bf16[1,128,768]{2,1,0:T(8,128)(2,1)}, bf16[1,128,768]{2,1,0:T(8,128)(2,1)}, u32[]{:S(2)}, u32[]{:S(2)}) collective-permute-start(bf16[1,128,768]{2,1,0:T(8,128)(2,1)} %pad_maximum_fusion), channel_id=1, source_target_pairs={{0,1},{1,0},{2,3},{3,2},{4,5},{5,4},{6,7},{7,6},{8,9},{9,8},{10,11... | collective-permute-start | bytes 589832 | tf_op jit(solution)/shard_map/ppermute | solution.py:588
  17.2 15.5 %collective-permute-start.1 = (bf16[2,128,768]{2,1,0:T(8,128)(2,1)S(1)}, bf16[2,128,768]{2,1,0:T(8,128)(2,1)}, u32[]{:S(2)}, u32[]{:S(2)}) collective-permute-start(bf16[2,128,768]{2,1,0:T(8,128)(2,1)S(1)} %maximum_select_fusion.11), channel_id=1, source_target_pairs={{0,2},{2,0},{4,6},{6,4},{8,10},{10,8},{12,14},{14,12},{16,18},{18,... | collective-permute-start | bytes 1179656 | tf_op jit(solution)/shard_map/ppermute | solution.py:588
  17.2 8.0 %collective-permute-start.2 = (bf16[1,128,768]{2,1,0:T(8,128)(2,1)}, bf16[1,128,768]{2,1,0:T(8,128)(2,1)}, u32[]{:S(2)}, u32[]{:S(2)}) collective-permute-start(bf16[1,128,768]{2,1,0:T(8,128)(2,1)} %pad_maximum_fusion.1), channel_id=1, source_target_pairs={{0,1},{1,0},{2,3},{3,2},{4,5},{5,4},{6,7},{7,6},{8,9},{9,8},{10,11... | collective-permute-start | bytes 589832 | tf_op jit(solution)/shard_map/ppermute | solution.py:588
  17.5 13.3 %collective-permute-start.5 = (bf16[1,256,512]{2,1,0:T(8,128)(2,1)S(1)}, bf16[1,256,512]{2,1,0:T(8,128)(2,1)}, u32[]{:S(2)}, u32[]{:S(2)}) collective-permute-start(bf16[1,256,512]{2,1,0:T(8,128)(2,1)S(1)} %dynamic-slice_bitcast_fusion.9), channel_id=1, source_target_pairs={{0,1},{1,0},{2,3},{3,2},{4,5},{5,4},{6,7},{7,6},{8,9},{9,8},{10,11... | collective-permute-start | bytes 786440 | tf_op jit(solution)/shard_map/ppermute | solution.py:588
  19.6 25.4 %collective-permute-start.4 = (bf16[1,128,2048]{2,1,0:T(8,128)(2,1)S(1)}, bf16[1,128,2048]{2,1,0:T(8,128)(2,1)S(1)}, u32[]{:S(2)}, u32[]{:S(2)}) collective-permute-start(bf16[1,128,2048]{2,1,0:T(8,128)(2,1)S(1)} %dynamic-slice_bitcast_fusion.4), channel_id=1, source_target_pairs={{0,1},{1,0},{2,3},{3,2},{4,5},{5,4},{6,7},{7,6},{8,9},{9,8},{10,11... | collective-permute-start | bytes 1572872 | tf_op jit(solution)/shard_map/ppermute | solution.py:588
  48.2 15.2 %collective-permute-start.9 = (bf16[2,128,2048]{2,1,0:T(8,128)(2,1)}, bf16[2,128,2048]{2,1,0:T(8,128)(2,1)S(1)}, u32[]{:S(2)}, u32[]{:S(2)}) collective-permute-start(bf16[2,128,2048]{2,1,0:T(8,128)(2,1)} %maximum_select_fusion.3), channel_id=1, source_target_pairs={{0,2},{2,0},{4,6},{6,4},{8,10},{10,8},{12,14},{14,12},{16,18},{18,... | collective-permute-start | bytes 3145736 | tf_op jit(solution)/shard_map/ppermute | solution.py:588
  48.2 14.6 %collective-permute-start.6 = (bf16[2,256,512]{2,1,0:T(8,128)(2,1)}, bf16[2,256,512]{2,1,0:T(8,128)(2,1)S(1)}, u32[]{:S(2)}, u32[]{:S(2)}) collective-permute-start(bf16[2,256,512]{2,1,0:T(8,128)(2,1)} %maximum_select_fusion.10), channel_id=1, source_target_pairs={{0,4},{2,6},{4,0},{6,2},{8,12},{10,14},{12,8},{14,10},{16,20},{18,... | collective-permute-start | bytes 1572872 | tf_op jit(solution)/shard_map/ppermute | solution.py:588
  63.2 11.9 %collective-permute-start.10 = (bf16[2,512,512]{2,1,0:T(8,128)(2,1)S(1)}, bf16[2,512,512]{2,1,0:T(8,128)(2,1)S(1)}, u32[]{:S(2)}, u32[]{:S(2)}) collective-permute-start(bf16[2,512,512]{2,1,0:T(8,128)(2,1)S(1)} %maximum_select_fusion.4), channel_id=1, source_target_pairs={{0,2},{2,0},{4,6},{6,4},{8,10},{10,8},{12,14},{14,12},{16,18},{18,... | collective-permute-start | bytes 3145736 | tf_op jit(solution)/shard_map/ppermute | solution.py:588
  169.9 14.2 %collective-permute-start.11 = (bf16[256,2688]{1,0:T(8,128)(2,1)}, bf16[256,2688]{1,0:T(8,128)(2,1)}, u32[]{:S(2)}, u32[]{:S(2)}) collective-permute-start(bf16[256,2688]{1,0:T(8,128)(2,1)} %get-tuple-element.145), channel_id=1, source_target_pairs={{0,2},{2,0},{4,6},{6,4},{8,10},{10,8},{12,14},{14,12},{16,18},{18,... | collective-permute-start | bytes 4128776 | tf_op jit(solution)/shard_map/ppermute | solution.py:588
  186.0 17.7 %collective-permute-start.13 = (bf16[2,2,2,16,2688]{4,3,2,1,0:T(8,128)(2,1)S(1)}, bf16[2,2,2,16,2688]{4,3,2,1,0:T(8,128)(2,1)S(1)}, u32[]{:S(2)}, u32[]{:S(2)}) collective-permute-start(bf16[2,2,2,16,2688]{4,3,2,1,0:T(8,128)(2,1)S(1)} %get-tuple-element.183), channel_id=1, source_target_pairs={{0,1},{1,0},{2,3},{3,2},{4,5},{5,4},{6,7},{7,6},{8,9},{9,8},{10,11... | collective-permute-start | bytes 2064392 | tf_op jit(solution)/shard_map/ppermute | solution.py:588
  192.7 14.8 %collective-permute-start.14 = (bf16[2,2,2,16,2048]{4,3,2,1,0:T(8,128)(2,1)S(1)}, bf16[2,2,2,16,2048]{4,3,2,1,0:T(8,128)(2,1)S(1)}, u32[]{:S(2)}, u32[]{:S(2)}) collective-permute-start(bf16[2,2,2,16,2048]{4,3,2,1,0:T(8,128)(2,1)S(1)} %get-tuple-element.195), channel_id=1, source_target_pairs={{0,4},{2,6},{4,0},{6,2},{8,12},{10,14},{12,8},{14,10},{16,20},{18,... | collective-permute-start | bytes 1572872 | tf_op jit(solution)/shard_map/ppermute | solution.py:588
  202.5 16.6 %collective-permute-start.17 = (bf16[256,768]{1,0:T(8,128)(2,1)S(1)}, bf16[256,768]{1,0:T(8,128)(2,1)S(1)}, u32[]{:S(2)}, u32[]{:S(2)}) collective-permute-start(bf16[256,768]{1,0:T(8,128)(2,1)S(1)} %get-tuple-element.162), channel_id=1, source_target_pairs={{0,2},{2,0},{4,6},{6,4},{8,10},{10,8},{12,14},{14,12},{16,18},{18,... | collective-permute-start | bytes 1179656 | tf_op jit(solution)/shard_map/ppermute | solution.py:588
  204.0 10.5 %collective-permute-start.15 = (bf16[2,2,16,2688]{3,2,1,0:T(8,128)(2,1)S(1)}, bf16[2,2,16,2688]{3,2,1,0:T(8,128)(2,1)S(1)}, u32[]{:S(2)}, u32[]{:S(2)}) collective-permute-start(bf16[2,2,16,2688]{3,2,1,0:T(8,128)(2,1)S(1)} %get-tuple-element.197), channel_id=1, source_target_pairs={{0,4},{2,6},{4,0},{6,2},{8,12},{10,14},{12,8},{14,10},{16,20},{18,... | collective-permute-start | bytes 1032200 | tf_op jit(solution)/shard_map/ppermute | solution.py:588
  207.7 12.6 %collective-permute-start.16 = (bf16[2,2,16,2048]{3,2,1,0:T(8,128)(2,1)S(1)}, bf16[2,2,16,2048]{3,2,1,0:T(8,128)(2,1)S(1)}, u32[]{:S(2)}, u32[]{:S(2)}) collective-permute-start(bf16[2,2,16,2048]{3,2,1,0:T(8,128)(2,1)S(1)} %get-tuple-element.199), channel_id=1, source_target_pairs={{0,1},{1,0},{2,3},{3,2},{4,5},{5,4},{6,7},{7,6},{8,9},{9,8},{10,11... | collective-permute-start | bytes 786440 | tf_op jit(solution)/shard_map/ppermute | solution.py:588
  214.6 14.2 %collective-permute-start.18 = (bf16[16,2688]{1,0:T(8,128)(2,1)S(1)}, bf16[16,2688]{1,0:T(8,128)(2,1)S(1)}, u32[]{:S(2)}, u32[]{:S(2)}) collective-permute-start(bf16[16,2688]{1,0:T(8,128)(2,1)S(1)} %get-tuple-element.214), channel_id=1, source_target_pairs={{0,8},{2,10},{4,12},{6,14},{8,0},{10,2},{12,4},{14,6},{16,24},{18,... | collective-permute-start | bytes 258056 | tf_op jit(solution)/shard_map/ppermute | solution.py:588
  216.2 13.4 %collective-permute-start.19 = (bf16[16,2688]{1,0:T(8,128)(2,1)S(1)}, bf16[16,2688]{1,0:T(8,128)(2,1)S(1)}, u32[]{:S(2)}, u32[]{:S(2)}) collective-permute-start(bf16[16,2688]{1,0:T(8,128)(2,1)S(1)} %get-tuple-element.216), channel_id=1, source_target_pairs={{0,16},{2,18},{4,20},{6,22},{8,24},{10,26},{12,28},{14,30},{16,0},... | collective-permute-start | bytes 258056 | tf_op jit(solution)/shard_map/ppermute | solution.py:588
  218.7 14.4 %collective-permute-start.20 = (bf16[16,2688]{1,0:T(8,128)(2,1)S(1)}, bf16[16,2688]{1,0:T(8,128)(2,1)S(1)}, u32[]{:S(2)}, u32[]{:S(2)}) collective-permute-start(bf16[16,2688]{1,0:T(8,128)(2,1)S(1)} %get-tuple-element.215), channel_id=1, source_target_pairs={{0,24},{2,26},{4,28},{6,30},{8,16},{10,18},{12,20},{14,22},{16,8},... | collective-permute-start | bytes 258056 | tf_op jit(solution)/shard_map/ppermute | solution.py:588
  219.2 14.1 %collective-permute-start.24 = (bf16[2,2,2,16,768]{4,3,2,1,0:T(8,128)(2,1)S(1)}, bf16[2,2,2,16,768]{4,3,2,1,0:T(8,128)(2,1)S(1)}, u32[]{:S(2)}, u32[]{:S(2)}) collective-permute-start(bf16[2,2,2,16,768]{4,3,2,1,0:T(8,128)(2,1)S(1)} %get-tuple-element.213), channel_id=1, source_target_pairs={{0,1},{1,0},{2,3},{3,2},{4,5},{5,4},{6,7},{7,6},{8,9},{9,8},{10,11... | collective-permute-start | bytes 589832 | tf_op jit(solution)/shard_map/ppermute | solution.py:588
  228.8 10.5 %collective-permute-start.25 = (bf16[256,768]{1,0:T(8,128)(2,1)S(1)}, bf16[256,768]{1,0:T(8,128)(2,1)S(1)}, u32[]{:S(2)}, u32[]{:S(2)}) collective-permute-start(bf16[256,768]{1,0:T(8,128)(2,1)S(1)} %get-tuple-element.169), channel_id=1, source_target_pairs={{0,2},{2,0},{4,6},{6,4},{8,10},{10,8},{12,14},{14,12},{16,18},{18,... | collective-permute-start | bytes 1179656 | tf_op jit(solution)/shard_map/ppermute | solution.py:588
  229.6 7.7 %collective-permute-start.22 = (bf16[16,2048]{1,0:T(8,128)(2,1)S(1)}, bf16[16,2048]{1,0:T(8,128)(2,1)S(1)}, u32[]{:S(2)}, u32[]{:S(2)}) collective-permute-start(bf16[16,2048]{1,0:T(8,128)(2,1)S(1)} %get-tuple-element.220), channel_id=1, source_target_pairs={{0,16},{2,18},{4,20},{6,22},{8,24},{10,26},{12,28},{14,30},{16,0},... | collective-permute-start | bytes 196616 | tf_op jit(solution)/shard_map/ppermute | solution.py:588
  233.1 6.1 %collective-permute-start.23 = (bf16[16,2048]{1,0:T(8,128)(2,1)S(1)}, bf16[16,2048]{1,0:T(8,128)(2,1)S(1)}, u32[]{:S(2)}, u32[]{:S(2)}) collective-permute-start(bf16[16,2048]{1,0:T(8,128)(2,1)S(1)} %get-tuple-element.219), channel_id=1, source_target_pairs={{0,24},{2,26},{4,28},{6,30},{8,16},{10,18},{12,20},{14,22},{16,8},... | collective-permute-start | bytes 196616 | tf_op jit(solution)/shard_map/ppermute | solution.py:588
  239.4 5.7 %collective-permute-start.26 = (bf16[2,2,2,16,768]{4,3,2,1,0:T(8,128)(2,1)S(1)}, bf16[2,2,2,16,768]{4,3,2,1,0:T(8,128)(2,1)S(1)}, u32[]{:S(2)}, u32[]{:S(2)}) collective-permute-start(bf16[2,2,2,16,768]{4,3,2,1,0:T(8,128)(2,1)S(1)} %dynamic-slice_bitcast_fusion.10), channel_id=1, source_target_pairs={{0,1},{1,0},{2,3},{3,2},{4,5},{5,4},{6,7},{7,6},{8,9},{9,8},{10,11... | collective-permute-start | bytes 589832 | tf_op jit(solution)/shard_map/ppermute | solution.py:588
  240.4 7.3 %collective-permute-start.36 = (bf16[16,4736]{1,0:T(8,128)(2,1)S(1)}, bf16[16,4736]{1,0:T(8,128)(2,1)S(1)}, u32[]{:S(2)}, u32[]{:S(2)}) collective-permute-start(bf16[16,4736]{1,0:T(8,128)(2,1)S(1)} %get-tuple-element.226), channel_id=1, source_target_pairs={{0,8},{2,10},{4,12},{6,14},{8,0},{10,2},{12,4},{14,6},{16,24},{18,... | collective-permute-start | bytes 454664 | tf_op jit(solution)/shard_map/ppermute | solution.py:588
  241.5 14.5 %collective-permute-start.37 = (bf16[16,4736]{1,0:T(8,128)(2,1)S(1)}, bf16[16,4736]{1,0:T(8,128)(2,1)S(1)}, u32[]{:S(2)}, u32[]{:S(2)}) collective-permute-start(bf16[16,4736]{1,0:T(8,128)(2,1)S(1)} %get-tuple-element.226), channel_id=1, source_target_pairs={{0,16},{2,18},{4,20},{6,22},{8,24},{10,26},{12,28},{14,30},{16,0},... | collective-permute-start | bytes 454664 | tf_op jit(solution)/shard_map/ppermute | solution.py:588
  243.1 13.0 %collective-permute-start.38 = (bf16[16,4736]{1,0:T(8,128)(2,1)S(1)}, bf16[16,4736]{1,0:T(8,128)(2,1)S(1)}, u32[]{:S(2)}, u32[]{:S(2)}) collective-permute-start(bf16[16,4736]{1,0:T(8,128)(2,1)S(1)} %get-tuple-element.226), channel_id=1, source_target_pairs={{0,24},{2,26},{4,28},{6,30},{8,16},{10,18},{12,20},{14,22},{16,8},... | collective-permute-start | bytes 454664 | tf_op jit(solution)/shard_map/ppermute | solution.py:588
  245.2 5.7 %collective-permute-start.27 = (bf16[2,2,16,1536]{3,2,1,0:T(8,128)(2,1)S(1)}, bf16[2,2,16,1536]{3,2,1,0:T(8,128)(2,1)S(1)}, u32[]{:S(2)}, u32[]{:S(2)}) collective-permute-start(bf16[2,2,16,1536]{3,2,1,0:T(8,128)(2,1)S(1)} %fusion.6), channel_id=1, source_target_pairs={{0,4},{2,6},{4,0},{6,2},{8,12},{10,14},{12,8},{14,10},{16,20},{18,... | collective-permute-start | bytes 589832 | tf_op jit(solution)/shard_map/ppermute | solution.py:588
  253.1 7.9 %collective-permute-start.29 = (bf16[16,1536]{1,0:T(8,128)(2,1)S(1)}, bf16[16,1536]{1,0:T(8,128)(2,1)S(1)}, u32[]{:S(2)}, u32[]{:S(2)}) collective-permute-start(bf16[16,1536]{1,0:T(8,128)(2,1)S(1)} %get-tuple-element.224), channel_id=1, source_target_pairs={{0,16},{2,18},{4,20},{6,22},{8,24},{10,26},{12,28},{14,30},{16,0},... | collective-permute-start | bytes 147464 | tf_op jit(solution)/shard_map/ppermute | solution.py:588
  254.0 6.9 %collective-permute-start.30 = (bf16[16,1536]{1,0:T(8,128)(2,1)S(1)}, bf16[16,1536]{1,0:T(8,128)(2,1)S(1)}, u32[]{:S(2)}, u32[]{:S(2)}) collective-permute-start(bf16[16,1536]{1,0:T(8,128)(2,1)S(1)} %get-tuple-element.223), channel_id=1, source_target_pairs={{0,24},{2,26},{4,28},{6,30},{8,16},{10,18},{12,20},{14,22},{16,8},... | collective-permute-start | bytes 147464 | tf_op jit(solution)/shard_map/ppermute | solution.py:588
  261.0 6.0 %collective-permute-start.31 = (bf16[16,1536]{1,0:T(8,128)(2,1)S(1)}, bf16[16,1536]{1,0:T(8,128)(2,1)S(1)}, u32[]{:S(2)}, u32[]{:S(2)}) collective-permute-start(bf16[16,1536]{1,0:T(8,128)(2,1)S(1)} %fusion.15), channel_id=1, source_target_pairs={{0,8},{2,10},{4,12},{6,14},{8,0},{10,2},{12,4},{14,6},{16,24},{18,... | collective-permute-start | bytes 147464 | tf_op jit(solution)/shard_map/ppermute | solution.py:588
  262.3 17.9 %collective-permute-start.39 = (bf16[2,2,1,16,4736]{4,3,2,1,0:T(8,128)(2,1)S(1)}, bf16[2,2,1,16,4736]{4,3,2,1,0:T(8,128)(2,1)S(1)}, u32[]{:S(2)}, u32[]{:S(2)}) collective-permute-start(bf16[2,2,1,16,4736]{4,3,2,1,0:T(8,128)(2,1)S(1)} %bitcast.123), channel_id=1, source_target_pairs={{0,4},{2,6},{4,0},{6,2},{8,12},{10,14},{12,8},{14,10},{16,20},{18,... | collective-permute-start | bytes 1818632 | tf_op jit(solution)/shard_map/ppermute | solution.py:588
  265.4 5.9 %collective-permute-start.33 = (bf16[16,1536]{1,0:T(8,128)(2,1)S(1)}, bf16[16,1536]{1,0:T(8,128)(2,1)S(1)}, u32[]{:S(2)}, u32[]{:S(2)}) collective-permute-start(bf16[16,1536]{1,0:T(8,128)(2,1)S(1)} %fusion.15), channel_id=1, source_target_pairs={{0,24},{2,26},{4,28},{6,30},{8,16},{10,18},{12,20},{14,22},{16,8},... | collective-permute-start | bytes 147464 | tf_op jit(solution)/shard_map/ppermute | solution.py:588
  271.4 8.7 %collective-permute-start.34 = (bf16[2,2,1,16,1536]{4,3,2,1,0:T(8,128)(2,1)S(1)}, bf16[2,2,1,16,1536]{4,3,2,1,0:T(8,128)(2,1)S(1)}, u32[]{:S(2)}, u32[]{:S(2)}) collective-permute-start(bf16[2,2,1,16,1536]{4,3,2,1,0:T(8,128)(2,1)S(1)} %maximum_select_fusion.22), channel_id=1, source_target_pairs={{0,4},{2,6},{4,0},{6,2},{8,12},{10,14},{12,8},{14,10},{16,20},{18,... | collective-permute-start | bytes 589832 | tf_op jit(solution)/shard_map/ppermute | solution.py:588
  (58 other events, 415.0 us)
where the time goes:
time: 293 us; the launch traced here: 290 us
  Pallas kernels  155 us (53%)
  starting transfers between devices  43.8 us (15%)
  waiting for transfers between devices  38.6 us (13%)
  other arithmetic  26.3 us (9%)
  local copies, waits for them, and re-layouts  23 us (8%)
  between operations  3.28 us (1%)
    pallas_call x19, Pallas kernels, call(): pl.pallas_call(kernel, out_shape=[jax.ShapeDtypeStruct(shape, dtype) for...  155 us
    ppermute x41, starting transfers between devices, flip(): return lax.ppermute(value, axis, [(i, i ^ bit) for i in range(count)])  43.8 us
    ppermute x41, waiting for transfers between devices, flip(): return lax.ppermute(value, axis, [(i, i ^ bit) for i in range(count)])  38.6 us
    select_n x27, other arithmetic, both(): return jnp.where(bit == 0, low, high)  15.1 us
    unnamed x99, local copies, waits for them, and re-layouts  13.6 us
  transfers between devices with their start and end apart: 41, of which 19 were waited for; matrix products, arithmetic and copies ran while one was open for 7% of the time, Pallas kernels for 22%

commit v1 on v0

--- a/solution.py
+++ b/solution.py
@@ -143,8 +143,9 @@
 
 def attend_kernel(first, size, x_ref, w_ref, seg_ref, *refs):
     if first:
-        w_t_ref = refs[0]
-        w_t_ref[...] = w_ref[...].T
+        group, w_t_ref = first - 1, refs[0]
+        count = w_t_ref.shape[0]
+        w_t_ref[...] = w_ref[:, group * count : (group + 1) * count].T
         refs = refs[1:]
     else:
         w_t_ref = w_ref
@@ -172,18 +173,11 @@
     o_ref[rows:, :] = ob_ref[...]
 
 
-def z_copy(z_ref, z_hbm_ref, sem_ref, step):
-    slot = step % 2
-    there = z_hbm_ref.at[:, step * B : (step + 1) * B]
-    return pltpu.make_async_copy(z_ref.at[slot], there, sem_ref.at[slot])
-
-
 def feed_in_kernel(
     oa_ref,
     ob_ref,
     x_ref,
-    wop_ref,
-    wi_ref,
+    wio_ref,
     o_ref,
     wo_t_ref,
     wi_t_ref,
@@ -191,24 +185,18 @@
     n1_ref,
     stat_ref,
     yr_ref,
-    z_hbm_ref,
+    z_ref,
     slope_ref,
-    z_ref,
-    sem_ref,
 ):
-    width, hidden = wi_ref.shape
+    width = wio_ref.shape[0]
+    hidden = wio_ref.shape[1] - width - 128
     join_heads(oa_ref, ob_ref, o_ref)
-    wo_t_ref[...] = wop_ref[:, :width].T
-    wi_t_ref[...] = wi_ref[...].T
-    params = wop_ref[:, width:].astype(f32)
+    wo_t_ref[...] = wio_ref[:, hidden : hidden + width].T
+    wi_t_ref[...] = wio_ref[:, :hidden].T
+    params = wio_ref[:, hidden + width :].astype(f32)
     gain_one, bias_one = params[:, 0:1], params[:, 1:2]
-    copies = []
     for at in range(0, x_ref.shape[1], B):
         cols = slice(at, at + B)
-        step = at // B
-        copies.append(z_copy(z_ref, z_hbm_ref, sem_ref, step))
-        if step > 1:
-            copies[step - 2].wait()
         h = x_ref[:, cols].astype(f32) + nn(wo_t_ref[...], o_ref[:, cols])
         n1, s1 = normalize(h)
         n1_ref[:, cols] = n1.astype(bf16)
@@ -219,36 +207,37 @@
         for f in range(0, hidden, CHUNK):
             u = nn(wi_t_ref[f : f + CHUNK, :], yr_ref[:, cols])
             z, slope = gelu_pair(u)
-            z_ref[step % 2, f : f + CHUNK, :] = z.astype(bf16)
+            z_ref[f : f + CHUNK, cols] = z.astype(bf16)
             slope_ref[f : f + CHUNK, cols] = slope.astype(bf16)
-        copies[step].start()
-    for copy in copies[-2:]:
-        copy.wait()
 
 
 def feed_out_kernel(
-    y_ref, z_hbm_ref, wop_ref, wu_ref, wu_t_ref, next_ref, x2_ref, n2_ref, stat_ref, z_ref, sem_ref
+    shards,
+    y_ref,
+    z_ref,
+    wio_ref,
+    groups_ref,
+    wu_ref,
+    wu_t_ref,
+    next_ref,
+    x2_ref,
+    n2_ref,
+    stat_ref,
 ):
-    width = wu_ref.shape[1]
-    length = y_ref.shape[1]
-
-    def fetch(step):
-        slot = step % 2
-        there = z_hbm_ref.at[:, step * B : (step + 1) * B]
-        return pltpu.make_async_copy(there, z_ref.at[slot], sem_ref.at[slot])
-
-    copies = [fetch(step) for step in range(length // B)]
-    copies[0].start()
+    hidden, width = wu_ref.shape
+    count = hidden // width
+    rows = width // shards
+    for shard in range(shards):
+        for group in range(count):
+            at = (shard * count + group) * rows
+            part = slice(shard * rows, (shard + 1) * rows)
+            wu_ref[at : at + rows, :] = groups_ref[part, group * width : (group + 1) * width]
     wu_t_ref[...] = wu_ref[...].T
-    params = wop_ref[:, width:].astype(f32)
+    params = wio_ref[:, hidden + width :].astype(f32)
     gain_two, bias_two = params[:, 2:3], params[:, 3:4]
     for at in range(0, y_ref.shape[1], B):
         cols = slice(at, at + B)
-        step = at // B
-        if step + 1 < len(copies):
-            copies[step + 1].start()
-        copies[step].wait()
-        h2 = y_ref[:, cols] + nn(wu_t_ref[...], z_ref[step % 2])
+        h2 = y_ref[:, cols] + nn(wu_t_ref[...], z_ref[:, cols])
         n2, s2 = normalize(h2)
         n2_ref[:, cols] = n2.astype(bf16)
         stat_ref[:, cols] = jnp.broadcast_to(s2, (8, B))
@@ -261,8 +250,7 @@
     oa_ref,
     ob_ref,
     x_ref,
-    wop_ref,
-    wi_ref,
+    wio_ref,
     wu_ref,
     wo_t_ref,
     wi_t_ref,
@@ -271,7 +259,7 @@
     scale_ref,
     o_ref,
     mixed_ref,
-    z_hbm_ref,
+    z_ref,
     du_ref,
     yr_ref,
     dfr_ref,
@@ -280,24 +268,18 @@
     do_ref,
     acc_ref,
     n1_ref,
-    z_ref,
-    sem_ref,
 ):
-    width, hidden = wi_ref.shape
+    width = wio_ref.shape[0]
+    hidden = wio_ref.shape[1] - width - 128
     join_heads(oa_ref, ob_ref, o_ref)
-    params = wop_ref[:, width:].astype(f32)
+    params = wio_ref[:, hidden + width :].astype(f32)
     gain_one, bias_one = params[:, 0:1], params[:, 1:2]
     gain_two, bias_two = params[:, 2:3], params[:, 3:4]
     acc_ref[...] = jnp.zeros_like(acc_ref)
 
-    copies = []
     for at in range(0, x_ref.shape[1], B):
         cols = slice(at, at + B)
-        step = at // B
-        slot = step % 2
-        copies.append(z_copy(z_ref, z_hbm_ref, sem_ref, step))
-        if step > 1:
-            copies[step - 2].wait()
+        slot = at // B % 2
         h = x_ref[:, cols] + nn(wo_t_ref[...], o_ref[:, cols])
         n1, s1 = normalize(h)
         n1_ref[slot] = n1
@@ -307,10 +289,9 @@
         for f in range(0, hidden, CHUNK):
             u = nn(wi_t_ref[f : f + CHUNK, :], yr_ref[:, cols])
             z, slope = gelu_pair(u)
-            z_ref[slot, f : f + CHUNK, :] = z.astype(bf16)
+            z_ref[f : f + CHUNK, cols] = z.astype(bf16)
             du_ref[f : f + CHUNK, cols] = slope.astype(bf16)
-        copies[step].start()
-        h2 = dh_ref[:, cols] + nn(wu_t_ref[...], z_ref[slot])
+        h2 = dh_ref[:, cols] + nn(wu_t_ref[...], z_ref[:, cols])
         n2, s2 = normalize(h2)
         out = n2 * gain_two + bias_two
         mixed_ref[cols, :] = out.astype(bf16).T
@@ -324,15 +305,13 @@
             dz = nn(wu_ref[f : f + CHUNK, :], dfr_ref[:, cols])
             slope = du_ref[f : f + CHUNK, cols].astype(f32)
             du_ref[f : f + CHUNK, cols] = (dz * slope).astype(bf16)
-        dy = dh_ref[:, cols] + nn(wi_ref[...], du_ref[:, cols])
+        dy = dh_ref[:, cols] + nn(wio_ref[:, :hidden], du_ref[:, cols])
         acc_ref[0] += lanes_sum(dy * n1_ref[slot])
         acc_ref[1] += lanes_sum(dy)
         dh = normalize_back(dy * gain_one, n1_ref[slot], s1)
         dh_ref[:, cols] = dh
         dar_ref[:, cols] = dh.astype(bf16)
-        do_ref[:, cols] = nn(wop_ref[:, :width], dar_ref[:, cols]).astype(bf16)
-    for copy in copies[-2:]:
-        copy.wait()
+        do_ref[:, cols] = nn(wio_ref[:, hidden : hidden + width], dar_ref[:, cols]).astype(bf16)
 
 
 def feed_back_kernel(
@@ -342,8 +321,7 @@
     stat1_ref,
     stat2_ref,
     slope_ref,
-    wop_ref,
-    wi_ref,
+    wio_ref,
     wu_ref,
     acc_in_ref,
     dh_ref,
@@ -353,8 +331,9 @@
     dar_ref,
     acc_ref,
 ):
-    width, hidden = wi_ref.shape
-    params = wop_ref[:, width:].astype(f32)
+    width = wio_ref.shape[0]
+    hidden = wio_ref.shape[1] - width - 128
+    params = wio_ref[:, hidden + width :].astype(f32)
     gain_one, gain_two = params[:, 0:1], params[:, 2:3]
     acc_ref[...] = acc_in_ref[...]
     for at in range(0, g_ref.shape[1], B):
@@ -370,14 +349,14 @@
             dz = nn(wu_ref[f : f + CHUNK, :], dfr_ref[:, cols])
             slope = slope_ref[f : f + CHUNK, cols].astype(f32)
             du_ref[f : f + CHUNK, cols] = (dz * slope).astype(bf16)
-        dy = dh_ref[:, cols] + nn(wi_ref[...], du_ref[:, cols])
+        dy = dh_ref[:, cols] + nn(wio_ref[:, :hidden], du_ref[:, cols])
         n1 = n1_ref[:, cols].astype(f32)
         acc_ref[0] += lanes_sum(dy * n1)
         acc_ref[1] += lanes_sum(dy)
         dh = normalize_back(dy * gain_one, n1, stat1_ref[0:1, cols])
         dh_ref[:, cols] = dh
         dar_ref[:, cols] = dh.astype(bf16)
-        do_ref[:, cols] = nn(wop_ref[:, :width], dar_ref[:, cols]).astype(bf16)
+        do_ref[:, cols] = nn(wio_ref[:, hidden : hidden + width], dar_ref[:, cols]).astype(bf16)
 
 
 def place(value, first, unit, core, keep_ref, send_ref, cols):
@@ -395,45 +374,15 @@
             send_ref[rows, cols] = part
 
 
-def outer_grad_kernel(
-    shards,
-    core_ref,
-    z1_hbm_ref,
-    z2_hbm_ref,
-    dfr1_ref,
-    dfr2_ref,
-    keep_ref,
-    send_ref,
-    z1_ref,
-    z2_ref,
-    sem_ref,
-):
+def outer_grad_kernel(shards, core_ref, z1_ref, z2_ref, dfr1_ref, dfr2_ref, keep_ref, send_ref):
     core = core_ref[0]
-    hidden, width = z1_hbm_ref.shape[0], dfr1_ref.shape[0]
+    hidden, width = z1_ref.shape[0], dfr1_ref.shape[0]
     unit = width // shards // 2
     groups = hidden // width
     per_group = hidden // shards // groups
-
-    def fetch(step, which, hbm_ref, vmem_ref):
-        slot = step % 2
-        there = hbm_ref.at[step * 256 : (step + 1) * 256]
-        return pltpu.make_async_copy(there, vmem_ref.at[slot], sem_ref.at[which, slot])
-
-    copies = [
-        (fetch(step, 0, z1_hbm_ref, z1_ref), fetch(step, 1, z2_hbm_ref, z2_ref))
-        for step in range(hidden // 256)
-    ]
-    for copy in copies[0]:
-        copy.start()
-    for step in range(hidden // 256):
-        first = step * 256
-        if step + 1 < len(copies):
-            for copy in copies[step + 1]:
-                copy.start()
-        for copy in copies[step]:
-            copy.wait()
-        slot = step % 2
-        dwu = nt(z1_ref[slot], dfr1_ref[...]) + nt(z2_ref[slot], dfr2_ref[...])
+    for first in range(0, hidden, 256):
+        part = slice(first, first + 256)
+        dwu = nt(z1_ref[part, :], dfr1_ref[...]) + nt(z2_ref[part, :], dfr2_ref[...])
         dwu = dwu.astype(bf16)
         for at in range(0, 256, per_group):
             block = (first + at) // per_group
@@ -541,7 +490,7 @@
         place(dw.astype(bf16), 0, unit, core, keep_ref, send_ref, slice(i * rows, (i + 1) * rows))
 
 
-def input_kernel(turned, wa_ref, wb_ref, dh_ref, *refs):
+def input_kernel(turned, w_ref, dh_ref, *refs):
     parts, grad_ref, join_ref = refs[:-2], refs[-2], refs[-1]
     length = dh_ref.shape[1]
     at = 0
@@ -552,11 +501,9 @@
                 rows = part.shape[1]
                 join_ref[at : at + rows, :] = part[i]
                 at += rows
-    half = at // 2
     for at in range(0, length, B):
         cols = slice(at, at + B)
-        grad = dh_ref[:, cols] + nn(wa_ref[...], join_ref[:half, cols])
-        grad += nn(wb_ref[...], join_ref[half:, cols])
+        grad = dh_ref[:, cols] + nn(w_ref[...], join_ref[:, cols])
         if turned:
             grad_ref[cols, :] = grad.T
         else:
@@ -565,16 +512,15 @@
 
 VM = pl.BlockSpec(memory_space=pltpu.VMEM)
 SM = pl.BlockSpec(memory_space=pltpu.SMEM)
-HB = pl.BlockSpec(memory_space=pltpu.HBM)
-
-
-def call(kernel, outs, scratch, args, specs=None, cost=10, limit=8, far=(), alias={}):
+
+
+def call(kernel, outs, scratch, args, specs=None, cost=10, limit=8, alias={}):
     return pl.pallas_call(
         kernel,
         out_shape=[jax.ShapeDtypeStruct(shape, dtype) for shape, dtype in outs],
         in_specs=specs if specs else [VM] * len(args),
-        out_specs=[HB if i in far else VM for i in range(len(outs))],
-        scratch_shapes=[pltpu.VMEM(*one) if isinstance(one, tuple) else one for one in scratch],
+        out_specs=[VM] * len(outs),
+        scratch_shapes=[pltpu.VMEM(*one) for one in scratch],
         input_output_aliases=alias,
         cost_estimate=pl.CostEstimate(
             flops=cost * 1000000000, bytes_accessed=cost * 3000000, transcendentals=0
@@ -613,16 +559,17 @@
     return lax.dynamic_slice_in_dim(block, bit_of("dp", 1) * rows, rows, axis=0)[None]
 
 
-def my_quarter(block):
-    rows = block.shape[0] // 4
-    place = 2 * bit_of("dp", 1) + bit_of("dp", 2)
-    return lax.dynamic_slice_in_dim(block, place * rows, rows, axis=0)[None]
-
-
-def over_shards(mine):
-    for axis, bit in reversed(bits_of("shard")):
-        mine = both(bit_of(axis, bit), mine, flip(mine, axis, bit), 0)
-    return mine
+class Gather:
+    def __init__(self, mine):
+        *steps, self.last = reversed(bits_of("shard"))
+        for axis, bit in steps:
+            mine = both(bit_of(axis, bit), mine, flip(mine, axis, bit), 0)
+        self.mine = mine
+        self.came = flip(mine, *self.last)
+
+    def merge(self, *after):
+        came = tie(self.came, *after) if after else self.came
+        return both(bit_of(*self.last), self.mine, came, 0)
 
 
 def over_cores(mine):
@@ -725,18 +672,22 @@
     return joined
 
 
-def tie_all(*values):
-    return lax.optimization_barrier(values)[:-1]
-
-
 def tie(value, *others):
     return lax.optimization_barrier((value,) + others)[0]
 
 
-def compute(tokens, seg_rows, scale_rows, cotangent, blocks):
-    wa_half, wb_half, wop_half, wi_half, wu_part = blocks
+def compute(tokens, seg_rows, scale_rows, cotangent, weights, hidden):
     length, width = tokens.shape
-    hidden = wi_half.shape[2]
+    *qkv, wo_block, vectors, wi_block, wu_block = weights
+
+    def later(done):
+        *args, _ = lax.optimization_barrier((wo_block, wi_block, wu_block, *vectors, done))
+        wo, wi, wu, *params = args
+        stacked = jnp.pad(jnp.stack(params, axis=1), ((0, 0), (0, 128 - len(params))))
+        groups = jnp.split(wu, hidden // width, axis=0)
+        parts = ((wi, wo, stacked), groups)
+        return [jnp.concatenate([my_half(w) for w in part], axis=-1) for part in parts]
+
     size = width // H
     rows = width // 2
     shards = lax.axis_size("shard")
@@ -746,69 +697,69 @@
     wide = ((hidden, length), bf16)
     bias = ((length, 3 * B), f32)
     pair = ((2, length, 3 * B), bf16)
-    z_tiles = [((2, hidden, B), bf16), pltpu.SemaphoreType.DMA((2,))]
-    heads = [((3, rows, length), bf16), ((rows, length), bf16), ((H // 2, 8, length), f32)]
-
-    wa_mine = over_shards(wa_half)
-    wa = over_cores(wa_mine)
-    wb_mine, wop_mine, wi_mine, wu_mine = (
-        over_shards(tie(part, wa_mine)) for part in (wb_half, wop_half, wi_half, wu_part)
-    )
-    (x1,) = call(turn_kernel, [tall], [], (tokens,), None, 1)
-    first_attend = functools.partial(attend_kernel, True, size)
+    shapes = [((3, rows, length), bf16), ((rows, length), bf16), ((H // 2, 8, length), f32)]
+
+    half = width // 2
+    cols = [w[:, at : at + half] for at in (0, half) for w in qkv]
+    packed = jnp.concatenate([my_half(w) for w in cols], axis=-1)
+    mine = Gather(packed).merge()
+    wqkv = over_cores(mine)
+    wio_part, wu_part = later(packed)
+    wio_gather = Gather(tie(wio_part, mine))
+    (x1,) = call(turn_kernel, [tall], [], (tie(tokens, packed),), None, 1)
+    attend = functools.partial(attend_kernel, 1, size)
     turned = [((3 * rows, width), bf16)]
-    wa_t, qkv1a, o1a, lse1a = call(first_attend, turned + heads, [bias], (x1, wa, seg_rows), limit=8)
-    wb_mine, wop_mine, wi_mine, wu_mine = tie_all(wb_mine, wop_mine, wi_mine, wu_mine, o1a)
-    wb = over_cores(wb_mine)
-    wi, wop = over_cores(wi_mine), over_cores(wop_mine)
-    wu_mine = both(bit_of("dp", 2), wu_mine, flip(wu_mine, "dp", 2), 1)
-    seg_b = tie(seg_rows, wi_mine, wop_mine)
-    wb_t, qkv1b, o1b, lse1b = call(first_attend, turned + heads, [bias], (x1, wb, seg_b), limit=8)
+    wa_t, qkv1a, o1a, lse1a = call(attend, turned + shapes, [bias], (x1, wqkv, seg_rows))
+    wio_mine = wio_gather.merge(o1a)
+    wio = over_cores(wio_mine)
+    wu_part = tie(wu_part, wio_mine)
+    wu_gather = Gather(wu_part)
+    attend = functools.partial(attend_kernel, 2, size)
+    wb_t, qkv1b, o1b, lse1b = call(
+        attend, turned + shapes, [bias], (x1, wqkv, tie(seg_rows, wio_mine, wu_part))
+    )
     o1, wo_t, wi_t, y1, n11, stat11, yr1, z1, slope1 = call(
         feed_in_kernel,
         [tall, ((width, width), bf16), ((hidden, width), bf16), tall32, tall]
         + [((8, length), f32), tall, wide, wide],
-        z_tiles,
-        (tie(o1a, wu_mine), o1b, x1, wop, wi),
-        far=(7,),
-    )
-    wu = over_cores(wu_mine)
-    wu_t, next1, x2, n21, stat12 = call(
-        feed_out_kernel,
-        [((width, hidden), bf16), tall32, tall, tall, ((8, length), f32)],
-        z_tiles,
-        (y1, z1, wop, wu),
-        [VM, HB, VM, VM],
-    )
-    attend = functools.partial(attend_kernel, False, size)
-    qkv2a, o2a, lse2a = call(attend, heads, [bias], (x2, wa_t, seg_rows), limit=8)
-    qkv2b, o2b, lse2b = call(attend, heads, [bias], (x2, wb_t, seg_rows), limit=8)
+        [],
+        (o1a, o1b, x1, wio),
+    )
+    wu_groups = over_cores(wu_gather.merge(o1b))
+    wu, wu_t, next1, x2, n21, stat12 = call(
+        functools.partial(feed_out_kernel, shards),
+        [((hidden, width), bf16), ((width, hidden), bf16), tall32, tall, tall]
+        + [((8, length), f32)],
+        [],
+        (y1, z1, wio, wu_groups),
+    )
+    attend = functools.partial(attend_kernel, 0, size)
+    qkv2a, o2a, lse2a = call(attend, shapes, [bias], (x2, wa_t, seg_rows), limit=8)
+    qkv2b, o2b, lse2b = call(attend, shapes, [bias], (x2, wb_t, seg_rows), limit=8)
     o2, mixed, z2, du2, yr2, dfr2, dar2, dh2, do2, acc = call(
         feed_last_kernel,
         [tall, ((length, width), bf16), wide, wide, tall, tall, tall, tall32, tall]
         + [((4, width, 128), f32)],
-        [((2, width, B), f32)] + z_tiles,
-        (o2a, o2b, next1, wop, wi, wu, wo_t, wi_t, wu_t, cotangent, scale_rows),
-        limit=12,
-        far=(2,),
+        [((2, width, B), f32)],
+        (o2a, o2b, next1, wio, wu, wo_t, wi_t, wu_t, cotangent, scale_rows),
+        limit=10,
     )
     back = [bias, pair, pair]
     dqkv2 = []
     for group, (qkv, lse) in enumerate(((qkv2a, lse2a), (qkv2b, lse2b))):
         kernel = functools.partial(attend_back_kernel, group * rows, size)
-        dqkv2 += call(kernel, heads[:1], back, (qkv, o2, do2, lse, seg_rows), limit=14)
+        dqkv2 += call(kernel, shapes[:1], back, (qkv, o2, do2, lse, seg_rows), limit=14)
     joined = [((3 * width, length), bf16)]
     (grad1,) = call(
-        functools.partial(input_kernel, False), [tall32], joined, (wa, wb, dh2, *dqkv2), None, 3, 8
+        functools.partial(input_kernel, False), [tall32], joined, (wqkv, dh2, *dqkv2), None, 3, 8
     )
     dh1, do1, du1, dfr1, dar1, acc = call(
         feed_back_kernel,
         [tall32, tall, wide, tall, tall, ((4, width, 128), f32)],
         [],
-        (grad1, n11, n21, stat11, stat12, slope1, wop, wi, wu, acc),
-        alias={5: 2, 9: 5},
-    )
-    half = width // 2
+        (grad1, n11, n21, stat11, stat12, slope1, wio, wu, acc),
+        alias={5: 2, 8: 5},
+    )
     keep_i, send_i = call(
         functools.partial(inner_grad_kernel, shards),
         [((half, hidden + width + 128), bf16)] * 2,
@@ -820,9 +771,9 @@
     keep_u, send_u = call(
         functools.partial(outer_grad_kernel, shards),
         [((half, hidden), bf16)] * 2,
-        [((2, 256, length), bf16)] * 2 + [pltpu.SemaphoreType.DMA((2, 2))],
+        [],
         (tie(core, send_i), z1, z2, dfr1, dfr2),
-        [SM, HB, HB, VM, VM],
+        [SM] + [VM] * 4,
     )
     parts = []
 
@@ -860,34 +811,37 @@
         one.after(parts[2])
     for label in x_bits:
         first.halve(*label)
-    inner.scatter()
-    outer.scatter()
-    second = Sum(*part(3, tie(seg_rows, inner.keep, outer.keep, first.sent)))
-    for one in (first, inner, outer):
-        one.after(second.sent)
     feed = join(inner, outer)
+    feed.scatter()
+    second = Sum(*part(3, tie(seg_rows, feed.keep, first.sent)))
+    feed.after(second.sent)
+    feed.settle()
     (input_grad,) = call(
         functools.partial(input_kernel, True),
         [((length, width), f32)],
         joined,
-        (wa, wb, tie(dh1, second.sent, feed.value), *parts),
+        (wqkv, tie(dh1, second.sent, feed.value), *parts),
         None,
-        5,
+        15,
         10,
     )
-    feed.collect()
+    second.after(input_grad)
     for label in x_bits:
         second.halve(*label)
+    feed.after(second.sent)
+    feed.collect()
+    first.after(second.sent)
     heads = join(first, second)
     heads.halve(*y_bit)
-    feed.after(heads.sent)
-    feed.double(*y_bit)
     heads.scatter()
     heads.settle()
-    feed.after(heads.value)
+    heads.after(feed.value)
+    feed.after(heads.keep)
+    feed.double(*y_bit)
     heads.collect()
+    heads.after(feed.value)
+    heads.double(*y_bit)
     feed.finish()
-    heads.double(*y_bit)
     heads.finish()
     return mixed, input_grad, feed, heads
 
@@ -912,22 +866,16 @@
     length, width = tokens.shape
     hidden = inner_weight.shape[1]
     half = width // 2
-    qkv = [my_half(w) for w in (query_weight, key_weight, value_weight)]
-    stacked = jnp.stack([attn_gain, attn_bias, feed_gain, feed_bias], axis=1)
-    stacked = jnp.pad(stacked, ((0, 0), (0, 124)))
-    blocks = (
-        jnp.concatenate([w[..., :half] for w in qkv], axis=-1),
-        jnp.concatenate([w[..., half:] for w in qkv], axis=-1),
-        my_half(jnp.concatenate([output_weight, stacked], axis=1)),
-        my_half(inner_weight),
-        my_quarter(outer_weight),
-    )
+    weights = (query_weight, key_weight, value_weight, output_weight)
+    weights += ((attn_gain, attn_bias, feed_gain, feed_bias), inner_weight, outer_weight)
     seg_rows = jnp.broadcast_to(segment_ids.astype(f32)[None], (8, length))
     valid = (jnp.arange(length) < row_counts[0]).astype(f32)
     tokens_total = lax.axis_size("dp") * lax.axis_size("shard") * length
     factor = jnp.float32(tokens_total) / global_count[0].astype(f32)
     scale_rows = jnp.broadcast_to((valid * factor)[None], (8, length))
-    mixed, input_grad, feed, heads = compute(tokens, seg_rows, scale_rows, cotangent, blocks)
+    mixed, input_grad, feed, heads = compute(
+        tokens, seg_rows, scale_rows, cotangent, weights, hidden
+    )
     dqkv = (
         jnp.concatenate([heads.columns(c, c + half) for c in (at, at + 3 * half)], axis=1)
         for at in range(0, 3 * half, half)

time: 293 us -> 283 us (0.966)
  waiting for transfers between devices: 38.6 us -> 50.7 us
  other arithmetic: 26.3 us -> 15 us
  starting transfers between devices: 43.8 us -> 37.3 us
  local copies, waits for them, and re-layouts: 23 us -> 18.3 us
    ppermute x41 -> x33, waiting for transfers between devices: 38.6 us -> 50.7 us  [flip(): return lax.ppermute(value, axis, [(i, i ^ bit) for i in range(count)])]
    select_n x27 -> x24, other arithmetic: 15.1 us -> 5.06 us  [both(): return jnp.where(bit == 0, low, high)]
    ppermute x41 -> x33, starting transfers between devices: 43.8 us -> 37.3 us  [flip(): return lax.ppermute(value, axis, [(i, i ^ bit) for i in range(count)])]
    unnamed x99 -> x77, local copies, waits for them, and re-layouts: 13.6 us -> 12.6 us
  transfers between devices with their start and end apart: 41 -> 33, of which waited for: 19 -> 19; matrix products, arithmetic and copies ran while one was open for 7% -> 3% of each run, Pallas kernels for 22% -> 22%
where the time goes in v1:
time: 283 us; the launch traced here: 282 us
  Pallas kernels  157 us (55%)
  waiting for transfers between devices  50.7 us (18%)
  starting transfers between devices  37.3 us (13%)
  local copies, waits for them, and re-layouts  18.3 us (6%)
  other arithmetic  15 us (5%)
  between operations  3.26 us (1%)
    pallas_call x19, Pallas kernels, call(): pl.pallas_call(kernel, out_shape=[jax.ShapeDtypeStruct(shape, dtype) for...  157 us
    ppermute x33, waiting for transfers between devices, flip(): return lax.ppermute(value, axis, [(i, i ^ bit) for i in range(count)])  50.7 us
    ppermute x33, starting transfers between devices, flip(): return lax.ppermute(value, axis, [(i, i ^ bit) for i in range(count)])  37.3 us
    unnamed x77, local copies, waits for them, and re-layouts  12.6 us
  transfers between devices with their start and end apart: 33, of which 19 were waited for; matrix products, arithmetic and copies ran while one was open for 3% of the time, Pallas kernels for 22%

profile of v1, /device:TPU:0, one launch (start us, length us, event | category | flops | bytes accessed | tf_op | source)
XLA Modules:
  0.0 281.7 jit_solution(3921749591979328740)
XLA Ops:
  4.0 3.0 %collective-permute-start = (bf16[1,128,1536]{2,1,0:T(8,128)(2,1)S(1)}, bf16[1,128,1536]{2,1,0:T(8,128)(2,1)}, u32[]{:S(2)}, u32[]{:S(2)}) collective-permute-start(bf16[1,128,1536]{2,1,0:T(8,128)(2,1)S(1)} %bitcast_dynamic-update-slice_fusion), channel_id=1, source_target_pairs={{0,1},{1,0},{2,3},{3,2},{4,5},{5,4},{6,7},{7,6},{8,9},{9,8},{10,11... | collective-permute-start | bytes 1179656 | tf_op jit(solution)/shard_map/ppermute | solution.py:534
  9.4 6.8 %collective-permute-done = bf16[1,128,1536]{2,1,0:T(8,128)(2,1)} collective-permute-done((bf16[1,128,1536]{2,1,0:T(8,128)(2,1)S(1)}, bf16[1,128,1536]{2,1,0:T(8,128)(2,1)}, u32[]{:S(2)}, u32[]{:S(2)}) %collective-permute-start) | collective-permute-done | bytes 393248 | tf_op jit(solution)/shard_map/ppermute | solution.py:534
  20.5 8.7 %shard_map.239 = (bf16[768,512]{1,0:T(8,128)(2,1)S(1)}, bf16[3,256,1024]{2,1,0:T(8,128)(2,1)S(1)}, bf16[256,1024]{1,0:T(8,128)(2,1)S(1)}, f32[4,8,1024]{2,1,0:T(8,128)S(1)}) custom-call(bf16[512,1024]{1,0:T(8,128)(2,1)S(1)} %shard_map.238.x_ref.refs_1_, bf16[512,1536]{1,0:T(8,128)(2,1)S(1)} %bitcast.104, f32[8,1024]{1,0:T(8,128)S(1)} %broadcast_in_dim.75.seg_ref), custom_call_target="tpu_custom_call" | custom-call | flops 10000000000 | bytes 30000000 | tf_op jit(solution)/shard_map/pallas_call | solution.py:518
  30.4 5.5 %collective-permute-done.2 = bf16[1,128,2688]{2,1,0:T(8,128)(2,1)S(1)} collective-permute-done((bf16[1,128,2688]{2,1,0:T(8,128)(2,1)S(1)}, bf16[1,128,2688]{2,1,0:T(8,128)(2,1)S(1)}, u32[]{:S(2)}, u32[]{:S(2)}) %collective-permute-start.2) | collective-permute-done | bytes 688160 | tf_op jit(solution)/shard_map/ppermute | solution.py:534
  38.1 8.7 %shard_map.240 = (bf16[768,512]{1,0:T(8,128)(2,1)S(1)}, bf16[3,256,1024]{2,1,0:T(8,128)(2,1)S(1)}, bf16[256,1024]{1,0:T(8,128)(2,1)S(1)}, f32[4,8,1024]{2,1,0:T(8,128)S(1)}) custom-call(bf16[512,1024]{1,0:T(8,128)(2,1)S(1)} %shard_map.238.x_ref.refs_1_, bf16[512,1536]{1,0:T(8,128)(2,1)S(1)} %bitcast.105, f32[8,1024]{1,0:T(8,128)S(1)} %broadcast_in_dim.75.seg_ref), custom_call_target="tpu_custom_call" | custom-call | flops 10000000000 | bytes 30000000 | tf_op jit(solution)/shard_map/pallas_call | solution.py:518
  48.0 2.7 collective-permute-done.4
  51.9 8.0 %shard_map.241 = (bf16[512,1024]{1,0:T(8,128)(2,1)S(1)}, bf16[512,512]{1,0:T(8,128)(2,1)S(1)}, bf16[2048,512]{1,0:T(8,128)(2,1)S(1)}, f32[512,1024]{1,0:T(8,128)...) custom-call(bf16[256,1024]{1,0:T(8,128)(2,1)S(1)} %get-tuple-element, ...), custom_call_target="tpu_custom_call" | custom-call | flops 10000000000 | bytes 30000000 | tf_op jit(solution)/shard_map/pallas_call | solution.py:518
  62.0 3.4 %shard_map.242 = (bf16[2048,512]{1,0:T(8,128)(2,1)S(1)}, bf16[512,2048]{1,0:T(8,128)(2,1)S(1)}, f32[512,1024]{1,0:T(8,128)S(1)}, bf16[512,1024]{1,0:T(8,128)(2,1...) custom-call(f32[512,1024]{1,0:T(8,128)S(1)} %get-tuple-element.114.y_ref, ...), custom_call_target="tpu_custom_call" | custom-call | flops 10000000000 | bytes 30000000 | tf_op jit(solution)/shard_map/pallas_call | solution.py:518
  65.4 21.6 %shard_map.244 = (bf16[3,256,1024]{2,1,0:T(8,128)(2,1)S(1)}, bf16[256,1024]{1,0:T(8,128)(2,1)S(1)}, f32[4,8,1024]{2,1,0:T(8,128)S(1)}) custom-call(bf16[512,1024]{1,0:T(8,128)(2,1)S(1)} %get-tuple-element.117.x_ref.refs_2_, bf16[768,512]{1,0:T(8,128)(2,1)S(1)} %get-tuple-element.120.w_ref, f32[8,1024]{1,0:T(8,128)S(1)} %broadcast_in_dim.75.seg_ref), custom_call_target="tpu_custom_call" | custom-call | flops 10000000000 | bytes 30000000 | tf_op jit(solution)/shard_map/pallas_call | solution.py:518
  87.0 8.8 %shard_map.243 = (bf16[3,256,1024]{2,1,0:T(8,128)(2,1)S(1)}, bf16[256,1024]{1,0:T(8,128)(2,1)S(1)}, f32[4,8,1024]{2,1,0:T(8,128)S(1)}) custom-call(bf16[512,1024]{1,0:T(8,128)(2,1)S(1)} %get-tuple-element.117.x_ref.refs_2_, bf16[768,512]{1,0:T(8,128)(2,1)S(1)} %get-tuple-element.118.w_ref, f32[8,1024]{1,0:T(8,128)S(1)} %broadcast_in_dim.75.seg_ref), custom_call_target="tpu_custom_call" | custom-call | flops 10000000000 | bytes 30000000 | tf_op jit(solution)/shard_map/pallas_call | solution.py:518
  95.8 22.5 %shard_map.245 = (bf16[512,1024]{1,0:T(8,128)(2,1)S(1)}, bf16[1024,512]{1,0:T(8,128)(2,1)}, bf16[2048,1024]{1,0:T(8,128)(2,1)S(1)}, bf16[2048,1024]{1,0:T(8,128)...) custom-call(bf16[256,1024]{1,0:T(8,128)(2,1)S(1)} %get-tuple-element, ...), custom_call_target="tpu_custom_call" | custom-call | flops 10000000000 | bytes 30000000 | tf_op jit(solution)/shard_map/pallas_call | solution.py:518
  118.3 8.7 %shard_map.247.refs_1_.refs_4_ = bf16[3,256,1024]{2,1,0:T(8,128)(2,1)S(1)} custom-call(bf16[3,256,1024]{2,1,0:T(8,128)(2,1)S(1)} %get-tuple-element.133.qkv_ref, bf16[512,1024]{1,0:T(8,128)(2,1)S(1)} %get-tuple-element.130.o_ref.o2_ref, bf16[512,1024]{1,0:T(8,128)(2,1)S(1)} %get-tuple-element.131.do_ref, f32[4,8,1024]{2,1,0:T(8,128)S(1)} %get-tuple-element.134.lse_ref, ...), custom_call_target="tpu_custom_call" | custom-call | flops 10000000000 | bytes 30000000 | tf_op jit(solution)/shard_map/pallas_call | solution.py:518
  127.0 8.8 %shard_map.246.refs_0_.refs_4_ = bf16[3,256,1024]{2,1,0:T(8,128)(2,1)S(1)} custom-call(bf16[3,256,1024]{2,1,0:T(8,128)(2,1)S(1)} %get-tuple-element.129.qkv_ref, bf16[512,1024]{1,0:T(8,128)(2,1)S(1)} %get-tuple-element.130.o_ref.o2_ref, bf16[512,1024]{1,0:T(8,128)(2,1)S(1)} %get-tuple-element.131.do_ref, f32[4,8,1024]{2,1,0:T(8,128)S(1)} %get-tuple-element.132.lse_ref, ...), custom_call_target="tpu_custom_call" | custom-call | flops 10000000000 | bytes 30000000 | tf_op jit(solution)/shard_map/pallas_call | solution.py:518
  137.7 9.7 %shard_map.249 = (f32[512,1024]{1,0:T(8,128)S(1)}, bf16[512,1024]{1,0:T(8,128)(2,1)S(1)}, bf16[2048,1024]{1,0:T(8,128)(2,1)S(1)}, bf16[512,1024]{1,0:T(8,128)(2,...) custom-call(f32[512,1024]{1,0:T(8,128)S(1)} %shard_map.248.g_ref, ...), custom_call_target="tpu_custom_call", output_to_operand_aliasing={{2}: (5, {}), {5}: (8, {})} | custom-call | flops 10000000000 | bytes 30000000 | tf_op jit(solution)/shard_map/pallas_call | solution.py:518
  149.7 10.9 %shard_map.250 = (bf16[256,2688]{1,0:T(8,128)(2,1)S(1)}, bf16[256,2688]{1,0:T(8,128)(2,1)}) custom-call(s32[1]{0:T(128)} %bitcast.18.core_ref.refs_0_, bf16[512,1024]{1,0:T(8,128)(2,1)S(1)} %get-tuple-element.146.yr1_ref, bf16[512,1024]{1,0:T(8,128)(2,1)S(1)} %get-tuple-element.147.yr2_ref, bf16[2048,1024]{1,0:T(8,128)(2,1)S(1)} %get-tuple-element.148.du1_ref, ...), custom_call_target="tpu_custom_call" | custom-call | flops 10000000000 | bytes 30000000 | tf_op jit(solution)/shard_map/pallas_call | solution.py:518
  161.1 2.2 copy-done.11
  163.3 2.2 copy-done.13
  167.9 6.5 %shard_map.251 = (bf16[256,2048]{1,0:T(8,128)(2,1)S(1)}, bf16[256,2048]{1,0:T(8,128)(2,1)S(1)}) custom-call(s32[1]{0:T(128)} %bitcast.18.core_ref.refs_0_, bf16[2048,1024]{1,0:T(8,128)(2,1)S(1)} %copy-done.13, bf16[2048,1024]{1,0:T(8,128)(2,1)S(1)} %copy-done.11, bf16[512,1024]{1,0:T(8,128)(2,1)S(1)} %copy-done.23, bf16[512,1024]{1,0:T(8,128)(2,1)S(1)} %copy-done.19), custom_call_target="tpu_custom_call" | custom-call | flops 10000000000 | bytes 30000000 | tf_op jit(solution)/shard_map/pallas_call | solution.py:518
  178.2 4.3 %shard_map.252.refs_3_.refs_0_ = bf16[3,128,1024]{2,1,0:T(8,128)(2,1)S(1)} custom-call(bf16[3,256,1024]{2,1,0:T(8,128)(2,1)S(1)} %copy-done.29, bf16[512,1024]{1,0:T(8,128)(2,1)S(1)} %copy-done.17, bf16[512,1024]{1,0:T(8,128)(2,1)S(1)} %copy-done.21, f32[4,8,1024]{2,1,0:T(8,128)S(1)} %get-tuple-element.162.lse_ref, f32[8,1024]{1,0:T(8,128)S(1)} %broadcast_in_dim.75.seg_ref), custom_call_target="tpu_custom_call" | custom-call | flops 15000000512 | bytes 45000000 | tf_op jit(solution)/shard_map/pallas_call | solution.py:518
  184.6 8.3 %shard_map.253 = (bf16[3,128,1024]{2,1,0:T(8,128)(2,1)S(1)}, bf16[256,768]{1,0:T(8,128)(2,1)S(1)}, bf16[256,768]{1,0:T(8,128)(2,1)S(1)}) custom-call(bf16[3,256,1024]{2,1,0:T(8,128)(2,1)S(1)} %copy-done.29, bf16[512,1024]{1,0:T(8,128)(2,1)S(1)} %copy-done.17, bf16[512,1024]{1,0:T(8,128)(2,1)S(1)} %copy-done.21, ...), custom_call_target="tpu_custom_call" | custom-call | flops 15000000512 | bytes 45000000 | tf_op jit(solution)/shard_map/pallas_call | solution.py:518
  199.0 4.3 %shard_map.254.refs_3_.refs_2_ = bf16[3,128,1024]{2,1,0:T(8,128)(2,1)S(1)} custom-call(bf16[3,256,1024]{2,1,0:T(8,128)(2,1)S(1)} %copy-done.27, bf16[512,1024]{1,0:T(8,128)(2,1)S(1)} %copy-done.17, bf16[512,1024]{1,0:T(8,128)(2,1)S(1)} %copy-done.21, f32[4,8,1024]{2,1,0:T(8,128)S(1)} %get-tuple-element.145.lse_ref, f32[8,1024]{1,0:T(8,128)S(1)} %broadcast_in_dim.75.seg_ref), custom_call_target="tpu_custom_call" | custom-call | flops 15000000512 | bytes 45000000 | tf_op jit(solution)/shard_map/pallas_call | solution.py:518
  208.4 2.6 collective-permute-start.14
  211.2 8.3 %shard_map.255 = (bf16[3,128,1024]{2,1,0:T(8,128)(2,1)S(1)}, bf16[256,768]{1,0:T(8,128)(2,1)S(1)}, bf16[256,768]{1,0:T(8,128)(2,1)S(1)}) custom-call(bf16[3,256,1024]{2,1,0:T(8,128)(2,1)S(1)} %copy-done.27, bf16[512,1024]{1,0:T(8,128)(2,1)S(1)} %copy-done.17, bf16[512,1024]{1,0:T(8,128)(2,1)S(1)} %copy-done.21, ...), custom_call_target="tpu_custom_call" | custom-call | flops 15000000512 | bytes 45000000 | tf_op jit(solution)/shard_map/pallas_call | solution.py:518
  220.9 3.4 %shard_map.256 = f32[1024,512]{1,0:T(8,128)} custom-call(bf16[512,1536]{1,0:T(8,128)(2,1)S(1)} %bitcast.107, f32[512,1024]{1,0:T(8,128)S(1)} %copy-done.15, bf16[3,128,1024]{2,1,0:T(8,128)(2,1)S(1)} %shard_map.252.refs_3_.refs_0_, bf16[3,128,1024]{2,1,0:T(8,128)(2,1)S(1)} %get-tuple-element.168.refs_1_, ...), custom_call_target="tpu_custom_call" | custom-call | flops 15000000512 | bytes 45000000 | tf_op jit(solution)/shard_map/pallas_call | solution.py:518
  224.4 2.2 collective-permute-start.23
  231.6 3.3 %collective-permute-done.18 = bf16[2,2,2,16,768]{4,3,2,1,0:T(8,128)(2,1)S(1)} collective-permute-done((bf16[2,2,2,16,768]{4,3,2,1,0:T(8,128)(2,1)S(1)}, bf16[2,2,2,16,768]{4,3,2,1,0:T(8,128)(2,1)S(1)}, u32[]{:S(2)}, u32[]{:S(2)}) %collective-permute-start.18) | collective-permute-done | bytes 196640 | tf_op jit(solution)/shard_map/ppermute | solution.py:534
  236.5 3.4 %collective-permute-done.24 = bf16[16,4736]{1,0:T(8,128)(2,1)S(1)} collective-permute-done((bf16[16,4736]{1,0:T(8,128)(2,1)S(1)}, bf16[16,4736]{1,0:T(8,128)(2,1)S(1)}, u32[]{:S(2)}, u32[]{:S(2)}) %collective-permute-start.24) | collective-permute-done | bytes 151584 | tf_op jit(solution)/shard_map/ppermute | solution.py:534
  245.4 2.5 collective-permute-done.21
  247.9 2.6 collective-permute-done.22
  252.0 3.0 %collective-permute-start.28 = (bf16[16,1536]{1,0:T(8,128)(2,1)S(1)}, bf16[16,1536]{1,0:T(8,128)(2,1)S(1)}, u32[]{:S(2)}, u32[]{:S(2)}) collective-permute-start(bf16[16,1536]{1,0:T(8,128)(2,1)S(1)} %add_convert_fusion.10), channel_id=1, source_target_pairs={{0,24},{2,26},{4,28},{6,30},{8,16},{10,18},{12,20},{14,22},{16,8},... | collective-permute-start | bytes 147464 | tf_op jit(solution)/shard_map/ppermute | solution.py:534
  260.0 5.8 %collective-permute-done.29 = bf16[2,2,1,16,1536]{4,3,2,1,0:T(8,128)(2,1)S(1)} collective-permute-done((bf16[2,2,1,16,1536]{4,3,2,1,0:T(8,128)(2,1)S(1)}, bf16[2,2,1,16,1536]{4,3,2,1,0:T(8,128)(2,1)S(1)}, u32[]{:S(2)}, u32[]{:S(2)}) %collective-permute-start.29) | collective-permute-done | bytes 196640 | tf_op jit(solution)/shard_map/ppermute | solution.py:534
  266.0 6.9 %collective-permute-done.31 = bf16[2,2,1,16,4736]{4,3,2,1,0:T(8,128)(2,1)S(1)} collective-permute-done((bf16[2,2,1,16,4736]{4,3,2,1,0:T(8,128)(2,1)S(1)}, bf16[2,2,1,16,4736]{4,3,2,1,0:T(8,128)(2,1)S(1)}, u32[]{:S(2)}, u32[]{:S(2)}) %collective-permute-start.31) | collective-permute-done | bytes 606240 | tf_op jit(solution)/shard_map/ppermute | solution.py:534
  (214 shorter events, 68.7 us)
Async XLA Ops:
  4.0 12.2 %collective-permute-start = (bf16[1,128,1536]{2,1,0:T(8,128)(2,1)S(1)}, bf16[1,128,1536]{2,1,0:T(8,128)(2,1)}, u32[]{:S(2)}, u32[]{:S(2)}) collective-permute-start(bf16[1,128,1536]{2,1,0:T(8,128)(2,1)S(1)} %bitcast_dynamic-update-slice_fusion), channel_id=1, source_target_pairs={{0,1},{1,0},{2,3},{3,2},{4,5},{5,4},{6,7},{7,6},{8,9},{9,8},{10,11... | collective-permute-start | bytes 1179656 | tf_op jit(solution)/shard_map/ppermute | solution.py:534
  18.1 17.9 %collective-permute-start.2 = (bf16[1,128,2688]{2,1,0:T(8,128)(2,1)S(1)}, bf16[1,128,2688]{2,1,0:T(8,128)(2,1)S(1)}, u32[]{:S(2)}, u32[]{:S(2)}) collective-permute-start(bf16[1,128,2688]{2,1,0:T(8,128)(2,1)S(1)} %pad_maximum_fusion), channel_id=1, source_target_pairs={{0,1},{1,0},{2,3},{3,2},{4,5},{5,4},{6,7},{7,6},{8,9},{9,8},{10,11... | collective-permute-start | bytes 2064392 | tf_op jit(solution)/shard_map/ppermute | solution.py:534
  36.2 14.8 %collective-permute-start.3 = (bf16[2,128,2688]{2,1,0:T(8,128)(2,1)S(1)}, bf16[2,128,2688]{2,1,0:T(8,128)(2,1)S(1)}, u32[]{:S(2)}, u32[]{:S(2)}) collective-permute-start(bf16[2,128,2688]{2,1,0:T(8,128)(2,1)S(1)} %maximum_select_fusion.3), channel_id=1, source_target_pairs={{0,2},{2,0},{4,6},{6,4},{8,10},{10,8},{12,14},{14,12},{16,18},{18,... | collective-permute-start | bytes 4128776 | tf_op jit(solution)/shard_map/ppermute | solution.py:534
  36.3 14.4 %collective-permute-start.4 = (bf16[1,128,2048]{2,1,0:T(8,128)(2,1)S(1)}, bf16[1,128,2048]{2,1,0:T(8,128)(2,1)S(1)}, u32[]{:S(2)}, u32[]{:S(2)}) collective-permute-start(bf16[1,128,2048]{2,1,0:T(8,128)(2,1)S(1)} %pad_maximum_fusion.2), channel_id=1, source_target_pairs={{0,1},{1,0},{2,3},{3,2},{4,5},{5,4},{6,7},{7,6},{8,9},{9,8},{10,11... | collective-permute-start | bytes 1572872 | tf_op jit(solution)/shard_map/ppermute | solution.py:534
  50.9 9.1 %collective-permute-start.5 = (bf16[2,128,2048]{2,1,0:T(8,128)(2,1)S(1)}, bf16[2,128,2048]{2,1,0:T(8,128)(2,1)S(1)}, u32[]{:S(2)}, u32[]{:S(2)}) collective-permute-start(bf16[2,128,2048]{2,1,0:T(8,128)(2,1)S(1)} %maximum_select_fusion.5), channel_id=1, source_target_pairs={{0,2},{2,0},{4,6},{6,4},{8,10},{10,8},{12,14},{14,12},{16,18},{18,... | collective-permute-start | bytes 3145736 | tf_op jit(solution)/shard_map/ppermute | solution.py:534
  160.6 13.8 %collective-permute-start.6 = (bf16[256,2688]{1,0:T(8,128)(2,1)}, bf16[256,2688]{1,0:T(8,128)(2,1)}, u32[]{:S(2)}, u32[]{:S(2)}) collective-permute-start(bf16[256,2688]{1,0:T(8,128)(2,1)} %get-tuple-element.154), channel_id=1, source_target_pairs={{0,2},{2,0},{4,6},{6,4},{8,10},{10,8},{12,14},{14,12},{16,18},{18,... | collective-permute-start | bytes 4128776 | tf_op jit(solution)/shard_map/ppermute | solution.py:534
  176.4 17.4 %collective-permute-start.8 = (bf16[2,2,2,16,2688]{4,3,2,1,0:T(8,128)(2,1)S(1)}, bf16[2,2,2,16,2688]{4,3,2,1,0:T(8,128)(2,1)S(1)}, u32[]{:S(2)}, u32[]{:S(2)}) collective-permute-start(bf16[2,2,2,16,2688]{4,3,2,1,0:T(8,128)(2,1)S(1)} %get-tuple-element.195), channel_id=1, source_target_pairs={{0,1},{1,0},{2,3},{3,2},{4,5},{5,4},{6,7},{7,6},{8,9},{9,8},{10,11... | collective-permute-start | bytes 2064392 | tf_op jit(solution)/shard_map/ppermute | solution.py:534
  178.2 4.3 %collective-permute-start.7 = (bf16[256,2048]{1,0:T(8,128)(2,1)S(1)}, bf16[256,2048]{1,0:T(8,128)(2,1)S(1)}, u32[]{:S(2)}, u32[]{:S(2)}) collective-permute-start(bf16[256,2048]{1,0:T(8,128)(2,1)S(1)} %get-tuple-element.166), channel_id=1, source_target_pairs={{0,2},{2,0},{4,6},{6,4},{8,10},{10,8},{12,14},{14,12},{16,18},{18,... | collective-permute-start | bytes 3145736 | tf_op jit(solution)/shard_map/ppermute | solution.py:534
  183.0 14.8 %collective-permute-start.9 = (bf16[2,2,2,16,2048]{4,3,2,1,0:T(8,128)(2,1)S(1)}, bf16[2,2,2,16,2048]{4,3,2,1,0:T(8,128)(2,1)S(1)}, u32[]{:S(2)}, u32[]{:S(2)}) collective-permute-start(bf16[2,2,2,16,2048]{4,3,2,1,0:T(8,128)(2,1)S(1)} %get-tuple-element.207), channel_id=1, source_target_pairs={{0,4},{2,6},{4,0},{6,2},{8,12},{10,14},{12,8},{14,10},{16,20},{18,... | collective-permute-start | bytes 1572872 | tf_op jit(solution)/shard_map/ppermute | solution.py:534
  192.9 10.3 %collective-permute-start.12 = (bf16[256,768]{1,0:T(8,128)(2,1)S(1)}, bf16[256,768]{1,0:T(8,128)(2,1)S(1)}, u32[]{:S(2)}, u32[]{:S(2)}) collective-permute-start(bf16[256,768]{1,0:T(8,128)(2,1)S(1)} %get-tuple-element.171), channel_id=1, source_target_pairs={{0,2},{2,0},{4,6},{6,4},{8,10},{10,8},{12,14},{14,12},{16,18},{18,... | collective-permute-start | bytes 1179656 | tf_op jit(solution)/shard_map/ppermute | solution.py:534
  194.1 10.7 %collective-permute-start.10 = (bf16[2,2,16,2688]{3,2,1,0:T(8,128)(2,1)S(1)}, bf16[2,2,16,2688]{3,2,1,0:T(8,128)(2,1)S(1)}, u32[]{:S(2)}, u32[]{:S(2)}) collective-permute-start(bf16[2,2,16,2688]{3,2,1,0:T(8,128)(2,1)S(1)} %get-tuple-element.213), channel_id=1, source_target_pairs={{0,4},{2,6},{4,0},{6,2},{8,12},{10,14},{12,8},{14,10},{16,20},{18,... | collective-permute-start | bytes 1032200 | tf_op jit(solution)/shard_map/ppermute | solution.py:534
  198.0 8.6 %collective-permute-start.11 = (bf16[2,2,16,2048]{3,2,1,0:T(8,128)(2,1)S(1)}, bf16[2,2,16,2048]{3,2,1,0:T(8,128)(2,1)S(1)}, u32[]{:S(2)}, u32[]{:S(2)}) collective-permute-start(bf16[2,2,16,2048]{3,2,1,0:T(8,128)(2,1)S(1)} %get-tuple-element.219), channel_id=1, source_target_pairs={{0,1},{1,0},{2,3},{3,2},{4,5},{5,4},{6,7},{7,6},{8,9},{9,8},{10,11... | collective-permute-start | bytes 786440 | tf_op jit(solution)/shard_map/ppermute | solution.py:534
  203.4 26.0 %collective-permute-start.17 = (bf16[2,2,2,16,768]{4,3,2,1,0:T(8,128)(2,1)S(1)}, bf16[2,2,2,16,768]{4,3,2,1,0:T(8,128)(2,1)S(1)}, u32[]{:S(2)}, u32[]{:S(2)}) collective-permute-start(bf16[2,2,2,16,768]{4,3,2,1,0:T(8,128)(2,1)S(1)} %get-tuple-element.233), channel_id=1, source_target_pairs={{0,1},{1,0},{2,3},{3,2},{4,5},{5,4},{6,7},{7,6},{8,9},{9,8},{10,11... | collective-permute-start | bytes 589832 | tf_op jit(solution)/shard_map/ppermute | solution.py:534
  206.8 12.9 %collective-permute-start.13 = (bf16[16,4736]{1,0:T(8,128)(2,1)S(1)}, bf16[16,4736]{1,0:T(8,128)(2,1)S(1)}, u32[]{:S(2)}, u32[]{:S(2)}) collective-permute-start(bf16[16,4736]{1,0:T(8,128)(2,1)S(1)} %get-tuple-element.214), channel_id=1, source_target_pairs={{0,8},{2,10},{4,12},{6,14},{8,0},{10,2},{12,4},{14,6},{16,24},{18,... | collective-permute-start | bytes 454664 | tf_op jit(solution)/shard_map/ppermute | solution.py:534
  208.4 12.4 %collective-permute-start.14 = (bf16[16,4736]{1,0:T(8,128)(2,1)S(1)}, bf16[16,4736]{1,0:T(8,128)(2,1)S(1)}, u32[]{:S(2)}, u32[]{:S(2)}) collective-permute-start(bf16[16,4736]{1,0:T(8,128)(2,1)S(1)} %get-tuple-element.216), channel_id=1, source_target_pairs={{0,16},{2,18},{4,20},{6,22},{8,24},{10,26},{12,28},{14,30},{16,0},... | collective-permute-start | bytes 454664 | tf_op jit(solution)/shard_map/ppermute | solution.py:534
  211.0 9.8 %collective-permute-start.15 = (bf16[16,4736]{1,0:T(8,128)(2,1)S(1)}, bf16[16,4736]{1,0:T(8,128)(2,1)S(1)}, u32[]{:S(2)}, u32[]{:S(2)}) collective-permute-start(bf16[16,4736]{1,0:T(8,128)(2,1)S(1)} %get-tuple-element.215), channel_id=1, source_target_pairs={{0,24},{2,26},{4,28},{6,30},{8,16},{10,18},{12,20},{14,22},{16,8},... | collective-permute-start | bytes 454664 | tf_op jit(solution)/shard_map/ppermute | solution.py:534
  219.6 4.8 %collective-permute-start.16 = (bf16[256,768]{1,0:T(8,128)(2,1)S(1)}, bf16[256,768]{1,0:T(8,128)(2,1)S(1)}, u32[]{:S(2)}, u32[]{:S(2)}) collective-permute-start(bf16[256,768]{1,0:T(8,128)(2,1)S(1)} %get-tuple-element.178), channel_id=1, source_target_pairs={{0,2},{2,0},{4,6},{6,4},{8,10},{10,8},{12,14},{14,12},{16,18},{18,... | collective-permute-start | bytes 1179656 | tf_op jit(solution)/shard_map/ppermute | solution.py:534
  224.4 7.1 %collective-permute-start.23 = (bf16[16,4736]{1,0:T(8,128)(2,1)S(1)}, bf16[16,4736]{1,0:T(8,128)(2,1)S(1)}, u32[]{:S(2)}, u32[]{:S(2)}) collective-permute-start(bf16[16,4736]{1,0:T(8,128)(2,1)S(1)} %add_convert_fusion.9), channel_id=1, source_target_pairs={{0,8},{2,10},{4,12},{6,14},{8,0},{10,2},{12,4},{14,6},{16,24},{18,... | collective-permute-start | bytes 454664 | tf_op jit(solution)/shard_map/ppermute | solution.py:534
  226.7 13.2 %collective-permute-start.24 = (bf16[16,4736]{1,0:T(8,128)(2,1)S(1)}, bf16[16,4736]{1,0:T(8,128)(2,1)S(1)}, u32[]{:S(2)}, u32[]{:S(2)}) collective-permute-start(bf16[16,4736]{1,0:T(8,128)(2,1)S(1)} %add_convert_fusion.9), channel_id=1, source_target_pairs={{0,16},{2,18},{4,20},{6,22},{8,24},{10,26},{12,28},{14,30},{16,0},... | collective-permute-start | bytes 454664 | tf_op jit(solution)/shard_map/ppermute | solution.py:534
  227.8 12.1 %collective-permute-start.25 = (bf16[16,4736]{1,0:T(8,128)(2,1)S(1)}, bf16[16,4736]{1,0:T(8,128)(2,1)S(1)}, u32[]{:S(2)}, u32[]{:S(2)}) collective-permute-start(bf16[16,4736]{1,0:T(8,128)(2,1)S(1)} %add_convert_fusion.9), channel_id=1, source_target_pairs={{0,24},{2,26},{4,28},{6,30},{8,16},{10,18},{12,20},{14,22},{16,8},... | collective-permute-start | bytes 454664 | tf_op jit(solution)/shard_map/ppermute | solution.py:534
  229.2 5.7 %collective-permute-start.18 = (bf16[2,2,2,16,768]{4,3,2,1,0:T(8,128)(2,1)S(1)}, bf16[2,2,2,16,768]{4,3,2,1,0:T(8,128)(2,1)S(1)}, u32[]{:S(2)}, u32[]{:S(2)}) collective-permute-start(bf16[2,2,2,16,768]{4,3,2,1,0:T(8,128)(2,1)S(1)} %dynamic-slice_bitcast_fusion.9), channel_id=1, source_target_pairs={{0,1},{1,0},{2,3},{3,2},{4,5},{5,4},{6,7},{7,6},{8,9},{9,8},{10,11... | collective-permute-start | bytes 589832 | tf_op jit(solution)/shard_map/ppermute | solution.py:534
  235.0 5.7 %collective-permute-start.19 = (bf16[2,2,16,1536]{3,2,1,0:T(8,128)(2,1)S(1)}, bf16[2,2,16,1536]{3,2,1,0:T(8,128)(2,1)S(1)}, u32[]{:S(2)}, u32[]{:S(2)}) collective-permute-start(bf16[2,2,16,1536]{3,2,1,0:T(8,128)(2,1)S(1)} %fusion.5), channel_id=1, source_target_pairs={{0,4},{2,6},{4,0},{6,2},{8,12},{10,14},{12,8},{14,10},{16,20},{18,... | collective-permute-start | bytes 589832 | tf_op jit(solution)/shard_map/ppermute | solution.py:534
  240.8 4.7 %collective-permute-start.20 = (bf16[16,1536]{1,0:T(8,128)(2,1)S(1)}, bf16[16,1536]{1,0:T(8,128)(2,1)S(1)}, u32[]{:S(2)}, u32[]{:S(2)}) collective-permute-start(bf16[16,1536]{1,0:T(8,128)(2,1)S(1)} %get-tuple-element.240), channel_id=1, source_target_pairs={{0,8},{2,10},{4,12},{6,14},{8,0},{10,2},{12,4},{14,6},{16,24},{18,... | collective-permute-start | bytes 147464 | tf_op jit(solution)/shard_map/ppermute | solution.py:534
  242.4 5.5 %collective-permute-start.21 = (bf16[16,1536]{1,0:T(8,128)(2,1)S(1)}, bf16[16,1536]{1,0:T(8,128)(2,1)S(1)}, u32[]{:S(2)}, u32[]{:S(2)}) collective-permute-start(bf16[16,1536]{1,0:T(8,128)(2,1)S(1)} %get-tuple-element.242), channel_id=1, source_target_pairs={{0,16},{2,18},{4,20},{6,22},{8,24},{10,26},{12,28},{14,30},{16,0},... | collective-permute-start | bytes 147464 | tf_op jit(solution)/shard_map/ppermute | solution.py:534
  244.3 6.2 %collective-permute-start.22 = (bf16[16,1536]{1,0:T(8,128)(2,1)S(1)}, bf16[16,1536]{1,0:T(8,128)(2,1)S(1)}, u32[]{:S(2)}, u32[]{:S(2)}) collective-permute-start(bf16[16,1536]{1,0:T(8,128)(2,1)S(1)} %get-tuple-element.241), channel_id=1, source_target_pairs={{0,24},{2,26},{4,28},{6,30},{8,16},{10,18},{12,20},{14,22},{16,8},... | collective-permute-start | bytes 147464 | tf_op jit(solution)/shard_map/ppermute | solution.py:534
  250.6 4.5 %collective-permute-start.26 = (bf16[16,1536]{1,0:T(8,128)(2,1)S(1)}, bf16[16,1536]{1,0:T(8,128)(2,1)S(1)}, u32[]{:S(2)}, u32[]{:S(2)}) collective-permute-start(bf16[16,1536]{1,0:T(8,128)(2,1)S(1)} %add_convert_fusion.10), channel_id=1, source_target_pairs={{0,8},{2,10},{4,12},{6,14},{8,0},{10,2},{12,4},{14,6},{16,24},{18,... | collective-permute-start | bytes 147464 | tf_op jit(solution)/shard_map/ppermute | solution.py:534
  250.6 5.1 %collective-permute-start.27 = (bf16[16,1536]{1,0:T(8,128)(2,1)S(1)}, bf16[16,1536]{1,0:T(8,128)(2,1)S(1)}, u32[]{:S(2)}, u32[]{:S(2)}) collective-permute-start(bf16[16,1536]{1,0:T(8,128)(2,1)S(1)} %add_convert_fusion.10), channel_id=1, source_target_pairs={{0,16},{2,18},{4,20},{6,22},{8,24},{10,26},{12,28},{14,30},{16,0},... | collective-permute-start | bytes 147464 | tf_op jit(solution)/shard_map/ppermute | solution.py:534
  252.0 5.9 %collective-permute-start.28 = (bf16[16,1536]{1,0:T(8,128)(2,1)S(1)}, bf16[16,1536]{1,0:T(8,128)(2,1)S(1)}, u32[]{:S(2)}, u32[]{:S(2)}) collective-permute-start(bf16[16,1536]{1,0:T(8,128)(2,1)S(1)} %add_convert_fusion.10), channel_id=1, source_target_pairs={{0,24},{2,26},{4,28},{6,30},{8,16},{10,18},{12,20},{14,22},{16,8},... | collective-permute-start | bytes 147464 | tf_op jit(solution)/shard_map/ppermute | solution.py:534
  257.9 7.9 %collective-permute-start.29 = (bf16[2,2,1,16,1536]{4,3,2,1,0:T(8,128)(2,1)S(1)}, bf16[2,2,1,16,1536]{4,3,2,1,0:T(8,128)(2,1)S(1)}, u32[]{:S(2)}, u32[]{:S(2)}) collective-permute-start(bf16[2,2,1,16,1536]{4,3,2,1,0:T(8,128)(2,1)S(1)} %bitcast.122), channel_id=1, source_target_pairs={{0,4},{2,6},{4,0},{6,2},{8,12},{10,14},{12,8},{14,10},{16,20},{18,... | collective-permute-start | bytes 589832 | tf_op jit(solution)/shard_map/ppermute | solution.py:534
  259.5 13.4 %collective-permute-start.31 = (bf16[2,2,1,16,4736]{4,3,2,1,0:T(8,128)(2,1)S(1)}, bf16[2,2,1,16,4736]{4,3,2,1,0:T(8,128)(2,1)S(1)}, u32[]{:S(2)}, u32[]{:S(2)}) collective-permute-start(bf16[2,2,1,16,4736]{4,3,2,1,0:T(8,128)(2,1)S(1)} %bitcast.115), channel_id=1, source_target_pairs={{0,4},{2,6},{4,0},{6,2},{8,12},{10,14},{12,8},{14,10},{16,20},{18,... | collective-permute-start | bytes 1818632 | tf_op jit(solution)/shard_map/ppermute | solution.py:534
  265.9 7.4 %collective-permute-start.30 = (bf16[128,1536]{1,0:T(8,128)(2,1)S(1)}, bf16[128,1536]{1,0:T(8,128)(2,1)S(1)}, u32[]{:S(2)}, u32[]{:S(2)}) collective-permute-start(bf16[128,1536]{1,0:T(8,128)(2,1)S(1)} %bitcast.117), channel_id=1, source_target_pairs={{0,2},{2,0},{4,6},{6,4},{8,10},{10,8},{12,14},{14,12},{16,18},{18,... | collective-permute-start | bytes 1179656 | tf_op jit(solution)/shard_map/ppermute | solution.py:534
  273.1 3.0 %collective-permute-start.32 = (bf16[128,4736]{1,0:T(8,128)(2,1)S(1)}, bf16[128,4736]{1,0:T(8,128)(2,1)S(1)}, u32[]{:S(2)}, u32[]{:S(2)}) collective-permute-start(bf16[128,4736]{1,0:T(8,128)(2,1)S(1)} %bitcast.109), channel_id=1, source_target_pairs={{0,2},{2,0},{4,6},{6,4},{8,10},{10,8},{12,14},{14,12},{16,18},{18,... | collective-permute-start | bytes 3637256 | tf_op jit(solution)/shard_map/ppermute | solution.py:534
  (37 other events, 318.3 us)

commit v2 on v1

--- a/solution.py
+++ b/solution.py
@@ -144,8 +144,10 @@
 def attend_kernel(first, size, x_ref, w_ref, seg_ref, *refs):
     if first:
         group, w_t_ref = first - 1, refs[0]
-        count = w_t_ref.shape[0]
-        w_t_ref[...] = w_ref[:, group * count : (group + 1) * count].T
+        count = w_t_ref.shape[0] // 3
+        for i in range(3):
+            at = i * x_ref.shape[0] + group * count
+            w_t_ref[i * count : (i + 1) * count, :] = w_ref[:, at : at + count].T
         refs = refs[1:]
     else:
         w_t_ref = w_ref
@@ -374,7 +376,21 @@
             send_ref[rows, cols] = part
 
 
-def outer_grad_kernel(shards, core_ref, z1_ref, z2_ref, dfr1_ref, dfr2_ref, keep_ref, send_ref):
+def outer_grad_kernel(
+    shards,
+    core_ref,
+    z1_ref,
+    z2_ref,
+    dfr1_ref,
+    dfr2_ref,
+    o1_ref,
+    o2_ref,
+    dar1_ref,
+    dar2_ref,
+    acc_ref,
+    keep_ref,
+    send_ref,
+):
     core = core_ref[0]
     hidden, width = z1_ref.shape[0], dfr1_ref.shape[0]
     unit = width // shards // 2
@@ -390,30 +406,6 @@
             cols = slice(group * width, (group + 1) * width)
             rows = dwu[at : at + per_group]
             place(rows, shard * per_group, unit, core, keep_ref, send_ref, cols)
-
-
-def inner_grad_kernel(
-    shards,
-    core_ref,
-    yr1_ref,
-    yr2_ref,
-    du1_ref,
-    du2_ref,
-    o1_ref,
-    o2_ref,
-    dar1_ref,
-    dar2_ref,
-    acc_ref,
-    keep_ref,
-    send_ref,
-):
-    core = core_ref[0]
-    width, hidden = yr1_ref.shape[0], du1_ref.shape[0]
-    unit = width // shards // 2
-    for first in range(0, hidden, CHUNK):
-        part = slice(first, first + CHUNK)
-        dwi_t = nt(du1_ref[part, :], yr1_ref[...]) + nt(du2_ref[part, :], yr2_ref[...])
-        place(dwi_t.astype(bf16).T, 0, unit, core, keep_ref, send_ref, part)
     for first in range(0, width, CHUNK):
         part = slice(first, first + CHUNK)
         cols = slice(hidden + first, hidden + first + CHUNK)
@@ -425,6 +417,18 @@
         dpar = jnp.where(lane == i, jnp.sum(acc_ref[i], axis=1, keepdims=True), dpar)
     last = slice(hidden + width, hidden + width + 128)
     place(dpar.astype(bf16), 0, unit, core, keep_ref, send_ref, last)
+
+
+def inner_grad_kernel(
+    shards, core_ref, yr1_ref, yr2_ref, du1_ref, du2_ref, keep_ref, send_ref
+):
+    core = core_ref[0]
+    width, hidden = yr1_ref.shape[0], du1_ref.shape[0]
+    unit = width // shards // 2
+    for first in range(0, hidden, CHUNK):
+        part = slice(first, first + CHUNK)
+        dwi_t = nt(du1_ref[part, :], yr1_ref[...]) + nt(du2_ref[part, :], yr2_ref[...])
+        place(dwi_t.astype(bf16).T, 0, unit, core, keep_ref, send_ref, part)
 
 
 def attend_back_kernel(first, size, qkv_ref, o_ref, do_ref, lse_ref, seg_ref, dqkv_ref, *refs):
@@ -494,13 +498,11 @@
     parts, grad_ref, join_ref = refs[:-2], refs[-2], refs[-1]
     length = dh_ref.shape[1]
     at = 0
-    each = len(parts) // 2
-    for group in range(2):
-        for i in range(3):
-            for part in parts[group * each : (group + 1) * each]:
-                rows = part.shape[1]
-                join_ref[at : at + rows, :] = part[i]
-                at += rows
+    for i in range(3):
+        for part in parts:
+            rows = part.shape[1]
+            join_ref[at : at + rows, :] = part[i]
+            at += rows
     for at in range(0, length, B):
         cols = slice(at, at + B)
         grad = dh_ref[:, cols] + nn(w_ref[...], join_ref[:, cols])
@@ -514,11 +516,16 @@
 SM = pl.BlockSpec(memory_space=pltpu.SMEM)
 
 
-def call(kernel, outs, scratch, args, specs=None, cost=10, limit=8, alias={}):
+def call(kernel, outs, scratch, args, specs=None, cost=10, limit=6, alias={}, deps=()):
+    count, after = len(args), len(args) + len(deps)
+
+    def run(*refs):
+        kernel(*refs[:count], *refs[after:])
+
     return pl.pallas_call(
-        kernel,
+        run,
         out_shape=[jax.ShapeDtypeStruct(shape, dtype) for shape, dtype in outs],
-        in_specs=specs if specs else [VM] * len(args),
+        in_specs=(specs if specs else [VM] * count) + [pl.BlockSpec(memory_space=pl.ANY)] * len(deps),
         out_specs=[VM] * len(outs),
         scratch_shapes=[pltpu.VMEM(*one) for one in scratch],
         input_output_aliases=alias,
@@ -526,7 +533,7 @@
             flops=cost * 1000000000, bytes_accessed=cost * 3000000, transcendentals=0
         ),
         compiler_params=pltpu.CompilerParams(vmem_limit_bytes=limit * 2**20),
-    )(*args)
+    )(*args, *deps)
 
 
 def flip(value, axis, bit):
@@ -661,6 +668,17 @@
         return both(bit_of("dp", 1), mine, other, 0).astype(f32)
 
 
+def copy_kernel(value_ref, copy_ref):
+    copy_ref[...] = value_ref[...]
+
+
+def copy_after(value, *deps):
+    flat = value.reshape(-1, value.shape[-1])
+    out = [(flat.shape, flat.dtype)]
+    (copy,) = call(copy_kernel, out, [], (flat,), None, 1, deps=deps)
+    return copy.reshape(value.shape)
+
+
 def join(*sums):
     for one in sums:
         one.settle()
@@ -700,8 +718,7 @@
     shapes = [((3, rows, length), bf16), ((rows, length), bf16), ((H // 2, 8, length), f32)]
 
     half = width // 2
-    cols = [w[:, at : at + half] for at in (0, half) for w in qkv]
-    packed = jnp.concatenate([my_half(w) for w in cols], axis=-1)
+    packed = jnp.concatenate([my_half(w) for w in qkv], axis=-1)
     mine = Gather(packed).merge()
     wqkv = over_cores(mine)
     wio_part, wu_part = later(packed)
@@ -734,8 +751,8 @@
         (y1, z1, wio, wu_groups),
     )
     attend = functools.partial(attend_kernel, 0, size)
-    qkv2a, o2a, lse2a = call(attend, shapes, [bias], (x2, wa_t, seg_rows), limit=8)
-    qkv2b, o2b, lse2b = call(attend, shapes, [bias], (x2, wb_t, seg_rows), limit=8)
+    qkv2a, o2a, lse2a = call(attend, shapes, [bias], (x2, wa_t, seg_rows), limit=6)
+    qkv2b, o2b, lse2b = call(attend, shapes, [bias], (x2, wb_t, seg_rows), limit=6)
     o2, mixed, z2, du2, yr2, dfr2, dar2, dh2, do2, acc = call(
         feed_last_kernel,
         [tall, ((length, width), bf16), wide, wide, tall, tall, tall, tall32, tall]
@@ -748,10 +765,10 @@
     dqkv2 = []
     for group, (qkv, lse) in enumerate(((qkv2a, lse2a), (qkv2b, lse2b))):
         kernel = functools.partial(attend_back_kernel, group * rows, size)
-        dqkv2 += call(kernel, shapes[:1], back, (qkv, o2, do2, lse, seg_rows), limit=14)
+        dqkv2 += call(kernel, shapes[:1], back, (qkv, o2, do2, lse, seg_rows), limit=10)
     joined = [((3 * width, length), bf16)]
     (grad1,) = call(
-        functools.partial(input_kernel, False), [tall32], joined, (wqkv, dh2, *dqkv2), None, 3, 8
+        functools.partial(input_kernel, False), [tall32], joined, (wqkv, dh2, *dqkv2), None, 3, 4
     )
     dh1, do1, du1, dfr1, dar1, acc = call(
         feed_back_kernel,
@@ -760,20 +777,23 @@
         (grad1, n11, n21, stat11, stat12, slope1, wio, wu, acc),
         alias={5: 2, 8: 5},
     )
+    keep_u, send_u = call(
+        functools.partial(outer_grad_kernel, shards),
+        [((half, hidden + width + 128), bf16)] * 2,
+        [],
+        (core, z1, z2, dfr1, dfr2, o1, o2, dar1, dar2, acc),
+        [SM] + [VM] * 9,
+        limit=4,
+    )
+    outer = Sum(keep_u, send_u)
     keep_i, send_i = call(
         functools.partial(inner_grad_kernel, shards),
-        [((half, hidden + width + 128), bf16)] * 2,
-        [],
-        (core, yr1, yr2, du1, du2, o1, o2, dar1, dar2, acc),
-        [SM] + [VM] * 9,
-    )
-    inner = Sum(keep_i, send_i)
-    keep_u, send_u = call(
-        functools.partial(outer_grad_kernel, shards),
         [((half, hidden), bf16)] * 2,
         [],
-        (tie(core, send_i), z1, z2, dfr1, dfr2),
+        (core, yr1, yr2, du1, du2),
         [SM] + [VM] * 4,
+        limit=4,
+        deps=(send_u,),
     )
     parts = []
 
@@ -787,45 +807,35 @@
             specs += [SM] + [VM] * 4
             outs += [((half, 3 * rows), bf16)] * 2
         kernel = functools.partial(attend_part_kernel, p, size, shards)
-        results = call(kernel, outs, back, args, specs, 15, 14)
+        results = call(kernel, outs, back, args, specs, 15, 10)
         parts.append(results[0])
         return results[1:]
 
     y_bit = bits_of("dp")[-2]
     x_bits = bits_of("shard")
-    inner.after(send_u)
+    outer.after(send_i)
+    for label in x_bits:
+        outer.halve(*label)
+    inner = Sum(keep_i, tie(send_i, outer.sent))
+    part(0, tie(seg_rows, outer.sent))
+    inner.after(parts[0])
+    inner.halve(*y_bit)
+    first = Sum(*part(1, tie(seg_rows, inner.sent)))
+    outer.after(parts[1])
+    outer.halve(*y_bit)
+    inner.after(parts[1])
     for label in x_bits:
         inner.halve(*label)
-    outer = Sum(keep_u, tie(send_u, inner.sent))
-    part(0, tie(seg_rows, inner.sent))
-    outer.after(parts[0])
-    outer.halve(*y_bit)
-    first = Sum(*part(1, tie(seg_rows, outer.sent)))
-    inner.after(parts[1])
-    inner.halve(*y_bit)
-    outer.after(parts[1])
-    for label in x_bits:
-        outer.halve(*label)
     part(2, tie(seg_rows, inner.sent, outer.sent, first.sent))
     for one in (first, inner, outer):
         one.after(parts[2])
     for label in x_bits:
         first.halve(*label)
-    feed = join(inner, outer)
+    feed = join(outer, inner)
     feed.scatter()
     second = Sum(*part(3, tie(seg_rows, feed.keep, first.sent)))
     feed.after(second.sent)
     feed.settle()
-    (input_grad,) = call(
-        functools.partial(input_kernel, True),
-        [((length, width), f32)],
-        joined,
-        (wqkv, tie(dh1, second.sent, feed.value), *parts),
-        None,
-        15,
-        10,
-    )
-    second.after(input_grad)
     for label in x_bits:
         second.halve(*label)
     feed.after(second.sent)
@@ -833,17 +843,35 @@
     first.after(second.sent)
     heads = join(first, second)
     heads.halve(*y_bit)
+    (input_grad,) = call(
+        functools.partial(input_kernel, True),
+        [((length, width), f32)],
+        joined,
+        (wqkv, dh1, *parts),
+        None,
+        5,
+        5,
+        deps=(heads.sent,),
+    )
+    feed.double(*y_bit)
+    feed.finish()
     heads.scatter()
     heads.settle()
-    heads.after(feed.value)
-    feed.after(heads.keep)
-    feed.double(*y_bit)
     heads.collect()
-    heads.after(feed.value)
+    inner_at = hidden + width + 128
+    dwu = [feed.columns(at, at + width) for at in range(0, hidden, width)]
+    dwu = jnp.concatenate(dwu, axis=0)
+    dwo = feed.columns(hidden, hidden + width)
+    dpar = feed.columns(hidden + width, inner_at)
+    dwi = feed.columns(inner_at, inner_at + hidden)
+    heads.value = copy_after(heads.value, dwu, dwi, dwo)
     heads.double(*y_bit)
-    feed.finish()
     heads.finish()
-    return mixed, input_grad, feed, heads
+    dqkv = [
+        jnp.concatenate([heads.columns(c, c + half) for c in (at, at + 3 * half)], axis=1)
+        for at in range(0, 3 * half, half)
+    ]
+    return (mixed, input_grad, *dqkv, dwo, dwi, dwu, *(dpar[:, i] for i in range(4)))
 
 
 def body(
@@ -873,28 +901,7 @@
     tokens_total = lax.axis_size("dp") * lax.axis_size("shard") * length
     factor = jnp.float32(tokens_total) / global_count[0].astype(f32)
     scale_rows = jnp.broadcast_to((valid * factor)[None], (8, length))
-    mixed, input_grad, feed, heads = compute(
-        tokens, seg_rows, scale_rows, cotangent, weights, hidden
-    )
-    dqkv = (
-        jnp.concatenate([heads.columns(c, c + half) for c in (at, at + 3 * half)], axis=1)
-        for at in range(0, 3 * half, half)
-    )
-    outer = hidden + width + 128
-    dwu = [feed.columns(at, at + width) for at in range(outer, outer + hidden, width)]
-    dpar = feed.columns(hidden + width, outer)
-    return (
-        mixed,
-        input_grad,
-        *dqkv,
-        feed.columns(hidden, hidden + width),
-        feed.columns(0, hidden),
-        jnp.concatenate(dwu, axis=0),
-        dpar[:, 0],
-        dpar[:, 1],
-        dpar[:, 2],
-        dpar[:, 3],
-    )
+    return compute(tokens, seg_rows, scale_rows, cotangent, weights, hidden)
 
 
 def solution(mesh):

time: 283 us -> 281 us (level)
  waiting for transfers between devices: 50.7 us -> 44.9 us
  local copies, waits for them, and re-layouts: 18.3 us -> 21.4 us
    ppermute x33, waiting for transfers between devices: 50.7 us -> 44.9 us  [flip(): return lax.ppermute(value, axis, [(i, i ^ bit) for i in range(count)])]
    broadcast_in_dim x4 -> x7, local copies, waits for them, and re-layouts: 0.11 us -> 3.92 us  [my_half(): lax.dynamic_slice_in_dim(block, bit_of('dp', 1) * rows, rows, axis=0)[None]]
    slice x4 -> x1, local copies, waits for them, and re-layouts: 4.03 us -> 0.92 us  [compute(): dpar[:, i]]
    unnamed x77 -> x74, local copies, waits for them, and re-layouts: 12.6 us -> 13 us
    pallas_call x19 -> x20, Pallas kernels: 157 us -> 157 us  [call(): pl.pallas_call(run, out_shape=[jax.ShapeDtypeStruct(shape, dtype) for sha...]
  transfers between devices with their start and end apart: 33 -> 33, of which waited for: 19 -> 17; matrix products, arithmetic and copies ran while one was open for 3% -> 3% of each run, Pallas kernels for 22% -> 22%
where the time goes in v2:
time: 281 us; the launch traced here: 279 us
  Pallas kernels  157 us (56%)
  waiting for transfers between devices  44.9 us (16%)
  starting transfers between devices  39.4 us (14%)
  local copies, waits for them, and re-layouts  21.4 us (8%)
  other arithmetic  13.2 us (5%)
  between operations  3.2 us (1%)
    pallas_call x20, Pallas kernels, call(): pl.pallas_call(run, out_shape=[jax.ShapeDtypeStruct(shape, dtype) for sha...  157 us
    ppermute x33, waiting for transfers between devices, flip(): return lax.ppermute(value, axis, [(i, i ^ bit) for i in range(count)])  44.9 us
    ppermute x33, starting transfers between devices, flip(): return lax.ppermute(value, axis, [(i, i ^ bit) for i in range(count)])  39.4 us
    unnamed x74, local copies, waits for them, and re-layouts  13 us
  transfers between devices with their start and end apart: 33, of which 17 were waited for; matrix products, arithmetic and copies ran while one was open for 3% of the time, Pallas kernels for 22%

profile of v2, /device:TPU:0, one launch (start us, length us, event | category | flops | bytes accessed | tf_op | source)
XLA Modules:
  0.0 279.1 jit_solution(1982527106084865420)
XLA Ops:
  4.4 2.9 %collective-permute-start = (bf16[1,128,1536]{2,1,0:T(8,128)(2,1)}, bf16[1,128,1536]{2,1,0:T(8,128)(2,1)}, u32[]{:S(2)}, u32[]{:S(2)}) collective-permute-start(bf16[1,128,1536]{2,1,0:T(8,128)(2,1)} %pad_maximum_fusion.3), channel_id=1, source_target_pairs={{0,1},{1,0},{2,3},{3,2},{4,5},{5,4},{6,7},{7,6},{8,9},{9,8},{10,11... | collective-permute-start | bytes 1179656 | tf_op jit(solution)/shard_map/ppermute | solution.py:541
  13.2 3.5 %collective-permute-done = bf16[1,128,1536]{2,1,0:T(8,128)(2,1)} collective-permute-done((bf16[1,128,1536]{2,1,0:T(8,128)(2,1)}, bf16[1,128,1536]{2,1,0:T(8,128)(2,1)}, u32[]{:S(2)}, u32[]{:S(2)}) %collective-permute-start) | collective-permute-done | bytes 393248 | tf_op jit(solution)/shard_map/ppermute | solution.py:541
  21.1 8.7 %shard_map.239 = (bf16[768,512]{1,0:T(8,128)(2,1)S(1)}, bf16[3,256,1024]{2,1,0:T(8,128)(2,1)S(1)}, bf16[256,1024]{1,0:T(8,128)(2,1)S(1)}, f32[4,8,1024]{2,1,0:T(8,128)S(1)}) custom-call(bf16[512,1024]{1,0:T(8,128)(2,1)S(1)} %shard_map.238.refs_0_.refs_2_.refs_6_, bf16[512,1536]{1,0:T(8,128)(2,1)S(1)} %bitcast.107, f32[8,1024]{1,0:T(8,128)S(1)} %broadcast_in_dim.27.refs_2_.refs_4_), custom_call_target="tpu_custom_call" | custom-call | flops 10000000000 | bytes 30000000 | tf_op jit(solution)/shard_map/pallas_call | solution.py:525
  31.0 5.6 %collective-permute-done.2 = bf16[1,128,2688]{2,1,0:T(8,128)(2,1)S(1)} collective-permute-done((bf16[1,128,2688]{2,1,0:T(8,128)(2,1)S(1)}, bf16[1,128,2688]{2,1,0:T(8,128)(2,1)S(1)}, u32[]{:S(2)}, u32[]{:S(2)}) %collective-permute-start.2) | collective-permute-done | bytes 688160 | tf_op jit(solution)/shard_map/ppermute | solution.py:541
  38.7 8.7 %shard_map.240 = (bf16[768,512]{1,0:T(8,128)(2,1)S(1)}, bf16[3,256,1024]{2,1,0:T(8,128)(2,1)S(1)}, bf16[256,1024]{1,0:T(8,128)(2,1)S(1)}, f32[4,8,1024]{2,1,0:T(8,128)S(1)}) custom-call(bf16[512,1024]{1,0:T(8,128)(2,1)S(1)} %shard_map.238.refs_0_.refs_2_.refs_6_, bf16[512,1536]{1,0:T(8,128)(2,1)S(1)} %bitcast.108, f32[8,1024]{1,0:T(8,128)S(1)} %broadcast_in_dim.27.refs_2_.refs_4_), custom_call_target="tpu_custom_call" | custom-call | flops 10000000000 | bytes 30000000 | tf_op jit(solution)/shard_map/pallas_call | solution.py:525
  48.6 2.7 collective-permute-done.4
  52.6 8.0 %shard_map.241 = (bf16[512,1024]{1,0:T(8,128)(2,1)S(1)}, bf16[512,512]{1,0:T(8,128)(2,1)S(1)}, bf16[2048,512]{1,0:T(8,128)(2,1)S(1)}, f32[512,1024]{1,0:T(8,128)...) custom-call(bf16[256,1024]{1,0:T(8,128)(2,1)S(1)} %get-tuple-element, ...), custom_call_target="tpu_custom_call" | custom-call | flops 10000000000 | bytes 30000000 | tf_op jit(solution)/shard_map/pallas_call | solution.py:525
  62.6 3.4 %shard_map.242 = (bf16[2048,512]{1,0:T(8,128)(2,1)S(1)}, bf16[512,2048]{1,0:T(8,128)(2,1)S(1)}, f32[512,1024]{1,0:T(8,128)S(1)}, bf16[512,1024]{1,0:T(8,128)(2,1...) custom-call(f32[512,1024]{1,0:T(8,128)S(1)} %get-tuple-element.109.refs_0_, ...), custom_call_target="tpu_custom_call" | custom-call | flops 10000000000 | bytes 30000000 | tf_op jit(solution)/shard_map/pallas_call | solution.py:525
  66.0 21.6 %shard_map.244 = (bf16[3,256,1024]{2,1,0:T(8,128)(2,1)S(1)}, bf16[256,1024]{1,0:T(8,128)(2,1)S(1)}, f32[4,8,1024]{2,1,0:T(8,128)S(1)}) custom-call(bf16[512,1024]{1,0:T(8,128)(2,1)S(1)} %get-tuple-element.112.refs_0_.refs_7_, bf16[768,512]{1,0:T(8,128)(2,1)S(1)} %get-tuple-element.115.refs_1_, f32[8,1024]{1,0:T(8,128)S(1)} %broadcast_in_dim.27.refs_2_.refs_4_), custom_call_target="tpu_custom_call" | custom-call | flops 10000000000 | bytes 30000000 | tf_op jit(solution)/shard_map/pallas_call | solution.py:525
  87.6 8.8 %shard_map.243 = (bf16[3,256,1024]{2,1,0:T(8,128)(2,1)S(1)}, bf16[256,1024]{1,0:T(8,128)(2,1)S(1)}, f32[4,8,1024]{2,1,0:T(8,128)S(1)}) custom-call(bf16[512,1024]{1,0:T(8,128)(2,1)S(1)} %get-tuple-element.112.refs_0_.refs_7_, bf16[768,512]{1,0:T(8,128)(2,1)S(1)} %get-tuple-element.113.refs_1_, f32[8,1024]{1,0:T(8,128)S(1)} %broadcast_in_dim.27.refs_2_.refs_4_), custom_call_target="tpu_custom_call" | custom-call | flops 10000000000 | bytes 30000000 | tf_op jit(solution)/shard_map/pallas_call | solution.py:525
  96.4 22.5 %shard_map.245 = (bf16[512,1024]{1,0:T(8,128)(2,1)S(1)}, bf16[1024,512]{1,0:T(8,128)(2,1)}, bf16[2048,1024]{1,0:T(8,128)(2,1)S(1)}, bf16[2048,1024]{1,0:T(8,128)...) custom-call(bf16[256,1024]{1,0:T(8,128)(2,1)S(1)} %get-tuple-element, ...), custom_call_target="tpu_custom_call" | custom-call | flops 10000000000 | bytes 30000000 | tf_op jit(solution)/shard_map/pallas_call | solution.py:525
  118.9 8.7 %shard_map.247.refs_3_.refs_9_ = bf16[3,256,1024]{2,1,0:T(8,128)(2,1)S(1)} custom-call(bf16[3,256,1024]{2,1,0:T(8,128)(2,1)S(1)} %get-tuple-element.128.refs_0_, bf16[512,1024]{1,0:T(8,128)(2,1)S(1)} %get-tuple-element.125.refs_1_.refs_6_, bf16[512,1024]{1,0:T(8,128)(2,1)S(1)} %get-tuple-element.126.refs_2_, f32[4,8,1024]{2,1,0:T(8,128)S(1)} %get-tuple-element.129.refs_3_, ...), custom_call_target="tpu_custom_call" | custom-call | flops 10000000000 | bytes 30000000 | tf_op jit(solution)/shard_map/pallas_call | solution.py:525
  127.6 8.8 %shard_map.246.refs_2_.refs_9_ = bf16[3,256,1024]{2,1,0:T(8,128)(2,1)S(1)} custom-call(bf16[3,256,1024]{2,1,0:T(8,128)(2,1)S(1)} %get-tuple-element.124.refs_0_, bf16[512,1024]{1,0:T(8,128)(2,1)S(1)} %get-tuple-element.125.refs_1_.refs_6_, bf16[512,1024]{1,0:T(8,128)(2,1)S(1)} %get-tuple-element.126.refs_2_, f32[4,8,1024]{2,1,0:T(8,128)S(1)} %get-tuple-element.127.refs_3_, ...), custom_call_target="tpu_custom_call" | custom-call | flops 10000000000 | bytes 30000000 | tf_op jit(solution)/shard_map/pallas_call | solution.py:525
  138.3 9.7 %shard_map.249 = (f32[512,1024]{1,0:T(8,128)S(1)}, bf16[512,1024]{1,0:T(8,128)(2,1)S(1)}, bf16[2048,1024]{1,0:T(8,128)(2,1)S(1)}, bf16[512,1024]{1,0:T(8,128)(2,...) custom-call(f32[512,1024]{1,0:T(8,128)S(1)} %shard_map.248.refs_0_, ...), custom_call_target="tpu_custom_call", output_to_operand_aliasing={{2}: (5, {}), {5}: (8, {})} | custom-call | flops 10000000000 | bytes 30000000 | tf_op jit(solution)/shard_map/pallas_call | solution.py:525
  149.3 10.4 %shard_map.250 = (bf16[256,2688]{1,0:T(8,128)(2,1)S(1)}, bf16[256,2688]{1,0:T(8,128)(2,1)}) custom-call(s32[1]{0:T(128)} %bitcast.15.refs_0_.refs_5_, bf16[2048,1024]{1,0:T(8,128)(2,1)S(1)} %get-tuple-element.110.refs_1_, bf16[2048,1024]{1,0:T(8,128)(2,1)S(1)} %get-tuple-element.141.refs_2_, bf16[512,1024]{1,0:T(8,128)(2,1)S(1)} %get-tuple-element.142.refs_3_, ...), custom_call_target="tpu_custom_call" | custom-call | flops 10000000000 | bytes 30000000 | tf_op jit(solution)/shard_map/pallas_call | solution.py:525
  160.2 2.2 copy-done.16
  162.4 2.2 copy-done.18
  167.0 7.1 %shard_map.251 = (bf16[256,2048]{1,0:T(8,128)(2,1)S(1)}, bf16[256,2048]{1,0:T(8,128)(2,1)S(1)}) custom-call(s32[1]{0:T(128)} %bitcast.15.refs_0_.refs_5_, bf16[512,1024]{1,0:T(8,128)(2,1)S(1)} %copy-done.28, bf16[512,1024]{1,0:T(8,128)(2,1)S(1)} %copy-done.22, bf16[2048,1024]{1,0:T(8,128)(2,1)S(1)} %copy-done.18, bf16[2048,1024]{1,0:T(8,128)(2,1)S(1)} %copy-done.16, ...), custom_call_target="tpu_custom_call" | custom-call | flops 10000000000 | bytes 30000000 | tf_op jit(solution)/shard_map/pallas_call | solution.py:525
  177.9 4.3 %shard_map.252.refs_8_.refs_2_ = bf16[3,128,1024]{2,1,0:T(8,128)(2,1)S(1)} custom-call(bf16[3,256,1024]{2,1,0:T(8,128)(2,1)S(1)} %copy-done.34, bf16[512,1024]{1,0:T(8,128)(2,1)S(1)} %copy-done.20, bf16[512,1024]{1,0:T(8,128)(2,1)S(1)} %copy-done.24, f32[4,8,1024]{2,1,0:T(8,128)S(1)} %get-tuple-element.140.refs_3_, ...), custom_call_target="tpu_custom_call" | custom-call | flops 15000000512 | bytes 45000000 | tf_op jit(solution)/shard_map/pallas_call | solution.py:525
  184.3 8.3 %shard_map.253 = (bf16[3,128,1024]{2,1,0:T(8,128)(2,1)S(1)}, bf16[256,768]{1,0:T(8,128)(2,1)S(1)}, bf16[256,768]{1,0:T(8,128)(2,1)S(1)}) custom-call(bf16[3,256,1024]{2,1,0:T(8,128)(2,1)S(1)} %copy-done.34, bf16[512,1024]{1,0:T(8,128)(2,1)S(1)} %copy-done.20, bf16[512,1024]{1,0:T(8,128)(2,1)S(1)} %copy-done.24, ...), custom_call_target="tpu_custom_call" | custom-call | flops 15000000512 | bytes 45000000 | tf_op jit(solution)/shard_map/pallas_call | solution.py:525
  198.8 4.3 %shard_map.254.refs_8_.refs_4_ = bf16[3,128,1024]{2,1,0:T(8,128)(2,1)S(1)} custom-call(bf16[3,256,1024]{2,1,0:T(8,128)(2,1)S(1)} %copy-done.32, bf16[512,1024]{1,0:T(8,128)(2,1)S(1)} %copy-done.20, bf16[512,1024]{1,0:T(8,128)(2,1)S(1)} %copy-done.24, f32[4,8,1024]{2,1,0:T(8,128)S(1)} %get-tuple-element.162.refs_3_, ...), custom_call_target="tpu_custom_call" | custom-call | flops 15000000512 | bytes 45000000 | tf_op jit(solution)/shard_map/pallas_call | solution.py:525
  207.9 2.6 collective-permute-start.24
  210.7 8.3 %shard_map.255 = (bf16[3,128,1024]{2,1,0:T(8,128)(2,1)S(1)}, bf16[256,768]{1,0:T(8,128)(2,1)S(1)}, bf16[256,768]{1,0:T(8,128)(2,1)S(1)}) custom-call(bf16[3,256,1024]{2,1,0:T(8,128)(2,1)S(1)} %copy-done.32, bf16[512,1024]{1,0:T(8,128)(2,1)S(1)} %copy-done.20, bf16[512,1024]{1,0:T(8,128)(2,1)S(1)} %copy-done.24, ...), custom_call_target="tpu_custom_call" | custom-call | flops 15000000512 | bytes 45000000 | tf_op jit(solution)/shard_map/pallas_call | solution.py:525
  223.0 2.3 collective-permute-start.27
  225.9 3.1 %collective-permute-done.26 = bf16[16,4736]{1,0:T(8,128)(2,1)S(1)} collective-permute-done((bf16[16,4736]{1,0:T(8,128)(2,1)S(1)}, bf16[16,4736]{1,0:T(8,128)(2,1)S(1)}, u32[]{:S(2)}, u32[]{:S(2)}) %collective-permute-start.26) | collective-permute-done | bytes 151584 | tf_op jit(solution)/shard_map/ppermute | solution.py:541
  229.1 8.2 %collective-permute-done.27 = bf16[16,4736]{1,0:T(8,128)(2,1)S(1)} collective-permute-done((bf16[16,4736]{1,0:T(8,128)(2,1)S(1)}, bf16[16,4736]{1,0:T(8,128)(2,1)S(1)}, u32[]{:S(2)}, u32[]{:S(2)}) %collective-permute-start.27) | collective-permute-done | bytes 151584 | tf_op jit(solution)/shard_map/ppermute | solution.py:541
  239.7 5.6 %collective-permute-done.16 = bf16[2,2,16,1536]{3,2,1,0:T(8,128)(2,1)S(1)} collective-permute-done((bf16[2,2,16,1536]{3,2,1,0:T(8,128)(2,1)S(1)}, bf16[2,2,16,1536]{3,2,1,0:T(8,128)(2,1)S(1)}, u32[]{:S(2)}, u32[]{:S(2)}) %collective-permute-start.16) | collective-permute-done | bytes 196640 | tf_op jit(solution)/shard_map/ppermute | solution.py:541
  245.4 2.4 collective-permute-start.17
  250.2 4.0 %collective-permute-done.29 = bf16[2,2,1,16,4736]{4,3,2,1,0:T(8,128)(2,1)S(1)} collective-permute-done((bf16[2,2,1,16,4736]{4,3,2,1,0:T(8,128)(2,1)S(1)}, bf16[2,2,1,16,4736]{4,3,2,1,0:T(8,128)(2,1)S(1)}, u32[]{:S(2)}, u32[]{:S(2)}) %collective-permute-start.29) | collective-permute-done | bytes 606240 | tf_op jit(solution)/shard_map/ppermute | solution.py:541
  254.8 3.7 %collective-permute-start.20 = (bf16[16,1536]{1,0:T(8,128)(2,1)S(1)}, bf16[16,1536]{1,0:T(8,128)(2,1)S(1)}, u32[]{:S(2)}, u32[]{:S(2)}) collective-permute-start(bf16[16,1536]{1,0:T(8,128)(2,1)S(1)} %fusion.12), channel_id=1, source_target_pairs={{0,8},{2,10},{4,12},{6,14},{8,0},{10,2},{12,4},{14,6},{16,24},{18,... | collective-permute-start | bytes 147464 | tf_op jit(solution)/shard_map/ppermute | solution.py:541
  261.1 4.6 %collective-permute-done.21 = bf16[16,1536]{1,0:T(8,128)(2,1)S(1)} collective-permute-done((bf16[16,1536]{1,0:T(8,128)(2,1)S(1)}, bf16[16,1536]{1,0:T(8,128)(2,1)S(1)}, u32[]{:S(2)}, u32[]{:S(2)}) %collective-permute-start.21) | collective-permute-done | bytes 49184 | tf_op jit(solution)/shard_map/ppermute | solution.py:541
  269.9 3.3 %shard_map.256 = f32[1024,512]{1,0:T(8,128)} custom-call(bf16[512,1536]{1,0:T(8,128)(2,1)S(1)} %bitcast.110, f32[512,1024]{1,0:T(8,128)S(1)} %copy-done.14, bf16[3,128,1024]{2,1,0:T(8,128)(2,1)S(1)} %shard_map.252.refs_8_.refs_2_, bf16[3,128,1024]{2,1,0:T(8,128)(2,1)S(1)} %get-tuple-element.160.refs_3_, ...), custom_call_target="tpu_custom_call" | custom-call | flops 5000000000 | bytes 15000000 | tf_op jit(solution)/shard_map/pallas_call | solution.py:525
  (214 shorter events, 65.5 us)
Async XLA Ops:
  4.4 12.4 %collective-permute-start = (bf16[1,128,1536]{2,1,0:T(8,128)(2,1)}, bf16[1,128,1536]{2,1,0:T(8,128)(2,1)}, u32[]{:S(2)}, u32[]{:S(2)}) collective-permute-start(bf16[1,128,1536]{2,1,0:T(8,128)(2,1)} %pad_maximum_fusion.3), channel_id=1, source_target_pairs={{0,1},{1,0},{2,3},{3,2},{4,5},{5,4},{6,7},{7,6},{8,9},{9,8},{10,11... | collective-permute-start | bytes 1179656 | tf_op jit(solution)/shard_map/ppermute | solution.py:541
  18.0 2.4 collective-permute-start.1
  18.6 17.9 %collective-permute-start.2 = (bf16[1,128,2688]{2,1,0:T(8,128)(2,1)S(1)}, bf16[1,128,2688]{2,1,0:T(8,128)(2,1)S(1)}, u32[]{:S(2)}, u32[]{:S(2)}) collective-permute-start(bf16[1,128,2688]{2,1,0:T(8,128)(2,1)S(1)} %pad_maximum_fusion), channel_id=1, source_target_pairs={{0,1},{1,0},{2,3},{3,2},{4,5},{5,4},{6,7},{7,6},{8,9},{9,8},{10,11... | collective-permute-start | bytes 2064392 | tf_op jit(solution)/shard_map/ppermute | solution.py:541
  36.8 14.8 %collective-permute-start.3 = (bf16[2,128,2688]{2,1,0:T(8,128)(2,1)S(1)}, bf16[2,128,2688]{2,1,0:T(8,128)(2,1)S(1)}, u32[]{:S(2)}, u32[]{:S(2)}) collective-permute-start(bf16[2,128,2688]{2,1,0:T(8,128)(2,1)S(1)} %maximum_select_fusion.3), channel_id=1, source_target_pairs={{0,2},{2,0},{4,6},{6,4},{8,10},{10,8},{12,14},{14,12},{16,18},{18,... | collective-permute-start | bytes 4128776 | tf_op jit(solution)/shard_map/ppermute | solution.py:541
  36.9 14.4 %collective-permute-start.4 = (bf16[1,128,2048]{2,1,0:T(8,128)(2,1)S(1)}, bf16[1,128,2048]{2,1,0:T(8,128)(2,1)S(1)}, u32[]{:S(2)}, u32[]{:S(2)}) collective-permute-start(bf16[1,128,2048]{2,1,0:T(8,128)(2,1)S(1)} %pad_maximum_fusion.2), channel_id=1, source_target_pairs={{0,1},{1,0},{2,3},{3,2},{4,5},{5,4},{6,7},{7,6},{8,9},{9,8},{10,11... | collective-permute-start | bytes 1572872 | tf_op jit(solution)/shard_map/ppermute | solution.py:541
  51.5 10.1 %collective-permute-start.5 = (bf16[2,128,2048]{2,1,0:T(8,128)(2,1)S(1)}, bf16[2,128,2048]{2,1,0:T(8,128)(2,1)S(1)}, u32[]{:S(2)}, u32[]{:S(2)}) collective-permute-start(bf16[2,128,2048]{2,1,0:T(8,128)(2,1)S(1)} %maximum_select_fusion.5), channel_id=1, source_target_pairs={{0,2},{2,0},{4,6},{6,4},{8,10},{10,8},{12,14},{14,12},{16,18},{18,... | collective-permute-start | bytes 3145736 | tf_op jit(solution)/shard_map/ppermute | solution.py:541
  159.7 14.4 %collective-permute-start.6 = (bf16[256,2688]{1,0:T(8,128)(2,1)}, bf16[256,2688]{1,0:T(8,128)(2,1)}, u32[]{:S(2)}, u32[]{:S(2)}) collective-permute-start(bf16[256,2688]{1,0:T(8,128)(2,1)} %get-tuple-element.152.refs_5_), channel_id=1, source_target_pairs={{0,2},{2,0},{4,6},{6,4},{8,10},{10,8},{12,14},{14,12},{16,18},{18,... | collective-permute-start | bytes 4128776 | tf_op jit(solution)/shard_map/ppermute | solution.py:541
  176.1 17.5 %collective-permute-start.9 = (bf16[2,2,2,16,2688]{4,3,2,1,0:T(8,128)(2,1)S(1)}, bf16[2,2,2,16,2688]{4,3,2,1,0:T(8,128)(2,1)S(1)}, u32[]{:S(2)}, u32[]{:S(2)}) collective-permute-start(bf16[2,2,2,16,2688]{4,3,2,1,0:T(8,128)(2,1)S(1)} %get-tuple-element.183), channel_id=1, source_target_pairs={{0,1},{1,0},{2,3},{3,2},{4,5},{5,4},{6,7},{7,6},{8,9},{9,8},{10,11... | collective-permute-start | bytes 2064392 | tf_op jit(solution)/shard_map/ppermute | solution.py:541
  177.9 4.3 %collective-permute-start.7 = (bf16[256,2048]{1,0:T(8,128)(2,1)S(1)}, bf16[256,2048]{1,0:T(8,128)(2,1)S(1)}, u32[]{:S(2)}, u32[]{:S(2)}) collective-permute-start(bf16[256,2048]{1,0:T(8,128)(2,1)S(1)} %get-tuple-element.158), channel_id=1, source_target_pairs={{0,2},{2,0},{4,6},{6,4},{8,10},{10,8},{12,14},{14,12},{16,18},{18,... | collective-permute-start | bytes 3145736 | tf_op jit(solution)/shard_map/ppermute | solution.py:541
  182.7 14.8 %collective-permute-start.8 = (bf16[2,2,2,16,2048]{4,3,2,1,0:T(8,128)(2,1)S(1)}, bf16[2,2,2,16,2048]{4,3,2,1,0:T(8,128)(2,1)S(1)}, u32[]{:S(2)}, u32[]{:S(2)}) collective-permute-start(bf16[2,2,2,16,2048]{4,3,2,1,0:T(8,128)(2,1)S(1)} %get-tuple-element.195), channel_id=1, source_target_pairs={{0,4},{2,6},{4,0},{6,2},{8,12},{10,14},{12,8},{14,10},{16,20},{18,... | collective-permute-start | bytes 1572872 | tf_op jit(solution)/shard_map/ppermute | solution.py:541
  192.6 10.5 %collective-permute-start.12 = (bf16[256,768]{1,0:T(8,128)(2,1)S(1)}, bf16[256,768]{1,0:T(8,128)(2,1)S(1)}, u32[]{:S(2)}, u32[]{:S(2)}) collective-permute-start(bf16[256,768]{1,0:T(8,128)(2,1)S(1)} %get-tuple-element.165), channel_id=1, source_target_pairs={{0,2},{2,0},{4,6},{6,4},{8,10},{10,8},{12,14},{14,12},{16,18},{18,... | collective-permute-start | bytes 1179656 | tf_op jit(solution)/shard_map/ppermute | solution.py:541
  193.8 10.7 %collective-permute-start.10 = (bf16[2,2,16,2688]{3,2,1,0:T(8,128)(2,1)S(1)}, bf16[2,2,16,2688]{3,2,1,0:T(8,128)(2,1)S(1)}, u32[]{:S(2)}, u32[]{:S(2)}) collective-permute-start(bf16[2,2,16,2688]{3,2,1,0:T(8,128)(2,1)S(1)} %get-tuple-element.201), channel_id=1, source_target_pairs={{0,4},{2,6},{4,0},{6,2},{8,12},{10,14},{12,8},{14,10},{16,20},{18,... | collective-permute-start | bytes 1032200 | tf_op jit(solution)/shard_map/ppermute | solution.py:541
  197.7 8.4 %collective-permute-start.11 = (bf16[2,2,16,2048]{3,2,1,0:T(8,128)(2,1)S(1)}, bf16[2,2,16,2048]{3,2,1,0:T(8,128)(2,1)S(1)}, u32[]{:S(2)}, u32[]{:S(2)}) collective-permute-start(bf16[2,2,16,2048]{3,2,1,0:T(8,128)(2,1)S(1)} %get-tuple-element.207), channel_id=1, source_target_pairs={{0,1},{1,0},{2,3},{3,2},{4,5},{5,4},{6,7},{7,6},{8,9},{9,8},{10,11... | collective-permute-start | bytes 786440 | tf_op jit(solution)/shard_map/ppermute | solution.py:541
  203.3 22.6 %collective-permute-start.14 = (bf16[2,2,2,16,768]{4,3,1,0,2:T(8,128)(2,1)S(1)}, bf16[2,2,2,16,768]{4,3,1,0,2:T(8,128)(2,1)S(1)}, u32[]{:S(2)}, u32[]{:S(2)}) collective-permute-start(bf16[2,2,2,16,768]{4,3,1,0,2:T(8,128)(2,1)S(1)} %bitcast.129), channel_id=1, source_target_pairs={{0,1},{1,0},{2,3},{3,2},{4,5},{5,4},{6,7},{7,6},{8,9},{9,8},{10,11... | collective-permute-start | bytes 589832 | tf_op jit(solution)/shard_map/ppermute | solution.py:541
  206.2 12.9 %collective-permute-start.23 = (bf16[16,4736]{1,0:T(8,128)(2,1)S(1)}, bf16[16,4736]{1,0:T(8,128)(2,1)S(1)}, u32[]{:S(2)}, u32[]{:S(2)}) collective-permute-start(bf16[16,4736]{1,0:T(8,128)(2,1)S(1)} %get-tuple-element.202), channel_id=1, source_target_pairs={{0,8},{2,10},{4,12},{6,14},{8,0},{10,2},{12,4},{14,6},{16,24},{18,... | collective-permute-start | bytes 454664 | tf_op jit(solution)/shard_map/ppermute | solution.py:541
  207.9 12.6 %collective-permute-start.24 = (bf16[16,4736]{1,0:T(8,128)(2,1)S(1)}, bf16[16,4736]{1,0:T(8,128)(2,1)S(1)}, u32[]{:S(2)}, u32[]{:S(2)}) collective-permute-start(bf16[16,4736]{1,0:T(8,128)(2,1)S(1)} %get-tuple-element.204), channel_id=1, source_target_pairs={{0,16},{2,18},{4,20},{6,22},{8,24},{10,26},{12,28},{14,30},{16,0},... | collective-permute-start | bytes 454664 | tf_op jit(solution)/shard_map/ppermute | solution.py:541
  210.5 10.0 %collective-permute-start.25 = (bf16[16,4736]{1,0:T(8,128)(2,1)S(1)}, bf16[16,4736]{1,0:T(8,128)(2,1)S(1)}, u32[]{:S(2)}, u32[]{:S(2)}) collective-permute-start(bf16[16,4736]{1,0:T(8,128)(2,1)S(1)} %get-tuple-element.203), channel_id=1, source_target_pairs={{0,24},{2,26},{4,28},{6,30},{8,16},{10,18},{12,20},{14,22},{16,8},... | collective-permute-start | bytes 454664 | tf_op jit(solution)/shard_map/ppermute | solution.py:541
  219.0 1.8 collective-permute-start.13
  221.0 8.0 %collective-permute-start.26 = (bf16[16,4736]{1,0:T(8,128)(2,1)S(1)}, bf16[16,4736]{1,0:T(8,128)(2,1)S(1)}, u32[]{:S(2)}, u32[]{:S(2)}) collective-permute-start(bf16[16,4736]{1,0:T(8,128)(2,1)S(1)} %add_convert_fusion.9), channel_id=1, source_target_pairs={{0,8},{2,10},{4,12},{6,14},{8,0},{10,2},{12,4},{14,6},{16,24},{18,... | collective-permute-start | bytes 454664 | tf_op jit(solution)/shard_map/ppermute | solution.py:541
  223.0 14.3 %collective-permute-start.27 = (bf16[16,4736]{1,0:T(8,128)(2,1)S(1)}, bf16[16,4736]{1,0:T(8,128)(2,1)S(1)}, u32[]{:S(2)}, u32[]{:S(2)}) collective-permute-start(bf16[16,4736]{1,0:T(8,128)(2,1)S(1)} %add_convert_fusion.9), channel_id=1, source_target_pairs={{0,16},{2,18},{4,20},{6,22},{8,24},{10,26},{12,28},{14,30},{16,0},... | collective-permute-start | bytes 454664 | tf_op jit(solution)/shard_map/ppermute | solution.py:541
  225.2 12.0 %collective-permute-start.28 = (bf16[16,4736]{1,0:T(8,128)(2,1)S(1)}, bf16[16,4736]{1,0:T(8,128)(2,1)S(1)}, u32[]{:S(2)}, u32[]{:S(2)}) collective-permute-start(bf16[16,4736]{1,0:T(8,128)(2,1)S(1)} %add_convert_fusion.9), channel_id=1, source_target_pairs={{0,24},{2,26},{4,28},{6,30},{8,16},{10,18},{12,20},{14,22},{16,8},... | collective-permute-start | bytes 454664 | tf_op jit(solution)/shard_map/ppermute | solution.py:541
  225.5 11.8 %collective-permute-start.15 = (bf16[2,2,2,16,768]{4,3,1,0,2:T(8,128)(2,1)S(1)}, bf16[2,2,2,16,768]{4,3,1,0,2:T(8,128)(2,1)S(1)}, u32[]{:S(2)}, u32[]{:S(2)}) collective-permute-start(bf16[2,2,2,16,768]{4,3,1,0,2:T(8,128)(2,1)S(1)} %bitcast.130), channel_id=1, source_target_pairs={{0,1},{1,0},{2,3},{3,2},{4,5},{5,4},{6,7},{7,6},{8,9},{9,8},{10,11... | collective-permute-start | bytes 589832 | tf_op jit(solution)/shard_map/ppermute | solution.py:541
  237.4 7.9 %collective-permute-start.16 = (bf16[2,2,16,1536]{3,2,1,0:T(8,128)(2,1)S(1)}, bf16[2,2,16,1536]{3,2,1,0:T(8,128)(2,1)S(1)}, u32[]{:S(2)}, u32[]{:S(2)}) collective-permute-start(bf16[2,2,16,1536]{3,2,1,0:T(8,128)(2,1)S(1)} %fusion.9.refs_6_), channel_id=1, source_target_pairs={{0,4},{2,6},{4,0},{6,2},{8,12},{10,14},{12,8},{14,10},{16,20},{18,... | collective-permute-start | bytes 589832 | tf_op jit(solution)/shard_map/ppermute | solution.py:541
  239.1 15.0 %collective-permute-start.29 = (bf16[2,2,1,16,4736]{4,3,2,1,0:T(8,128)(2,1)S(1)}, bf16[2,2,1,16,4736]{4,3,2,1,0:T(8,128)(2,1)S(1)}, u32[]{:S(2)}, u32[]{:S(2)}) collective-permute-start(bf16[2,2,1,16,4736]{4,3,2,1,0:T(8,128)(2,1)S(1)} %maximum_select_fusion.8), channel_id=1, source_target_pairs={{0,4},{2,6},{4,0},{6,2},{8,12},{10,14},{12,8},{14,10},{16,20},{18,... | collective-permute-start | bytes 1818632 | tf_op jit(solution)/shard_map/ppermute | solution.py:541
  245.4 9.0 %collective-permute-start.17 = (bf16[16,1536]{1,0:T(8,128)(2,1)S(1)}, bf16[16,1536]{1,0:T(8,128)(2,1)S(1)}, u32[]{:S(2)}, u32[]{:S(2)}) collective-permute-start(bf16[16,1536]{1,0:T(8,128)(2,1)S(1)} %get-tuple-element.224), channel_id=1, source_target_pairs={{0,8},{2,10},{4,12},{6,14},{8,0},{10,2},{12,4},{14,6},{16,24},{18,... | collective-permute-start | bytes 147464 | tf_op jit(solution)/shard_map/ppermute | solution.py:541
  247.8 6.7 %collective-permute-start.18 = (bf16[16,1536]{1,0:T(8,128)(2,1)S(1)}, bf16[16,1536]{1,0:T(8,128)(2,1)S(1)}, u32[]{:S(2)}, u32[]{:S(2)}) collective-permute-start(bf16[16,1536]{1,0:T(8,128)(2,1)S(1)} %get-tuple-element.226), channel_id=1, source_target_pairs={{0,16},{2,18},{4,20},{6,22},{8,24},{10,26},{12,28},{14,30},{16,0},... | collective-permute-start | bytes 147464 | tf_op jit(solution)/shard_map/ppermute | solution.py:541
  248.8 6.0 %collective-permute-start.19 = (bf16[16,1536]{1,0:T(8,128)(2,1)S(1)}, bf16[16,1536]{1,0:T(8,128)(2,1)S(1)}, u32[]{:S(2)}, u32[]{:S(2)}) collective-permute-start(bf16[16,1536]{1,0:T(8,128)(2,1)S(1)} %get-tuple-element.225), channel_id=1, source_target_pairs={{0,24},{2,26},{4,28},{6,30},{8,16},{10,18},{12,20},{14,22},{16,8},... | collective-permute-start | bytes 147464 | tf_op jit(solution)/shard_map/ppermute | solution.py:541
  254.3 11.6 %collective-permute-start.30 = (bf16[128,4736]{1,0:T(8,128)(2,1)S(1)}, bf16[128,4736]{1,0:T(8,128)(2,1)S(1)}, u32[]{:S(2)}, u32[]{:S(2)}) collective-permute-start(bf16[128,4736]{1,0:T(8,128)(2,1)S(1)} %bitcast.115), channel_id=1, source_target_pairs={{0,2},{2,0},{4,6},{6,4},{8,10},{10,8},{12,14},{14,12},{16,18},{18,... | collective-permute-start | bytes 3637256 | tf_op jit(solution)/shard_map/ppermute | solution.py:541
  254.8 6.3 %collective-permute-start.20 = (bf16[16,1536]{1,0:T(8,128)(2,1)S(1)}, bf16[16,1536]{1,0:T(8,128)(2,1)S(1)}, u32[]{:S(2)}, u32[]{:S(2)}) collective-permute-start(bf16[16,1536]{1,0:T(8,128)(2,1)S(1)} %fusion.12), channel_id=1, source_target_pairs={{0,8},{2,10},{4,12},{6,14},{8,0},{10,2},{12,4},{14,6},{16,24},{18,... | collective-permute-start | bytes 147464 | tf_op jit(solution)/shard_map/ppermute | solution.py:541
  258.5 7.2 %collective-permute-start.21 = (bf16[16,1536]{1,0:T(8,128)(2,1)S(1)}, bf16[16,1536]{1,0:T(8,128)(2,1)S(1)}, u32[]{:S(2)}, u32[]{:S(2)}) collective-permute-start(bf16[16,1536]{1,0:T(8,128)(2,1)S(1)} %fusion.12), channel_id=1, source_target_pairs={{0,16},{2,18},{4,20},{6,22},{8,24},{10,26},{12,28},{14,30},{16,0},... | collective-permute-start | bytes 147464 | tf_op jit(solution)/shard_map/ppermute | solution.py:541
  259.7 6.0 %collective-permute-start.22 = (bf16[16,1536]{1,0:T(8,128)(2,1)S(1)}, bf16[16,1536]{1,0:T(8,128)(2,1)S(1)}, u32[]{:S(2)}, u32[]{:S(2)}) collective-permute-start(bf16[16,1536]{1,0:T(8,128)(2,1)S(1)} %fusion.12), channel_id=1, source_target_pairs={{0,24},{2,26},{4,28},{6,30},{8,16},{10,18},{12,20},{14,22},{16,8},... | collective-permute-start | bytes 147464 | tf_op jit(solution)/shard_map/ppermute | solution.py:541
  268.4 5.8 %collective-permute-start.31 = (bf16[2,2,1,16,1536]{4,3,1,0,2:T(8,128)(2,1)S(1)}, bf16[2,2,1,16,1536]{4,3,1,0,2:T(8,128)(2,1)S(1)}, u32[]{:S(2)}, u32[]{:S(2)}) collective-permute-start(bf16[2,2,1,16,1536]{4,3,1,0,2:T(8,128)(2,1)S(1)} %bitcast.112), channel_id=1, source_target_pairs={{0,4},{2,6},{4,0},{6,2},{8,12},{10,14},{12,8},{14,10},{16,20},{18,... | collective-permute-start | bytes 589832 | tf_op jit(solution)/shard_map/ppermute | solution.py:541
  (37 other events, 287.5 us)

commit v3 on v2

--- a/solution.py
+++ b/solution.py
@@ -376,29 +376,39 @@
             send_ref[rows, cols] = part
 
 
+def partial_kernel(
+    z_ref, dfr_ref, du_ref, yr_ref, o_ref, dar_ref, outer_ref, inner_ref, output_ref
+):
+    for first in range(0, z_ref.shape[0], CHUNK):
+        part = slice(first, first + CHUNK)
+        outer_ref[part, :] = nt(z_ref[part, :], dfr_ref[...]).astype(bf16)
+        inner_ref[part, :] = nt(du_ref[part, :], yr_ref[...]).astype(bf16)
+    for first in range(0, o_ref.shape[0], CHUNK):
+        part = slice(first, first + CHUNK)
+        output_ref[part, :] = nt(o_ref[part, :], dar_ref[...]).astype(bf16)
+
+
 def outer_grad_kernel(
     shards,
     core_ref,
-    z1_ref,
-    z2_ref,
-    dfr1_ref,
-    dfr2_ref,
-    o1_ref,
-    o2_ref,
-    dar1_ref,
-    dar2_ref,
+    z_ref,
+    dfr_ref,
+    more_ref,
+    o_ref,
+    dar_ref,
+    more_o_ref,
     acc_ref,
     keep_ref,
     send_ref,
 ):
     core = core_ref[0]
-    hidden, width = z1_ref.shape[0], dfr1_ref.shape[0]
+    hidden, width = z_ref.shape[0], dfr_ref.shape[0]
     unit = width // shards // 2
     groups = hidden // width
     per_group = hidden // shards // groups
     for first in range(0, hidden, 256):
         part = slice(first, first + 256)
-        dwu = nt(z1_ref[part, :], dfr1_ref[...]) + nt(z2_ref[part, :], dfr2_ref[...])
+        dwu = nt(z_ref[part, :], dfr_ref[...]) + more_ref[part, :].astype(f32)
         dwu = dwu.astype(bf16)
         for at in range(0, 256, per_group):
             block = (first + at) // per_group
@@ -408,9 +418,8 @@
             place(rows, shard * per_group, unit, core, keep_ref, send_ref, cols)
     for first in range(0, width, CHUNK):
         part = slice(first, first + CHUNK)
-        cols = slice(hidden + first, hidden + first + CHUNK)
-        dwo = nt(o1_ref[...], dar1_ref[part, :]) + nt(o2_ref[...], dar2_ref[part, :])
-        place(dwo.astype(bf16), 0, unit, core, keep_ref, send_ref, cols)
+        dwo = nt(o_ref[part, :], dar_ref[...]) + more_o_ref[part, :].astype(f32)
+        place(dwo.astype(bf16), first, unit, core, keep_ref, send_ref, slice(hidden, hidden + width))
     lane = lax.broadcasted_iota(jnp.int32, (width, 128), 1)
     dpar = jnp.zeros((width, 128), f32)
     for i in range(4):
@@ -419,19 +428,19 @@
     place(dpar.astype(bf16), 0, unit, core, keep_ref, send_ref, last)
 
 
-def inner_grad_kernel(
-    shards, core_ref, yr1_ref, yr2_ref, du1_ref, du2_ref, keep_ref, send_ref
-):
+def inner_grad_kernel(shards, core_ref, yr_ref, du_ref, more_ref, keep_ref, send_ref):
     core = core_ref[0]
-    width, hidden = yr1_ref.shape[0], du1_ref.shape[0]
+    width, hidden = yr_ref.shape[0], du_ref.shape[0]
     unit = width // shards // 2
     for first in range(0, hidden, CHUNK):
         part = slice(first, first + CHUNK)
-        dwi_t = nt(du1_ref[part, :], yr1_ref[...]) + nt(du2_ref[part, :], yr2_ref[...])
+        dwi_t = nt(du_ref[part, :], yr_ref[...]) + more_ref[part, :].astype(f32)
         place(dwi_t.astype(bf16).T, 0, unit, core, keep_ref, send_ref, part)
 
 
-def attend_back_kernel(first, size, qkv_ref, o_ref, do_ref, lse_ref, seg_ref, dqkv_ref, *refs):
+def attend_back_kernel(
+    first, size, qkv_ref, o_ref, do_ref, lse_ref, seg_ref, x_ref, dqkv_ref, more_ref, *refs
+):
     bias_ref, prob_ref, ds_ref = refs
     rows = dqkv_ref.shape[1]
     fill_bias(seg_ref, bias_ref)
@@ -456,6 +465,8 @@
         return carry
 
     lax.fori_loop(0, rows // size // 2, two_heads, 0)
+    for i in range(3):
+        more_ref[:, i * rows : (i + 1) * rows] = nt(x_ref[...], dqkv_ref[i]).astype(bf16)
 
 
 def attend_part_kernel(
@@ -463,8 +474,8 @@
 ):
     grads = p % 2 == 1
     if grads:
-        core_ref, x1_ref, x2_ref, before_ref, second_ref = refs[:5]
-        dqkv_ref, keep_ref, send_ref, bias_ref, prob_ref, ds_ref = refs[5:]
+        core_ref, x1_ref, before_ref, more_ref = refs[:4]
+        dqkv_ref, keep_ref, send_ref, bias_ref, prob_ref, ds_ref = refs[4:]
     else:
         dqkv_ref, bias_ref, prob_ref, ds_ref = refs
     fill_bias(seg_ref, bias_ref)
@@ -490,8 +501,9 @@
     unit = x1_ref.shape[0] // shards // 2
     for i in range(3):
         joined = jnp.concatenate([before_ref[i], dqkv_ref[i]], axis=0)
-        dw = nt(x1_ref[...], joined) + nt(x2_ref[...], second_ref[i])
-        place(dw.astype(bf16), 0, unit, core, keep_ref, send_ref, slice(i * rows, (i + 1) * rows))
+        cols = slice(i * rows, (i + 1) * rows)
+        dw = nt(x1_ref[...], joined) + more_ref[:, cols].astype(f32)
+        place(dw.astype(bf16), 0, unit, core, keep_ref, send_ref, cols)
 
 
 def input_kernel(turned, w_ref, dh_ref, *refs):
@@ -762,10 +774,21 @@
         limit=10,
     )
     back = [bias, pair, pair]
-    dqkv2 = []
+    more_u, more_i, more_o = call(
+        partial_kernel,
+        [((hidden, width), bf16)] * 2 + [((width, width), bf16)],
+        [],
+        (z2, dfr2, du2, yr2, o2, dar2),
+        limit=4,
+    )
+    dqkv2, more = [], []
+    more_qkv = shapes[:1] + [((width, 3 * rows), bf16)]
     for group, (qkv, lse) in enumerate(((qkv2a, lse2a), (qkv2b, lse2b))):
         kernel = functools.partial(attend_back_kernel, group * rows, size)
-        dqkv2 += call(kernel, shapes[:1], back, (qkv, o2, do2, lse, seg_rows), limit=10)
+        args = (qkv, o2, do2, lse, seg_rows, x2)
+        found = call(kernel, more_qkv, back, args, limit=10, deps=(more_u,))
+        dqkv2.append(found[0])
+        more.append(found[1])
     joined = [((3 * width, length), bf16)]
     (grad1,) = call(
         functools.partial(input_kernel, False), [tall32], joined, (wqkv, dh2, *dqkv2), None, 3, 4
@@ -781,8 +804,8 @@
         functools.partial(outer_grad_kernel, shards),
         [((half, hidden + width + 128), bf16)] * 2,
         [],
-        (core, z1, z2, dfr1, dfr2, o1, o2, dar1, dar2, acc),
-        [SM] + [VM] * 9,
+        (core, z1, dfr1, more_u, o1, dar1, more_o, acc),
+        [SM] + [VM] * 7,
         limit=4,
     )
     outer = Sum(keep_u, send_u)
@@ -790,8 +813,8 @@
         functools.partial(inner_grad_kernel, shards),
         [((half, hidden), bf16)] * 2,
         [],
-        (core, yr1, yr2, du1, du2),
-        [SM] + [VM] * 4,
+        (core, yr1, du1, more_i),
+        [SM] + [VM] * 3,
         limit=4,
         deps=(send_u,),
     )
@@ -803,8 +826,8 @@
         specs = [VM] * 5
         outs = [((3, 2 * size, length), bf16)]
         if p % 2:
-            args += (core, x1, x2, parts[-1], dqkv2[p // 2])
-            specs += [SM] + [VM] * 4
+            args += (core, x1, parts[-1], more[p // 2])
+            specs += [SM] + [VM] * 3
             outs += [((half, 3 * rows), bf16)] * 2
         kernel = functools.partial(attend_part_kernel, p, size, shards)
         results = call(kernel, outs, back, args, specs, 15, 10)

time: 281 us -> 279 us (level)
    pallas_call x20 -> x21, Pallas kernels: 157 us -> 155 us  [call(): pl.pallas_call(run, out_shape=[jax.ShapeDtypeStruct(shape, dtype) for sha...]
    unnamed x74 -> x72, local copies, waits for them, and re-layouts: 13 us -> 12.2 us
  transfers between devices with their start and end apart: 33 -> 33, of which waited for: 17 -> 17; matrix products, arithmetic and copies ran while one was open for 3% -> 4% of each run, Pallas kernels for 22% -> 20%
where the time goes in v3:
time: 279 us; the launch traced here: 277 us
  Pallas kernels  155 us (56%)
  waiting for transfers between devices  46.7 us (17%)
  starting transfers between devices  38.8 us (14%)
  local copies, waits for them, and re-layouts  20.6 us (7%)
  other arithmetic  13.2 us (5%)
  between operations  3.22 us (1%)
    pallas_call x21, Pallas kernels, call(): pl.pallas_call(run, out_shape=[jax.ShapeDtypeStruct(shape, dtype) for sha...  155 us
    ppermute x33, waiting for transfers between devices, flip(): return lax.ppermute(value, axis, [(i, i ^ bit) for i in range(count)])  46.7 us
    ppermute x33, starting transfers between devices, flip(): return lax.ppermute(value, axis, [(i, i ^ bit) for i in range(count)])  38.8 us
    unnamed x72, local copies, waits for them, and re-layouts  12.2 us
  transfers between devices with their start and end apart: 33, of which 17 were waited for; matrix products, arithmetic and copies ran while one was open for 4% of the time, Pallas kernels for 20%

profile of v3, /device:TPU:0, one launch (start us, length us, event | category | flops | bytes accessed | tf_op | source)
XLA Modules:
  0.0 277.2 jit_solution(11389932243918160311)
XLA Ops:
  4.4 2.9 %collective-permute-start = (bf16[1,128,1536]{2,1,0:T(8,128)(2,1)}, bf16[1,128,1536]{2,1,0:T(8,128)(2,1)}, u32[]{:S(2)}, u32[]{:S(2)}) collective-permute-start(bf16[1,128,1536]{2,1,0:T(8,128)(2,1)} %pad_maximum_fusion.3), channel_id=1, source_target_pairs={{0,1},{1,0},{2,3},{3,2},{4,5},{5,4},{6,7},{7,6},{8,9},{9,8},{10,11... | collective-permute-start | bytes 1179656 | tf_op jit(solution)/shard_map/ppermute | solution.py:553
  13.2 3.5 %collective-permute-done = bf16[1,128,1536]{2,1,0:T(8,128)(2,1)} collective-permute-done((bf16[1,128,1536]{2,1,0:T(8,128)(2,1)}, bf16[1,128,1536]{2,1,0:T(8,128)(2,1)}, u32[]{:S(2)}, u32[]{:S(2)}) %collective-permute-start) | collective-permute-done | bytes 393248 | tf_op jit(solution)/shard_map/ppermute | solution.py:553
  21.1 8.7 %shard_map.239 = (bf16[768,512]{1,0:T(8,128)(2,1)S(1)}, bf16[3,256,1024]{2,1,0:T(8,128)(2,1)S(1)}, bf16[256,1024]{1,0:T(8,128)(2,1)S(1)}, f32[4,8,1024]{2,1,0:T(8,128)S(1)}) custom-call(bf16[512,1024]{1,0:T(8,128)(2,1)S(1)} %shard_map.238.refs_0_.refs_2_.refs_6_, bf16[512,1536]{1,0:T(8,128)(2,1)S(1)} %bitcast.107, f32[8,1024]{1,0:T(8,128)S(1)} %broadcast_in_dim.27.refs_2_.refs_4_), custom_call_target="tpu_custom_call" | custom-call | flops 10000000000 | bytes 30000000 | tf_op jit(solution)/shard_map/pallas_call | solution.py:537
  31.0 5.5 %collective-permute-done.2 = bf16[1,128,2688]{2,1,0:T(8,128)(2,1)S(1)} collective-permute-done((bf16[1,128,2688]{2,1,0:T(8,128)(2,1)S(1)}, bf16[1,128,2688]{2,1,0:T(8,128)(2,1)S(1)}, u32[]{:S(2)}, u32[]{:S(2)}) %collective-permute-start.2) | collective-permute-done | bytes 688160 | tf_op jit(solution)/shard_map/ppermute | solution.py:553
  38.7 8.7 %shard_map.240 = (bf16[768,512]{1,0:T(8,128)(2,1)S(1)}, bf16[3,256,1024]{2,1,0:T(8,128)(2,1)S(1)}, bf16[256,1024]{1,0:T(8,128)(2,1)S(1)}, f32[4,8,1024]{2,1,0:T(8,128)S(1)}) custom-call(bf16[512,1024]{1,0:T(8,128)(2,1)S(1)} %shard_map.238.refs_0_.refs_2_.refs_6_, bf16[512,1536]{1,0:T(8,128)(2,1)S(1)} %bitcast.108, f32[8,1024]{1,0:T(8,128)S(1)} %broadcast_in_dim.27.refs_2_.refs_4_), custom_call_target="tpu_custom_call" | custom-call | flops 10000000000 | bytes 30000000 | tf_op jit(solution)/shard_map/pallas_call | solution.py:537
  48.6 2.7 collective-permute-done.4
  52.6 8.0 %shard_map.241 = (bf16[512,1024]{1,0:T(8,128)(2,1)S(1)}, bf16[512,512]{1,0:T(8,128)(2,1)S(1)}, bf16[2048,512]{1,0:T(8,128)(2,1)S(1)}, f32[512,1024]{1,0:T(8,128)...) custom-call(bf16[256,1024]{1,0:T(8,128)(2,1)S(1)} %get-tuple-element, ...), custom_call_target="tpu_custom_call" | custom-call | flops 10000000000 | bytes 30000000 | tf_op jit(solution)/shard_map/pallas_call | solution.py:537
  62.6 3.4 %shard_map.242 = (bf16[2048,512]{1,0:T(8,128)(2,1)S(1)}, bf16[512,2048]{1,0:T(8,128)(2,1)S(1)}, f32[512,1024]{1,0:T(8,128)S(1)}, bf16[512,1024]{1,0:T(8,128)(2,1...) custom-call(f32[512,1024]{1,0:T(8,128)S(1)} %get-tuple-element.116.refs_0_, ...), custom_call_target="tpu_custom_call" | custom-call | flops 10000000000 | bytes 30000000 | tf_op jit(solution)/shard_map/pallas_call | solution.py:537
  66.0 21.6 %shard_map.244 = (bf16[3,256,1024]{2,1,0:T(8,128)(2,1)S(1)}, bf16[256,1024]{1,0:T(8,128)(2,1)S(1)}, f32[4,8,1024]{2,1,0:T(8,128)S(1)}) custom-call(bf16[512,1024]{1,0:T(8,128)(2,1)S(1)} %get-tuple-element.119.refs_0_.refs_5_, bf16[768,512]{1,0:T(8,128)(2,1)S(1)} %get-tuple-element.122.refs_1_, f32[8,1024]{1,0:T(8,128)S(1)} %broadcast_in_dim.27.refs_2_.refs_4_), custom_call_target="tpu_custom_call" | custom-call | flops 10000000000 | bytes 30000000 | tf_op jit(solution)/shard_map/pallas_call | solution.py:537
  87.6 8.8 %shard_map.243 = (bf16[3,256,1024]{2,1,0:T(8,128)(2,1)S(1)}, bf16[256,1024]{1,0:T(8,128)(2,1)S(1)}, f32[4,8,1024]{2,1,0:T(8,128)S(1)}) custom-call(bf16[512,1024]{1,0:T(8,128)(2,1)S(1)} %get-tuple-element.119.refs_0_.refs_5_, bf16[768,512]{1,0:T(8,128)(2,1)S(1)} %get-tuple-element.120.refs_1_, f32[8,1024]{1,0:T(8,128)S(1)} %broadcast_in_dim.27.refs_2_.refs_4_), custom_call_target="tpu_custom_call" | custom-call | flops 10000000000 | bytes 30000000 | tf_op jit(solution)/shard_map/pallas_call | solution.py:537
  96.4 22.5 %shard_map.245 = (bf16[512,1024]{1,0:T(8,128)(2,1)S(1)}, bf16[1024,512]{1,0:T(8,128)(2,1)}, bf16[2048,1024]{1,0:T(8,128)(2,1)S(1)}, bf16[2048,1024]{1,0:T(8,128)...) custom-call(bf16[256,1024]{1,0:T(8,128)(2,1)S(1)} %get-tuple-element, ...), custom_call_target="tpu_custom_call" | custom-call | flops 10000000000 | bytes 30000000 | tf_op jit(solution)/shard_map/pallas_call | solution.py:537
  118.9 5.1 %shard_map.246 = (bf16[2048,512]{1,0:T(8,128)(2,1)S(1)}, bf16[2048,512]{1,0:T(8,128)(2,1)S(1)}, bf16[512,512]{1,0:T(8,128)(2,1)S(1)}) custom-call(bf16[2048,1024]{1,0:T(8,128)(2,1)S(1)} %get-tuple-element.135.refs_0_, bf16[512,1024]{1,0:T(8,128)(2,1)S(1)} %get-tuple-element.136.refs_1_, bf16[2048,1024]{1,0:T(8,128)(2,1)S(1)} %get-tuple-element.137.refs_2_, ...), custom_call_target="tpu_custom_call" | custom-call | flops 10000000000 | bytes 30000000 | tf_op jit(solution)/shard_map/pallas_call | solution.py:537
  125.3 9.9 %shard_map.248 = (bf16[3,256,1024]{2,1,0:T(8,128)(2,1)S(1)}, bf16[512,768]{1,0:T(8,128)(2,1)S(1)}) custom-call(bf16[3,256,1024]{2,1,0:T(8,128)(2,1)S(1)} %copy-done.18, bf16[512,1024]{1,0:T(8,128)(2,1)S(1)} %get-tuple-element.132.refs_4_.refs_1_, bf16[512,1024]{1,0:T(8,128)(2,1)S(1)} %get-tuple-element.133.refs_2_, ...), custom_call_target="tpu_custom_call" | custom-call | flops 10000000000 | bytes 30000000 | tf_op jit(solution)/shard_map/pallas_call | solution.py:537
  135.2 9.9 %shard_map.247 = (bf16[3,256,1024]{2,1,0:T(8,128)(2,1)S(1)}, bf16[512,768]{1,0:T(8,128)(2,1)S(1)}) custom-call(bf16[3,256,1024]{2,1,0:T(8,128)(2,1)S(1)} %get-tuple-element.131.refs_0_, bf16[512,1024]{1,0:T(8,128)(2,1)S(1)} %get-tuple-element.132.refs_4_.refs_1_, bf16[512,1024]{1,0:T(8,128)(2,1)S(1)} %get-tuple-element.133.refs_2_, ...), custom_call_target="tpu_custom_call" | custom-call | flops 10000000000 | bytes 30000000 | tf_op jit(solution)/shard_map/pallas_call | solution.py:537
  146.9 9.7 %shard_map.250 = (f32[512,1024]{1,0:T(8,128)S(1)}, bf16[512,1024]{1,0:T(8,128)(2,1)S(1)}, bf16[2048,1024]{1,0:T(8,128)(2,1)S(1)}, bf16[512,1024]{1,0:T(8,128)(2,...) custom-call(f32[512,1024]{1,0:T(8,128)S(1)} %shard_map.249.refs_0_, ...), custom_call_target="tpu_custom_call", output_to_operand_aliasing={{2}: (5, {}), {5}: (8, {})} | custom-call | flops 10000000000 | bytes 30000000 | tf_op jit(solution)/shard_map/pallas_call | solution.py:537
  157.6 6.9 %shard_map.251 = (bf16[256,2688]{1,0:T(8,128)(2,1)S(1)}, bf16[256,2688]{1,0:T(8,128)(2,1)}) custom-call(s32[1]{0:T(128)} %bitcast.15.refs_0_.refs_5_, bf16[2048,1024]{1,0:T(8,128)(2,1)S(1)} %get-tuple-element.117.refs_1_, bf16[512,1024]{1,0:T(8,128)(2,1)S(1)} %get-tuple-element.156.refs_2_, bf16[2048,512]{1,0:T(8,128)(2,1)S(1)} %get-tuple-element.140.refs_6_.refs_3_, ...), custom_call_target="tpu_custom_call" | custom-call | flops 10000000000 | bytes 30000000 | tf_op jit(solution)/shard_map/pallas_call | solution.py:537
  165.0 2.2 copy-done.12
  170.0 4.6 %shard_map.252 = (bf16[256,2048]{1,0:T(8,128)(2,1)S(1)}, bf16[256,2048]{1,0:T(8,128)(2,1)S(1)}) custom-call(s32[1]{0:T(128)} %bitcast.15.refs_0_.refs_5_, bf16[512,1024]{1,0:T(8,128)(2,1)S(1)} %copy-done.29, bf16[2048,1024]{1,0:T(8,128)(2,1)S(1)} %copy-done.12, bf16[2048,512]{1,0:T(8,128)(2,1)S(1)} %copy-done.14, bf16[256,2688]{1,0:T(8,128)(2,1)} %get-tuple-element.164.refs_4_), custom_call_target="tpu_custom_call" | custom-call | flops 10000000000 | bytes 30000000 | tf_op jit(solution)/shard_map/pallas_call | solution.py:537
  178.3 4.3 %shard_map.253.refs_7_.refs_2_ = bf16[3,128,1024]{2,1,0:T(8,128)(2,1)S(1)} custom-call(bf16[3,256,1024]{2,1,0:T(8,128)(2,1)S(1)} %copy-done.27, bf16[512,1024]{1,0:T(8,128)(2,1)S(1)} %copy-done.23, bf16[512,1024]{1,0:T(8,128)(2,1)S(1)} %copy-done.16, f32[4,8,1024]{2,1,0:T(8,128)S(1)} %get-tuple-element.155.refs_3_, ...), custom_call_target="tpu_custom_call" | custom-call | flops 15000000512 | bytes 45000000 | tf_op jit(solution)/shard_map/pallas_call | solution.py:537
  184.7 6.5 %shard_map.254 = (bf16[3,128,1024]{2,1,0:T(8,128)(2,1)S(1)}, bf16[256,768]{1,0:T(8,128)(2,1)S(1)}, bf16[256,768]{1,0:T(8,128)(2,1)S(1)}) custom-call(bf16[3,256,1024]{2,1,0:T(8,128)(2,1)S(1)} %copy-done.27, bf16[512,1024]{1,0:T(8,128)(2,1)S(1)} %copy-done.23, bf16[512,1024]{1,0:T(8,128)(2,1)S(1)} %copy-done.16, ...), custom_call_target="tpu_custom_call" | custom-call | flops 15000000512 | bytes 45000000 | tf_op jit(solution)/shard_map/pallas_call | solution.py:537
  191.5 2.5 collective-permute-done.9
  199.2 4.3 %shard_map.255.refs_7_.refs_4_ = bf16[3,128,1024]{2,1,0:T(8,128)(2,1)S(1)} custom-call(bf16[3,256,1024]{2,1,0:T(8,128)(2,1)S(1)} %copy-done.25, bf16[512,1024]{1,0:T(8,128)(2,1)S(1)} %copy-done.23, bf16[512,1024]{1,0:T(8,128)(2,1)S(1)} %copy-done.16, f32[4,8,1024]{2,1,0:T(8,128)S(1)} %get-tuple-element.175.refs_3_, ...), custom_call_target="tpu_custom_call" | custom-call | flops 15000000512 | bytes 45000000 | tf_op jit(solution)/shard_map/pallas_call | solution.py:537
  208.3 2.6 collective-permute-start.24
  211.1 6.5 %shard_map.256 = (bf16[3,128,1024]{2,1,0:T(8,128)(2,1)S(1)}, bf16[256,768]{1,0:T(8,128)(2,1)S(1)}, bf16[256,768]{1,0:T(8,128)(2,1)S(1)}) custom-call(bf16[3,256,1024]{2,1,0:T(8,128)(2,1)S(1)} %copy-done.25, bf16[512,1024]{1,0:T(8,128)(2,1)S(1)} %copy-done.23, bf16[512,1024]{1,0:T(8,128)(2,1)S(1)} %copy-done.16, ...), custom_call_target="tpu_custom_call" | custom-call | flops 15000000512 | bytes 45000000 | tf_op jit(solution)/shard_map/pallas_call | solution.py:537
  217.8 3.1 %collective-permute-done.24 = bf16[16,4736]{1,0:T(8,128)(2,1)S(1)} collective-permute-done((bf16[16,4736]{1,0:T(8,128)(2,1)S(1)}, bf16[16,4736]{1,0:T(8,128)(2,1)S(1)}, u32[]{:S(2)}, u32[]{:S(2)}) %collective-permute-start.24) | collective-permute-done | bytes 151584 | tf_op jit(solution)/shard_map/ppermute | solution.py:553
  221.2 2.2 collective-permute-start.26
  228.0 8.1 %collective-permute-done.27 = bf16[16,4736]{1,0:T(8,128)(2,1)S(1)} collective-permute-done((bf16[16,4736]{1,0:T(8,128)(2,1)S(1)}, bf16[16,4736]{1,0:T(8,128)(2,1)S(1)}, u32[]{:S(2)}, u32[]{:S(2)}) %collective-permute-start.27) | collective-permute-done | bytes 151584 | tf_op jit(solution)/shard_map/ppermute | solution.py:553
  238.5 5.6 %collective-permute-done.16 = bf16[2,2,16,1536]{3,2,1,0:T(8,128)(2,1)S(1)} collective-permute-done((bf16[2,2,16,1536]{3,2,1,0:T(8,128)(2,1)S(1)}, bf16[2,2,16,1536]{3,2,1,0:T(8,128)(2,1)S(1)}, u32[]{:S(2)}, u32[]{:S(2)}) %collective-permute-start.16) | collective-permute-done | bytes 196640 | tf_op jit(solution)/shard_map/ppermute | solution.py:553
  244.2 2.2 collective-permute-start.17
  253.5 3.2 %collective-permute-start.20 = (bf16[16,1536]{1,0:T(8,128)(2,1)S(1)}, bf16[16,1536]{1,0:T(8,128)(2,1)S(1)}, u32[]{:S(2)}, u32[]{:S(2)}) collective-permute-start(bf16[16,1536]{1,0:T(8,128)(2,1)S(1)} %fusion.12), channel_id=1, source_target_pairs={{0,8},{2,10},{4,12},{6,14},{8,0},{10,2},{12,4},{14,6},{16,24},{18,... | collective-permute-start | bytes 147464 | tf_op jit(solution)/shard_map/ppermute | solution.py:553
  259.2 4.8 %collective-permute-done.21 = bf16[16,1536]{1,0:T(8,128)(2,1)S(1)} collective-permute-done((bf16[16,1536]{1,0:T(8,128)(2,1)S(1)}, bf16[16,1536]{1,0:T(8,128)(2,1)S(1)}, u32[]{:S(2)}, u32[]{:S(2)}) %collective-permute-start.21) | collective-permute-done | bytes 49184 | tf_op jit(solution)/shard_map/ppermute | solution.py:553
  268.2 3.3 %shard_map.257 = f32[1024,512]{1,0:T(8,128)} custom-call(bf16[512,1536]{1,0:T(8,128)(2,1)S(1)} %bitcast.110, f32[512,1024]{1,0:T(8,128)S(1)} %copy-done.10, bf16[3,128,1024]{2,1,0:T(8,128)(2,1)S(1)} %shard_map.253.refs_7_.refs_2_, bf16[3,128,1024]{2,1,0:T(8,128)(2,1)S(1)} %get-tuple-element.173.refs_3_, ...), custom_call_target="tpu_custom_call" | custom-call | flops 5000000000 | bytes 15000000 | tf_op jit(solution)/shard_map/pallas_call | solution.py:537
  (213 shorter events, 70.3 us)
Async XLA Ops:
  4.4 12.4 %collective-permute-start = (bf16[1,128,1536]{2,1,0:T(8,128)(2,1)}, bf16[1,128,1536]{2,1,0:T(8,128)(2,1)}, u32[]{:S(2)}, u32[]{:S(2)}) collective-permute-start(bf16[1,128,1536]{2,1,0:T(8,128)(2,1)} %pad_maximum_fusion.3), channel_id=1, source_target_pairs={{0,1},{1,0},{2,3},{3,2},{4,5},{5,4},{6,7},{7,6},{8,9},{9,8},{10,11... | collective-permute-start | bytes 1179656 | tf_op jit(solution)/shard_map/ppermute | solution.py:553
  18.0 2.4 collective-permute-start.1
  18.6 17.9 %collective-permute-start.2 = (bf16[1,128,2688]{2,1,0:T(8,128)(2,1)S(1)}, bf16[1,128,2688]{2,1,0:T(8,128)(2,1)S(1)}, u32[]{:S(2)}, u32[]{:S(2)}) collective-permute-start(bf16[1,128,2688]{2,1,0:T(8,128)(2,1)S(1)} %pad_maximum_fusion), channel_id=1, source_target_pairs={{0,1},{1,0},{2,3},{3,2},{4,5},{5,4},{6,7},{7,6},{8,9},{9,8},{10,11... | collective-permute-start | bytes 2064392 | tf_op jit(solution)/shard_map/ppermute | solution.py:553
  36.8 14.8 %collective-permute-start.3 = (bf16[2,128,2688]{2,1,0:T(8,128)(2,1)S(1)}, bf16[2,128,2688]{2,1,0:T(8,128)(2,1)S(1)}, u32[]{:S(2)}, u32[]{:S(2)}) collective-permute-start(bf16[2,128,2688]{2,1,0:T(8,128)(2,1)S(1)} %maximum_select_fusion.3), channel_id=1, source_target_pairs={{0,2},{2,0},{4,6},{6,4},{8,10},{10,8},{12,14},{14,12},{16,18},{18,... | collective-permute-start | bytes 4128776 | tf_op jit(solution)/shard_map/ppermute | solution.py:553
  36.9 14.4 %collective-permute-start.4 = (bf16[1,128,2048]{2,1,0:T(8,128)(2,1)S(1)}, bf16[1,128,2048]{2,1,0:T(8,128)(2,1)S(1)}, u32[]{:S(2)}, u32[]{:S(2)}) collective-permute-start(bf16[1,128,2048]{2,1,0:T(8,128)(2,1)S(1)} %pad_maximum_fusion.2), channel_id=1, source_target_pairs={{0,1},{1,0},{2,3},{3,2},{4,5},{5,4},{6,7},{7,6},{8,9},{9,8},{10,11... | collective-permute-start | bytes 1572872 | tf_op jit(solution)/shard_map/ppermute | solution.py:553
  51.5 10.1 %collective-permute-start.5 = (bf16[2,128,2048]{2,1,0:T(8,128)(2,1)S(1)}, bf16[2,128,2048]{2,1,0:T(8,128)(2,1)S(1)}, u32[]{:S(2)}, u32[]{:S(2)}) collective-permute-start(bf16[2,128,2048]{2,1,0:T(8,128)(2,1)S(1)} %maximum_select_fusion.5), channel_id=1, source_target_pairs={{0,2},{2,0},{4,6},{6,4},{8,10},{10,8},{12,14},{14,12},{16,18},{18,... | collective-permute-start | bytes 3145736 | tf_op jit(solution)/shard_map/ppermute | solution.py:553
  164.5 10.0 %collective-permute-start.6 = (bf16[256,2688]{1,0:T(8,128)(2,1)}, bf16[256,2688]{1,0:T(8,128)(2,1)}, u32[]{:S(2)}, u32[]{:S(2)}) collective-permute-start(bf16[256,2688]{1,0:T(8,128)(2,1)} %get-tuple-element.164.refs_4_), channel_id=1, source_target_pairs={{0,2},{2,0},{4,6},{6,4},{8,10},{10,8},{12,14},{14,12},{16,18},{18,... | collective-permute-start | bytes 4128776 | tf_op jit(solution)/shard_map/ppermute | solution.py:553
  176.5 17.5 %collective-permute-start.9 = (bf16[2,2,2,16,2688]{4,3,2,1,0:T(8,128)(2,1)S(1)}, bf16[2,2,2,16,2688]{4,3,2,1,0:T(8,128)(2,1)S(1)}, u32[]{:S(2)}, u32[]{:S(2)}) collective-permute-start(bf16[2,2,2,16,2688]{4,3,2,1,0:T(8,128)(2,1)S(1)} %get-tuple-element.197), channel_id=1, source_target_pairs={{0,1},{1,0},{2,3},{3,2},{4,5},{5,4},{6,7},{7,6},{8,9},{9,8},{10,11... | collective-permute-start | bytes 2064392 | tf_op jit(solution)/shard_map/ppermute | solution.py:553
  178.3 4.3 %collective-permute-start.7 = (bf16[256,2048]{1,0:T(8,128)(2,1)S(1)}, bf16[256,2048]{1,0:T(8,128)(2,1)S(1)}, u32[]{:S(2)}, u32[]{:S(2)}) collective-permute-start(bf16[256,2048]{1,0:T(8,128)(2,1)S(1)} %get-tuple-element.170), channel_id=1, source_target_pairs={{0,2},{2,0},{4,6},{6,4},{8,10},{10,8},{12,14},{14,12},{16,18},{18,... | collective-permute-start | bytes 3145736 | tf_op jit(solution)/shard_map/ppermute | solution.py:553
  183.1 14.8 %collective-permute-start.8 = (bf16[2,2,2,16,2048]{4,3,2,1,0:T(8,128)(2,1)S(1)}, bf16[2,2,2,16,2048]{4,3,2,1,0:T(8,128)(2,1)S(1)}, u32[]{:S(2)}, u32[]{:S(2)}) collective-permute-start(bf16[2,2,2,16,2048]{4,3,2,1,0:T(8,128)(2,1)S(1)} %get-tuple-element.209), channel_id=1, source_target_pairs={{0,4},{2,6},{4,0},{6,2},{8,12},{10,14},{12,8},{14,10},{16,20},{18,... | collective-permute-start | bytes 1572872 | tf_op jit(solution)/shard_map/ppermute | solution.py:553
  191.2 12.3 %collective-permute-start.12 = (bf16[256,768]{1,0:T(8,128)(2,1)S(1)}, bf16[256,768]{1,0:T(8,128)(2,1)S(1)}, u32[]{:S(2)}, u32[]{:S(2)}) collective-permute-start(bf16[256,768]{1,0:T(8,128)(2,1)S(1)} %get-tuple-element.178), channel_id=1, source_target_pairs={{0,2},{2,0},{4,6},{6,4},{8,10},{10,8},{12,14},{14,12},{16,18},{18,... | collective-permute-start | bytes 1179656 | tf_op jit(solution)/shard_map/ppermute | solution.py:553
  194.2 10.7 %collective-permute-start.10 = (bf16[2,2,16,2688]{3,2,1,0:T(8,128)(2,1)S(1)}, bf16[2,2,16,2688]{3,2,1,0:T(8,128)(2,1)S(1)}, u32[]{:S(2)}, u32[]{:S(2)}) collective-permute-start(bf16[2,2,16,2688]{3,2,1,0:T(8,128)(2,1)S(1)} %get-tuple-element.215), channel_id=1, source_target_pairs={{0,4},{2,6},{4,0},{6,2},{8,12},{10,14},{12,8},{14,10},{16,20},{18,... | collective-permute-start | bytes 1032200 | tf_op jit(solution)/shard_map/ppermute | solution.py:553
  198.1 8.4 %collective-permute-start.11 = (bf16[2,2,16,2048]{3,2,1,0:T(8,128)(2,1)S(1)}, bf16[2,2,16,2048]{3,2,1,0:T(8,128)(2,1)S(1)}, u32[]{:S(2)}, u32[]{:S(2)}) collective-permute-start(bf16[2,2,16,2048]{3,2,1,0:T(8,128)(2,1)S(1)} %get-tuple-element.221), channel_id=1, source_target_pairs={{0,1},{1,0},{2,3},{3,2},{4,5},{5,4},{6,7},{7,6},{8,9},{9,8},{10,11... | collective-permute-start | bytes 786440 | tf_op jit(solution)/shard_map/ppermute | solution.py:553
  203.7 22.6 %collective-permute-start.14 = (bf16[2,2,2,16,768]{4,3,1,0,2:T(8,128)(2,1)S(1)}, bf16[2,2,2,16,768]{4,3,1,0,2:T(8,128)(2,1)S(1)}, u32[]{:S(2)}, u32[]{:S(2)}) collective-permute-start(bf16[2,2,2,16,768]{4,3,1,0,2:T(8,128)(2,1)S(1)} %bitcast.129), channel_id=1, source_target_pairs={{0,1},{1,0},{2,3},{3,2},{4,5},{5,4},{6,7},{7,6},{8,9},{9,8},{10,11... | collective-permute-start | bytes 589832 | tf_op jit(solution)/shard_map/ppermute | solution.py:553
  206.7 11.1 %collective-permute-start.23 = (bf16[16,4736]{1,0:T(8,128)(2,1)S(1)}, bf16[16,4736]{1,0:T(8,128)(2,1)S(1)}, u32[]{:S(2)}, u32[]{:S(2)}) collective-permute-start(bf16[16,4736]{1,0:T(8,128)(2,1)S(1)} %get-tuple-element.216), channel_id=1, source_target_pairs={{0,8},{2,10},{4,12},{6,14},{8,0},{10,2},{12,4},{14,6},{16,24},{18,... | collective-permute-start | bytes 454664 | tf_op jit(solution)/shard_map/ppermute | solution.py:553
  208.3 12.5 %collective-permute-start.24 = (bf16[16,4736]{1,0:T(8,128)(2,1)S(1)}, bf16[16,4736]{1,0:T(8,128)(2,1)S(1)}, u32[]{:S(2)}, u32[]{:S(2)}) collective-permute-start(bf16[16,4736]{1,0:T(8,128)(2,1)S(1)} %get-tuple-element.218), channel_id=1, source_target_pairs={{0,16},{2,18},{4,20},{6,22},{8,24},{10,26},{12,28},{14,30},{16,0},... | collective-permute-start | bytes 454664 | tf_op jit(solution)/shard_map/ppermute | solution.py:553
  210.9 10.0 %collective-permute-start.25 = (bf16[16,4736]{1,0:T(8,128)(2,1)S(1)}, bf16[16,4736]{1,0:T(8,128)(2,1)S(1)}, u32[]{:S(2)}, u32[]{:S(2)}) collective-permute-start(bf16[16,4736]{1,0:T(8,128)(2,1)S(1)} %get-tuple-element.217), channel_id=1, source_target_pairs={{0,24},{2,26},{4,28},{6,30},{8,16},{10,18},{12,20},{14,22},{16,8},... | collective-permute-start | bytes 454664 | tf_op jit(solution)/shard_map/ppermute | solution.py:553
  217.7 3.3 %collective-permute-start.13 = (bf16[256,768]{1,0:T(8,128)(2,1)S(1)}, bf16[256,768]{1,0:T(8,128)(2,1)S(1)}, u32[]{:S(2)}, u32[]{:S(2)}) collective-permute-start(bf16[256,768]{1,0:T(8,128)(2,1)S(1)} %get-tuple-element.188), channel_id=1, source_target_pairs={{0,2},{2,0},{4,6},{6,4},{8,10},{10,8},{12,14},{14,12},{16,18},{18,... | collective-permute-start | bytes 1179656 | tf_op jit(solution)/shard_map/ppermute | solution.py:553
  221.2 6.8 %collective-permute-start.26 = (bf16[16,4736]{1,0:T(8,128)(2,1)S(1)}, bf16[16,4736]{1,0:T(8,128)(2,1)S(1)}, u32[]{:S(2)}, u32[]{:S(2)}) collective-permute-start(bf16[16,4736]{1,0:T(8,128)(2,1)S(1)} %add_convert_fusion.9), channel_id=1, source_target_pairs={{0,8},{2,10},{4,12},{6,14},{8,0},{10,2},{12,4},{14,6},{16,24},{18,... | collective-permute-start | bytes 454664 | tf_op jit(solution)/shard_map/ppermute | solution.py:553
  223.4 12.6 %collective-permute-start.27 = (bf16[16,4736]{1,0:T(8,128)(2,1)S(1)}, bf16[16,4736]{1,0:T(8,128)(2,1)S(1)}, u32[]{:S(2)}, u32[]{:S(2)}) collective-permute-start(bf16[16,4736]{1,0:T(8,128)(2,1)S(1)} %add_convert_fusion.9), channel_id=1, source_target_pairs={{0,16},{2,18},{4,20},{6,22},{8,24},{10,26},{12,28},{14,30},{16,0},... | collective-permute-start | bytes 454664 | tf_op jit(solution)/shard_map/ppermute | solution.py:553
  224.5 11.5 %collective-permute-start.28 = (bf16[16,4736]{1,0:T(8,128)(2,1)S(1)}, bf16[16,4736]{1,0:T(8,128)(2,1)S(1)}, u32[]{:S(2)}, u32[]{:S(2)}) collective-permute-start(bf16[16,4736]{1,0:T(8,128)(2,1)S(1)} %add_convert_fusion.9), channel_id=1, source_target_pairs={{0,24},{2,26},{4,28},{6,30},{8,16},{10,18},{12,20},{14,22},{16,8},... | collective-permute-start | bytes 454664 | tf_op jit(solution)/shard_map/ppermute | solution.py:553
  225.9 10.2 %collective-permute-start.15 = (bf16[2,2,2,16,768]{4,3,1,0,2:T(8,128)(2,1)S(1)}, bf16[2,2,2,16,768]{4,3,1,0,2:T(8,128)(2,1)S(1)}, u32[]{:S(2)}, u32[]{:S(2)}) collective-permute-start(bf16[2,2,2,16,768]{4,3,1,0,2:T(8,128)(2,1)S(1)} %bitcast.130), channel_id=1, source_target_pairs={{0,1},{1,0},{2,3},{3,2},{4,5},{5,4},{6,7},{7,6},{8,9},{9,8},{10,11... | collective-permute-start | bytes 589832 | tf_op jit(solution)/shard_map/ppermute | solution.py:553
  236.2 7.9 %collective-permute-start.16 = (bf16[2,2,16,1536]{3,2,1,0:T(8,128)(2,1)S(1)}, bf16[2,2,16,1536]{3,2,1,0:T(8,128)(2,1)S(1)}, u32[]{:S(2)}, u32[]{:S(2)}) collective-permute-start(bf16[2,2,16,1536]{3,2,1,0:T(8,128)(2,1)S(1)} %fusion.9.refs_6_), channel_id=1, source_target_pairs={{0,4},{2,6},{4,0},{6,2},{8,12},{10,14},{12,8},{14,10},{16,20},{18,... | collective-permute-start | bytes 589832 | tf_op jit(solution)/shard_map/ppermute | solution.py:553
  237.9 13.1 %collective-permute-start.29 = (bf16[2,2,1,16,4736]{4,3,2,1,0:T(8,128)(2,1)S(1)}, bf16[2,2,1,16,4736]{4,3,2,1,0:T(8,128)(2,1)S(1)}, u32[]{:S(2)}, u32[]{:S(2)}) collective-permute-start(bf16[2,2,1,16,4736]{4,3,2,1,0:T(8,128)(2,1)S(1)} %maximum_select_fusion.8), channel_id=1, source_target_pairs={{0,4},{2,6},{4,0},{6,2},{8,12},{10,14},{12,8},{14,10},{16,20},{18,... | collective-permute-start | bytes 1818632 | tf_op jit(solution)/shard_map/ppermute | solution.py:553
  244.2 7.1 %collective-permute-start.17 = (bf16[16,1536]{1,0:T(8,128)(2,1)S(1)}, bf16[16,1536]{1,0:T(8,128)(2,1)S(1)}, u32[]{:S(2)}, u32[]{:S(2)}) collective-permute-start(bf16[16,1536]{1,0:T(8,128)(2,1)S(1)} %get-tuple-element.238), channel_id=1, source_target_pairs={{0,8},{2,10},{4,12},{6,14},{8,0},{10,2},{12,4},{14,6},{16,24},{18,... | collective-permute-start | bytes 147464 | tf_op jit(solution)/shard_map/ppermute | solution.py:553
  246.4 5.5 %collective-permute-start.18 = (bf16[16,1536]{1,0:T(8,128)(2,1)S(1)}, bf16[16,1536]{1,0:T(8,128)(2,1)S(1)}, u32[]{:S(2)}, u32[]{:S(2)}) collective-permute-start(bf16[16,1536]{1,0:T(8,128)(2,1)S(1)} %get-tuple-element.240), channel_id=1, source_target_pairs={{0,16},{2,18},{4,20},{6,22},{8,24},{10,26},{12,28},{14,30},{16,0},... | collective-permute-start | bytes 147464 | tf_op jit(solution)/shard_map/ppermute | solution.py:553
  247.5 6.0 %collective-permute-start.19 = (bf16[16,1536]{1,0:T(8,128)(2,1)S(1)}, bf16[16,1536]{1,0:T(8,128)(2,1)S(1)}, u32[]{:S(2)}, u32[]{:S(2)}) collective-permute-start(bf16[16,1536]{1,0:T(8,128)(2,1)S(1)} %get-tuple-element.239), channel_id=1, source_target_pairs={{0,24},{2,26},{4,28},{6,30},{8,16},{10,18},{12,20},{14,22},{16,8},... | collective-permute-start | bytes 147464 | tf_op jit(solution)/shard_map/ppermute | solution.py:553
  251.2 13.0 %collective-permute-start.30 = (bf16[128,4736]{1,0:T(8,128)(2,1)S(1)}, bf16[128,4736]{1,0:T(8,128)(2,1)S(1)}, u32[]{:S(2)}, u32[]{:S(2)}) collective-permute-start(bf16[128,4736]{1,0:T(8,128)(2,1)S(1)} %bitcast.115), channel_id=1, source_target_pairs={{0,2},{2,0},{4,6},{6,4},{8,10},{10,8},{12,14},{14,12},{16,18},{18,... | collective-permute-start | bytes 3637256 | tf_op jit(solution)/shard_map/ppermute | solution.py:553
  253.5 5.7 %collective-permute-start.20 = (bf16[16,1536]{1,0:T(8,128)(2,1)S(1)}, bf16[16,1536]{1,0:T(8,128)(2,1)S(1)}, u32[]{:S(2)}, u32[]{:S(2)}) collective-permute-start(bf16[16,1536]{1,0:T(8,128)(2,1)S(1)} %fusion.12), channel_id=1, source_target_pairs={{0,8},{2,10},{4,12},{6,14},{8,0},{10,2},{12,4},{14,6},{16,24},{18,... | collective-permute-start | bytes 147464 | tf_op jit(solution)/shard_map/ppermute | solution.py:553
  256.8 7.2 %collective-permute-start.21 = (bf16[16,1536]{1,0:T(8,128)(2,1)S(1)}, bf16[16,1536]{1,0:T(8,128)(2,1)S(1)}, u32[]{:S(2)}, u32[]{:S(2)}) collective-permute-start(bf16[16,1536]{1,0:T(8,128)(2,1)S(1)} %fusion.12), channel_id=1, source_target_pairs={{0,16},{2,18},{4,20},{6,22},{8,24},{10,26},{12,28},{14,30},{16,0},... | collective-permute-start | bytes 147464 | tf_op jit(solution)/shard_map/ppermute | solution.py:553
  257.6 6.4 %collective-permute-start.22 = (bf16[16,1536]{1,0:T(8,128)(2,1)S(1)}, bf16[16,1536]{1,0:T(8,128)(2,1)S(1)}, u32[]{:S(2)}, u32[]{:S(2)}) collective-permute-start(bf16[16,1536]{1,0:T(8,128)(2,1)S(1)} %fusion.12), channel_id=1, source_target_pairs={{0,24},{2,26},{4,28},{6,30},{8,16},{10,18},{12,20},{14,22},{16,8},... | collective-permute-start | bytes 147464 | tf_op jit(solution)/shard_map/ppermute | solution.py:553
  266.6 5.7 %collective-permute-start.31 = (bf16[2,2,1,16,1536]{4,3,1,0,2:T(8,128)(2,1)S(1)}, bf16[2,2,1,16,1536]{4,3,1,0,2:T(8,128)(2,1)S(1)}, u32[]{:S(2)}, u32[]{:S(2)}) collective-permute-start(bf16[2,2,1,16,1536]{4,3,1,0,2:T(8,128)(2,1)S(1)} %bitcast.112), channel_id=1, source_target_pairs={{0,4},{2,6},{4,0},{6,2},{8,12},{10,14},{12,8},{14,10},{16,20},{18,... | collective-permute-start | bytes 589832 | tf_op jit(solution)/shard_map/ppermute | solution.py:553
  (36 other events, 204.2 us)

commit v4 on v3

--- a/solution.py
+++ b/solution.py
@@ -809,6 +809,11 @@
         limit=4,
     )
     outer = Sum(keep_u, send_u)
+    y_bit = bits_of("dp")[-2]
+    x_bits = bits_of("shard")
+    outer = Sum(keep_u, send_u)
+    for label in x_bits:
+        outer.halve(*label)
     keep_i, send_i = call(
         functools.partial(inner_grad_kernel, shards),
         [((half, hidden), bf16)] * 2,
@@ -816,13 +821,14 @@
         (core, yr1, du1, more_i),
         [SM] + [VM] * 3,
         limit=4,
-        deps=(send_u,),
+        deps=(outer.sent,),
     )
+    inner = Sum(keep_i, send_i)
     parts = []
 
-    def part(p, seg):
+    def part(p, *deps):
         qkv, lse = ((qkv1a, lse1a), (qkv1b, lse1b))[p // 2]
-        args = (qkv, o1, do1, lse, seg)
+        args = (qkv, o1, do1, lse, seg_rows)
         specs = [VM] * 5
         outs = [((3, 2 * size, length), bf16)]
         if p % 2:
@@ -830,42 +836,33 @@
             specs += [SM] + [VM] * 3
             outs += [((half, 3 * rows), bf16)] * 2
         kernel = functools.partial(attend_part_kernel, p, size, shards)
-        results = call(kernel, outs, back, args, specs, 15, 10)
+        results = call(kernel, outs, back, args, specs, 15, 10, deps=deps)
         parts.append(results[0])
         return results[1:]
 
-    y_bit = bits_of("dp")[-2]
-    x_bits = bits_of("shard")
-    outer.after(send_i)
-    for label in x_bits:
-        outer.halve(*label)
-    inner = Sum(keep_i, tie(send_i, outer.sent))
-    part(0, tie(seg_rows, outer.sent))
-    inner.after(parts[0])
-    inner.halve(*y_bit)
-    first = Sum(*part(1, tie(seg_rows, inner.sent)))
-    outer.after(parts[1])
+    part(0, send_i)
+    outer.keep = copy_after(outer.keep, parts[0])
     outer.halve(*y_bit)
-    inner.after(parts[1])
     for label in x_bits:
         inner.halve(*label)
-    part(2, tie(seg_rows, inner.sent, outer.sent, first.sent))
-    for one in (first, inner, outer):
-        one.after(parts[2])
+    first = Sum(*part(1, outer.sent, inner.sent))
+    part(2, parts[1])
+    outer.keep = copy_after(outer.keep, parts[1])
+    inner.halve(*y_bit)
     for label in x_bits:
         first.halve(*label)
+    outer.settle()
+    second = Sum(*part(3, inner.sent, first.sent, outer.value))
     feed = join(outer, inner)
     feed.scatter()
-    second = Sum(*part(3, tie(seg_rows, feed.keep, first.sent)))
-    feed.after(second.sent)
-    feed.settle()
     for label in x_bits:
         second.halve(*label)
-    feed.after(second.sent)
-    feed.collect()
-    first.after(second.sent)
     heads = join(first, second)
     heads.halve(*y_bit)
+    heads.settle()
+    feed.keep = copy_after(feed.keep, heads.value)
+    feed.settle()
+    feed.collect()
     (input_grad,) = call(
         functools.partial(input_kernel, True),
         [((length, width), f32)],
@@ -887,7 +884,7 @@
     dwo = feed.columns(hidden, hidden + width)
     dpar = feed.columns(hidden + width, inner_at)
     dwi = feed.columns(inner_at, inner_at + hidden)
-    heads.value = copy_after(heads.value, dwu, dwi, dwo)
+    heads.value = copy_after(heads.value, feed.value)
     heads.double(*y_bit)
     heads.finish()
     dqkv = [

time: 279 us -> 291 us (1.043)
  waiting for transfers between devices: 46.7 us -> 52.6 us
  starting transfers between devices: 38.8 us -> 43.3 us
  local copies, waits for them, and re-layouts: 20.6 us -> 16.5 us
  other arithmetic: 13.2 us -> 16.7 us
    ppermute x33, waiting for transfers between devices: 46.7 us -> 52.6 us  [flip(): return lax.ppermute(value, axis, [(i, i ^ bit) for i in range(count)])]
    ppermute x33, starting transfers between devices: 38.8 us -> 43.3 us  [flip(): return lax.ppermute(value, axis, [(i, i ^ bit) for i in range(count)])]
    unnamed x72 -> x64, local copies, waits for them, and re-layouts: 12.2 us -> 7.94 us
    pallas_call x21 -> x24, Pallas kernels: 155 us -> 155 us  [call(): pl.pallas_call(run, out_shape=[jax.ShapeDtypeStruct(shape, dtype) for sha...]
  transfers between devices with their start and end apart: 33 -> 33, of which waited for: 17 -> 15; matrix products, arithmetic and copies ran while one was open for 4% -> 4% of each run, Pallas kernels for 20% -> 19%
where the time goes in v4:
time: 291 us; the launch traced here: 287 us
  Pallas kernels  155 us (53%)
  waiting for transfers between devices  52.6 us (18%)
  starting transfers between devices  43.3 us (15%)
  other arithmetic  16.7 us (6%)
  local copies, waits for them, and re-layouts  16.5 us (6%)
  between operations  3.15 us (1%)
    pallas_call x24, Pallas kernels, call(): pl.pallas_call(run, out_shape=[jax.ShapeDtypeStruct(shape, dtype) for sha...  155 us
    ppermute x33, waiting for transfers between devices, flip(): return lax.ppermute(value, axis, [(i, i ^ bit) for i in range(count)])  52.6 us
    ppermute x33, starting transfers between devices, flip(): return lax.ppermute(value, axis, [(i, i ^ bit) for i in range(count)])  43.3 us
    unnamed x64, local copies, waits for them, and re-layouts  7.94 us
  transfers between devices with their start and end apart: 33, of which 15 were waited for; matrix products, arithmetic and copies ran while one was open for 4% of the time, Pallas kernels for 19%

profile of v4, /device:TPU:0, one launch (start us, length us, event | category | flops | bytes accessed | tf_op | source)
XLA Modules:
  0.0 287.1 jit_solution(15233863979194107182)
XLA Ops:
  4.4 2.9 %collective-permute-start = (bf16[1,128,1536]{2,1,0:T(8,128)(2,1)}, bf16[1,128,1536]{2,1,0:T(8,128)(2,1)}, u32[]{:S(2)}, u32[]{:S(2)}) collective-permute-start(bf16[1,128,1536]{2,1,0:T(8,128)(2,1)} %pad_maximum_fusion.3), channel_id=1, source_target_pairs={{0,1},{1,0},{2,3},{3,2},{4,5},{5,4},{6,7},{7,6},{8,9},{9,8},{10,11... | collective-permute-start | bytes 1179656 | tf_op jit(solution)/shard_map/ppermute | solution.py:553
  13.2 3.5 %collective-permute-done = bf16[1,128,1536]{2,1,0:T(8,128)(2,1)} collective-permute-done((bf16[1,128,1536]{2,1,0:T(8,128)(2,1)}, bf16[1,128,1536]{2,1,0:T(8,128)(2,1)}, u32[]{:S(2)}, u32[]{:S(2)}) %collective-permute-start) | collective-permute-done | bytes 393248 | tf_op jit(solution)/shard_map/ppermute | solution.py:553
  21.1 8.7 %shard_map.239 = (bf16[768,512]{1,0:T(8,128)(2,1)S(1)}, bf16[3,256,1024]{2,1,0:T(8,128)(2,1)S(1)}, bf16[256,1024]{1,0:T(8,128)(2,1)S(1)}, f32[4,8,1024]{2,1,0:T(8,128)S(1)}) custom-call(bf16[512,1024]{1,0:T(8,128)(2,1)S(1)} %shard_map.238.refs_0_.refs_2_.refs_6_, bf16[512,1536]{1,0:T(8,128)(2,1)S(1)} %bitcast.124, f32[8,1024]{1,0:T(8,128)S(1)} %broadcast_in_dim.27.refs_2_.refs_4_), custom_call_target="tpu_custom_call" | custom-call | flops 10000000000 | bytes 30000000 | tf_op jit(solution)/shard_map/pallas_call | solution.py:537
  31.0 5.6 %collective-permute-done.2 = bf16[1,128,2688]{2,1,0:T(8,128)(2,1)S(1)} collective-permute-done((bf16[1,128,2688]{2,1,0:T(8,128)(2,1)S(1)}, bf16[1,128,2688]{2,1,0:T(8,128)(2,1)S(1)}, u32[]{:S(2)}, u32[]{:S(2)}) %collective-permute-start.2) | collective-permute-done | bytes 688160 | tf_op jit(solution)/shard_map/ppermute | solution.py:553
  38.7 8.7 %shard_map.240 = (bf16[768,512]{1,0:T(8,128)(2,1)S(1)}, bf16[3,256,1024]{2,1,0:T(8,128)(2,1)S(1)}, bf16[256,1024]{1,0:T(8,128)(2,1)S(1)}, f32[4,8,1024]{2,1,0:T(8,128)S(1)}) custom-call(bf16[512,1024]{1,0:T(8,128)(2,1)S(1)} %shard_map.238.refs_0_.refs_2_.refs_6_, bf16[512,1536]{1,0:T(8,128)(2,1)S(1)} %bitcast.125, f32[8,1024]{1,0:T(8,128)S(1)} %broadcast_in_dim.27.refs_2_.refs_4_), custom_call_target="tpu_custom_call" | custom-call | flops 10000000000 | bytes 30000000 | tf_op jit(solution)/shard_map/pallas_call | solution.py:537
  48.6 2.7 collective-permute-done.4
  52.6 8.0 %shard_map.241 = (bf16[512,1024]{1,0:T(8,128)(2,1)S(1)}, bf16[512,512]{1,0:T(8,128)(2,1)S(1)}, bf16[2048,512]{1,0:T(8,128)(2,1)S(1)}, f32[512,1024]{1,0:T(8,128)...) custom-call(bf16[256,1024]{1,0:T(8,128)(2,1)S(1)} %get-tuple-element, ...), custom_call_target="tpu_custom_call" | custom-call | flops 10000000000 | bytes 30000000 | tf_op jit(solution)/shard_map/pallas_call | solution.py:537
  62.6 3.4 %shard_map.242 = (bf16[2048,512]{1,0:T(8,128)(2,1)S(1)}, bf16[512,2048]{1,0:T(8,128)(2,1)S(1)}, f32[512,1024]{1,0:T(8,128)S(1)}, bf16[512,1024]{1,0:T(8,128)(2,1...) custom-call(f32[512,1024]{1,0:T(8,128)S(1)} %get-tuple-element.101.refs_0_, ...), custom_call_target="tpu_custom_call" | custom-call | flops 10000000000 | bytes 30000000 | tf_op jit(solution)/shard_map/pallas_call | solution.py:537
  66.0 21.6 %shard_map.244 = (bf16[3,256,1024]{2,1,0:T(8,128)(2,1)S(1)}, bf16[256,1024]{1,0:T(8,128)(2,1)S(1)}, f32[4,8,1024]{2,1,0:T(8,128)S(1)}) custom-call(bf16[512,1024]{1,0:T(8,128)(2,1)S(1)} %get-tuple-element.104.refs_0_.refs_5_, bf16[768,512]{1,0:T(8,128)(2,1)S(1)} %get-tuple-element.107.refs_1_, f32[8,1024]{1,0:T(8,128)S(1)} %broadcast_in_dim.27.refs_2_.refs_4_), custom_call_target="tpu_custom_call" | custom-call | flops 10000000000 | bytes 30000000 | tf_op jit(solution)/shard_map/pallas_call | solution.py:537
  87.6 8.8 %shard_map.243 = (bf16[3,256,1024]{2,1,0:T(8,128)(2,1)S(1)}, bf16[256,1024]{1,0:T(8,128)(2,1)S(1)}, f32[4,8,1024]{2,1,0:T(8,128)S(1)}) custom-call(bf16[512,1024]{1,0:T(8,128)(2,1)S(1)} %get-tuple-element.104.refs_0_.refs_5_, bf16[768,512]{1,0:T(8,128)(2,1)S(1)} %get-tuple-element.105.refs_1_, f32[8,1024]{1,0:T(8,128)S(1)} %broadcast_in_dim.27.refs_2_.refs_4_), custom_call_target="tpu_custom_call" | custom-call | flops 10000000000 | bytes 30000000 | tf_op jit(solution)/shard_map/pallas_call | solution.py:537
  96.4 22.5 %shard_map.245 = (bf16[512,1024]{1,0:T(8,128)(2,1)S(1)}, bf16[1024,512]{1,0:T(8,128)(2,1)}, bf16[2048,1024]{1,0:T(8,128)(2,1)S(1)}, bf16[2048,1024]{1,0:T(8,128)...) custom-call(bf16[256,1024]{1,0:T(8,128)(2,1)S(1)} %get-tuple-element, ...), custom_call_target="tpu_custom_call" | custom-call | flops 10000000000 | bytes 30000000 | tf_op jit(solution)/shard_map/pallas_call | solution.py:537
  119.0 5.1 %shard_map.246 = (bf16[2048,512]{1,0:T(8,128)(2,1)S(1)}, bf16[2048,512]{1,0:T(8,128)(2,1)S(1)}, bf16[512,512]{1,0:T(8,128)(2,1)S(1)}) custom-call(bf16[2048,1024]{1,0:T(8,128)(2,1)S(1)} %get-tuple-element.120.refs_0_, bf16[512,1024]{1,0:T(8,128)(2,1)S(1)} %get-tuple-element.121.refs_1_, bf16[2048,1024]{1,0:T(8,128)(2,1)S(1)} %get-tuple-element.122.refs_2_, ...), custom_call_target="tpu_custom_call" | custom-call | flops 10000000000 | bytes 30000000 | tf_op jit(solution)/shard_map/pallas_call | solution.py:537
  125.4 9.9 %shard_map.248 = (bf16[3,256,1024]{2,1,0:T(8,128)(2,1)S(1)}, bf16[512,768]{1,0:T(8,128)(2,1)S(1)}) custom-call(bf16[3,256,1024]{2,1,0:T(8,128)(2,1)S(1)} %copy-done.15, bf16[512,1024]{1,0:T(8,128)(2,1)S(1)} %get-tuple-element.117.refs_4_.refs_1_, bf16[512,1024]{1,0:T(8,128)(2,1)S(1)} %get-tuple-element.118.refs_2_, ...), custom_call_target="tpu_custom_call" | custom-call | flops 10000000000 | bytes 30000000 | tf_op jit(solution)/shard_map/pallas_call | solution.py:537
  135.2 9.9 %shard_map.247 = (bf16[3,256,1024]{2,1,0:T(8,128)(2,1)S(1)}, bf16[512,768]{1,0:T(8,128)(2,1)S(1)}) custom-call(bf16[3,256,1024]{2,1,0:T(8,128)(2,1)S(1)} %get-tuple-element.116.refs_0_, bf16[512,1024]{1,0:T(8,128)(2,1)S(1)} %get-tuple-element.117.refs_4_.refs_1_, bf16[512,1024]{1,0:T(8,128)(2,1)S(1)} %get-tuple-element.118.refs_2_, ...), custom_call_target="tpu_custom_call" | custom-call | flops 10000000000 | bytes 30000000 | tf_op jit(solution)/shard_map/pallas_call | solution.py:537
  147.0 9.7 %shard_map.250 = (f32[512,1024]{1,0:T(8,128)S(1)}, bf16[512,1024]{1,0:T(8,128)(2,1)S(1)}, bf16[2048,1024]{1,0:T(8,128)(2,1)S(1)}, bf16[512,1024]{1,0:T(8,128)(2,...) custom-call(f32[512,1024]{1,0:T(8,128)S(1)} %shard_map.249.refs_0_, ...), custom_call_target="tpu_custom_call", output_to_operand_aliasing={{2}: (5, {}), {5}: (8, {})} | custom-call | flops 10000000000 | bytes 30000000 | tf_op jit(solution)/shard_map/pallas_call | solution.py:537
  157.7 6.9 %shard_map.251 = (bf16[256,2688]{1,0:T(8,128)(2,1)S(1)}, bf16[256,2688]{1,0:T(8,128)(2,1)}) custom-call(s32[1]{0:T(128)} %bitcast.15.refs_0_.refs_5_, bf16[2048,1024]{1,0:T(8,128)(2,1)S(1)} %get-tuple-element.102.refs_1_, bf16[512,1024]{1,0:T(8,128)(2,1)S(1)} %get-tuple-element.144.refs_2_, bf16[2048,512]{1,0:T(8,128)(2,1)S(1)} %get-tuple-element.125.refs_6_.refs_3_, ...), custom_call_target="tpu_custom_call" | custom-call | flops 10000000000 | bytes 30000000 | tf_op jit(solution)/shard_map/pallas_call | solution.py:537
  165.0 3.1 %collective-permute-done.6 = bf16[256,2688]{1,0:T(8,128)(2,1)} collective-permute-done((bf16[256,2688]{1,0:T(8,128)(2,1)}, bf16[256,2688]{1,0:T(8,128)(2,1)}, u32[]{:S(2)}, u32[]{:S(2)}) %collective-permute-start.6) | collective-permute-done | bytes 1376288 | tf_op jit(solution)/shard_map/ppermute | solution.py:553
  173.1 4.6 %shard_map.252 = (bf16[256,2048]{1,0:T(8,128)(2,1)S(1)}, bf16[256,2048]{1,0:T(8,128)(2,1)S(1)}) custom-call(s32[1]{0:T(128)} %bitcast.15.refs_0_.refs_5_, bf16[512,1024]{1,0:T(8,128)(2,1)S(1)} %copy-done.26, bf16[2048,1024]{1,0:T(8,128)(2,1)S(1)} %copy-done.9, bf16[2048,512]{1,0:T(8,128)(2,1)S(1)} %copy-done.11, ...), custom_call_target="tpu_custom_call" | custom-call | flops 10000000000 | bytes 30000000 | tf_op jit(solution)/shard_map/pallas_call | solution.py:537
  178.1 4.3 %shard_map.253.refs_1_.refs_7_.refs_2_ = bf16[3,128,1024]{2,1,0:T(8,128)(2,1)S(1)} custom-call(bf16[3,256,1024]{2,1,0:T(8,128)(2,1)S(1)} %copy-done.24, bf16[512,1024]{1,0:T(8,128)(2,1)S(1)} %copy-done.20, bf16[512,1024]{1,0:T(8,128)(2,1)S(1)} %copy-done.13, f32[4,8,1024]{2,1,0:T(8,128)S(1)} %get-tuple-element.140.refs_3_, ...), custom_call_target="tpu_custom_call" | custom-call | flops 15000000512 | bytes 45000000 | tf_op jit(solution)/shard_map/pallas_call | solution.py:537
  182.4 5.4 %collective-permute-done.7 = bf16[2,2,2,16,2688]{4,3,2,1,0:T(8,128)(2,1)S(1)} collective-permute-done((bf16[2,2,2,16,2688]{4,3,2,1,0:T(8,128)(2,1)S(1)}, bf16[2,2,2,16,2688]{4,3,2,1,0:T(8,128)(2,1)S(1)}, u32[]{:S(2)}, u32[]{:S(2)}) %collective-permute-start.7) | collective-permute-done | bytes 688160 | tf_op jit(solution)/shard_map/ppermute | solution.py:553
  192.1 6.5 %shard_map.255 = (bf16[3,128,1024]{2,1,0:T(8,128)(2,1)S(1)}, bf16[256,768]{1,0:T(8,128)(2,1)S(1)}, bf16[256,768]{1,0:T(8,128)(2,1)S(1)}) custom-call(bf16[3,256,1024]{2,1,0:T(8,128)(2,1)S(1)} %copy-done.24, bf16[512,1024]{1,0:T(8,128)(2,1)S(1)} %copy-done.20, bf16[512,1024]{1,0:T(8,128)(2,1)S(1)} %copy-done.13, ...), custom_call_target="tpu_custom_call" | custom-call | flops 15000000512 | bytes 45000000 | tf_op jit(solution)/shard_map/pallas_call | solution.py:537
  198.6 4.3 %shard_map.256.refs_7_.refs_4_ = bf16[3,128,1024]{2,1,0:T(8,128)(2,1)S(1)} custom-call(bf16[3,256,1024]{2,1,0:T(8,128)(2,1)S(1)} %copy-done.22, bf16[512,1024]{1,0:T(8,128)(2,1)S(1)} %copy-done.20, bf16[512,1024]{1,0:T(8,128)(2,1)S(1)} %copy-done.13, f32[4,8,1024]{2,1,0:T(8,128)S(1)} %get-tuple-element.155.refs_3_, ...), custom_call_target="tpu_custom_call" | custom-call | flops 15000000512 | bytes 45000000 | tf_op jit(solution)/shard_map/pallas_call | solution.py:537
  205.3 6.5 %shard_map.258 = (bf16[3,128,1024]{2,1,0:T(8,128)(2,1)S(1)}, bf16[256,768]{1,0:T(8,128)(2,1)S(1)}, bf16[256,768]{1,0:T(8,128)(2,1)S(1)}) custom-call(bf16[3,256,1024]{2,1,0:T(8,128)(2,1)S(1)} %copy-done.22, bf16[512,1024]{1,0:T(8,128)(2,1)S(1)} %copy-done.20, bf16[512,1024]{1,0:T(8,128)(2,1)S(1)} %copy-done.13, ...), custom_call_target="tpu_custom_call" | custom-call | flops 15000000512 | bytes 45000000 | tf_op jit(solution)/shard_map/pallas_call | solution.py:537
  214.7 6.1 %collective-permute-done.14 = bf16[2,2,2,16,768]{4,3,1,0,2:T(8,128)(2,1)S(1)} collective-permute-done((bf16[2,2,2,16,768]{4,3,1,0,2:T(8,128)(2,1)S(1)}, bf16[2,2,2,16,768]{4,3,1,0,2:T(8,128)(2,1)S(1)}, u32[]{:S(2)}, u32[]{:S(2)}) %collective-permute-start.14) | collective-permute-done | bytes 196640 | tf_op jit(solution)/shard_map/ppermute | solution.py:553
  224.1 2.6 collective-permute-start.24
  231.4 2.6 collective-permute-start.18
  234.0 6.0 %collective-permute-done.24 = bf16[16,4736]{1,0:T(8,128)(2,1)S(1)} collective-permute-done((bf16[16,4736]{1,0:T(8,128)(2,1)S(1)}, bf16[16,4736]{1,0:T(8,128)(2,1)S(1)}, u32[]{:S(2)}, u32[]{:S(2)}) %collective-permute-start.24) | collective-permute-done | bytes 151584 | tf_op jit(solution)/shard_map/ppermute | solution.py:553
  240.0 3.3 %collective-permute-start.26 = (bf16[16,4736]{1,0:T(8,128)(2,1)S(1)}, bf16[16,4736]{1,0:T(8,128)(2,1)S(1)}, u32[]{:S(2)}, u32[]{:S(2)}) collective-permute-start(bf16[16,4736]{1,0:T(8,128)(2,1)S(1)} %add_convert_fusion.4), channel_id=1, source_target_pairs={{0,8},{2,10},{4,12},{6,14},{8,0},{10,2},{12,4},{14,6},{16,24},{18,... | collective-permute-start | bytes 454664 | tf_op jit(solution)/shard_map/ppermute | solution.py:553
  248.9 4.7 %collective-permute-start.21 = (bf16[16,1536]{1,0:T(8,128)(2,1)S(1)}, bf16[16,1536]{1,0:T(8,128)(2,1)S(1)}, u32[]{:S(2)}, u32[]{:S(2)}) collective-permute-start(bf16[16,1536]{1,0:T(8,128)(2,1)S(1)} %fusion.17), channel_id=1, source_target_pairs={{0,24},{2,26},{4,28},{6,30},{8,16},{10,18},{12,20},{14,22},{16,8},... | collective-permute-start | bytes 147464 | tf_op jit(solution)/shard_map/ppermute | solution.py:553
  253.7 3.9 %collective-permute-done.27 = bf16[16,4736]{1,0:T(8,128)(2,1)S(1)} collective-permute-done((bf16[16,4736]{1,0:T(8,128)(2,1)S(1)}, bf16[16,4736]{1,0:T(8,128)(2,1)S(1)}, u32[]{:S(2)}, u32[]{:S(2)}) %collective-permute-start.27) | collective-permute-done | bytes 151584 | tf_op jit(solution)/shard_map/ppermute | solution.py:553
  260.4 9.6 %collective-permute-done.29 = bf16[2,2,1,16,4736]{4,3,1,2,0:T(8,128)(2,1)S(1)} collective-permute-done((bf16[2,2,1,16,4736]{4,3,1,2,0:T(8,128)(2,1)S(1)}, bf16[2,2,1,16,4736]{4,3,1,2,0:T(8,128)(2,1)S(1)}, u32[]{:S(2)}, u32[]{:S(2)}) %collective-permute-start.29) | collective-permute-done | bytes 606240 | tf_op jit(solution)/shard_map/ppermute | solution.py:553
  271.9 3.3 %shard_map.259 = f32[1024,512]{1,0:T(8,128)} custom-call(bf16[512,1536]{1,0:T(8,128)(2,1)S(1)} %bitcast.127, f32[512,1024]{1,0:T(8,128)S(1)} %copy-done.7, bf16[3,128,1024]{2,1,0:T(8,128)(2,1)S(1)} %shard_map.253.refs_1_.refs_7_.refs_2_, bf16[3,128,1024]{2,1,0:T(8,128)(2,1)S(1)} %get-tuple-element.153.refs_5_.refs_1_.refs_3_, ...), custom_call_target="tpu_custom_call" | custom-call | flops 5000000000 | bytes 15000000 | tf_op jit(solution)/shard_map/pallas_call | solution.py:537
  (211 shorter events, 69.4 us)
Async XLA Ops:
  4.4 12.4 %collective-permute-start = (bf16[1,128,1536]{2,1,0:T(8,128)(2,1)}, bf16[1,128,1536]{2,1,0:T(8,128)(2,1)}, u32[]{:S(2)}, u32[]{:S(2)}) collective-permute-start(bf16[1,128,1536]{2,1,0:T(8,128)(2,1)} %pad_maximum_fusion.3), channel_id=1, source_target_pairs={{0,1},{1,0},{2,3},{3,2},{4,5},{5,4},{6,7},{7,6},{8,9},{9,8},{10,11... | collective-permute-start | bytes 1179656 | tf_op jit(solution)/shard_map/ppermute | solution.py:553
  18.0 2.4 collective-permute-start.1
  18.6 17.9 %collective-permute-start.2 = (bf16[1,128,2688]{2,1,0:T(8,128)(2,1)S(1)}, bf16[1,128,2688]{2,1,0:T(8,128)(2,1)S(1)}, u32[]{:S(2)}, u32[]{:S(2)}) collective-permute-start(bf16[1,128,2688]{2,1,0:T(8,128)(2,1)S(1)} %pad_maximum_fusion), channel_id=1, source_target_pairs={{0,1},{1,0},{2,3},{3,2},{4,5},{5,4},{6,7},{7,6},{8,9},{9,8},{10,11... | collective-permute-start | bytes 2064392 | tf_op jit(solution)/shard_map/ppermute | solution.py:553
  36.8 14.8 %collective-permute-start.3 = (bf16[2,128,2688]{2,1,0:T(8,128)(2,1)S(1)}, bf16[2,128,2688]{2,1,0:T(8,128)(2,1)S(1)}, u32[]{:S(2)}, u32[]{:S(2)}) collective-permute-start(bf16[2,128,2688]{2,1,0:T(8,128)(2,1)S(1)} %maximum_select_fusion.3), channel_id=1, source_target_pairs={{0,2},{2,0},{4,6},{6,4},{8,10},{10,8},{12,14},{14,12},{16,18},{18,... | collective-permute-start | bytes 4128776 | tf_op jit(solution)/shard_map/ppermute | solution.py:553
  36.9 14.4 %collective-permute-start.4 = (bf16[1,128,2048]{2,1,0:T(8,128)(2,1)S(1)}, bf16[1,128,2048]{2,1,0:T(8,128)(2,1)S(1)}, u32[]{:S(2)}, u32[]{:S(2)}) collective-permute-start(bf16[1,128,2048]{2,1,0:T(8,128)(2,1)S(1)} %pad_maximum_fusion.2), channel_id=1, source_target_pairs={{0,1},{1,0},{2,3},{3,2},{4,5},{5,4},{6,7},{7,6},{8,9},{9,8},{10,11... | collective-permute-start | bytes 1572872 | tf_op jit(solution)/shard_map/ppermute | solution.py:553
  51.5 10.1 %collective-permute-start.5 = (bf16[2,128,2048]{2,1,0:T(8,128)(2,1)S(1)}, bf16[2,128,2048]{2,1,0:T(8,128)(2,1)S(1)}, u32[]{:S(2)}, u32[]{:S(2)}) collective-permute-start(bf16[2,128,2048]{2,1,0:T(8,128)(2,1)S(1)} %maximum_select_fusion.5), channel_id=1, source_target_pairs={{0,2},{2,0},{4,6},{6,4},{8,10},{10,8},{12,14},{14,12},{16,18},{18,... | collective-permute-start | bytes 3145736 | tf_op jit(solution)/shard_map/ppermute | solution.py:553
  164.6 3.6 %collective-permute-start.6 = (bf16[256,2688]{1,0:T(8,128)(2,1)}, bf16[256,2688]{1,0:T(8,128)(2,1)}, u32[]{:S(2)}, u32[]{:S(2)}) collective-permute-start(bf16[256,2688]{1,0:T(8,128)(2,1)} %get-tuple-element.149), channel_id=1, source_target_pairs={{0,2},{2,0},{4,6},{6,4},{8,10},{10,8},{12,14},{14,12},{16,18},{18,... | collective-permute-start | bytes 4128776 | tf_op jit(solution)/shard_map/ppermute | solution.py:553
  170.1 17.8 %collective-permute-start.7 = (bf16[2,2,2,16,2688]{4,3,2,1,0:T(8,128)(2,1)S(1)}, bf16[2,2,2,16,2688]{4,3,2,1,0:T(8,128)(2,1)S(1)}, u32[]{:S(2)}, u32[]{:S(2)}) collective-permute-start(bf16[2,2,2,16,2688]{4,3,2,1,0:T(8,128)(2,1)S(1)} %get-tuple-element.167.refs_4_), channel_id=1, source_target_pairs={{0,1},{1,0},{2,3},{3,2},{4,5},{5,4},{6,7},{7,6},{8,9},{9,8},{10,11... | collective-permute-start | bytes 2064392 | tf_op jit(solution)/shard_map/ppermute | solution.py:553
  177.7 12.2 %collective-permute-start.8 = (bf16[256,2048]{1,0:T(8,128)(2,1)S(1)}, bf16[256,2048]{1,0:T(8,128)(2,1)S(1)}, u32[]{:S(2)}, u32[]{:S(2)}) collective-permute-start(bf16[256,2048]{1,0:T(8,128)(2,1)S(1)} %get-tuple-element.150.refs_5_), channel_id=1, source_target_pairs={{0,2},{2,0},{4,6},{6,4},{8,10},{10,8},{12,14},{14,12},{16,18},{18,... | collective-permute-start | bytes 3145736 | tf_op jit(solution)/shard_map/ppermute | solution.py:553
  188.1 14.9 %collective-permute-start.11 = (bf16[2,2,16,2688]{3,2,1,0:T(8,128)(2,1)S(1)}, bf16[2,2,16,2688]{3,2,1,0:T(8,128)(2,1)S(1)}, u32[]{:S(2)}, u32[]{:S(2)}) collective-permute-start(bf16[2,2,16,2688]{3,2,1,0:T(8,128)(2,1)S(1)} %get-tuple-element.185.refs_9_), channel_id=1, source_target_pairs={{0,4},{2,6},{4,0},{6,2},{8,12},{10,14},{12,8},{14,10},{16,20},{18,... | collective-permute-start | bytes 1032200 | tf_op jit(solution)/shard_map/ppermute | solution.py:553
  190.5 14.0 %collective-permute-start.9 = (bf16[2,2,2,16,2048]{4,3,1,0,2:T(8,128)(2,1)S(1)}, bf16[2,2,2,16,2048]{4,3,1,0,2:T(8,128)(2,1)S(1)}, u32[]{:S(2)}, u32[]{:S(2)}) collective-permute-start(bf16[2,2,2,16,2048]{4,3,1,0,2:T(8,128)(2,1)S(1)} %bitcast.146), channel_id=1, source_target_pairs={{0,1},{1,0},{2,3},{3,2},{4,5},{5,4},{6,7},{7,6},{8,9},{9,8},{10,11... | collective-permute-start | bytes 1572872 | tf_op jit(solution)/shard_map/ppermute | solution.py:553
  198.6 4.5 %collective-permute-start.10 = (bf16[256,768]{1,0:T(8,128)(2,1)S(1)}, bf16[256,768]{1,0:T(8,128)(2,1)S(1)}, u32[]{:S(2)}, u32[]{:S(2)}) collective-permute-start(bf16[256,768]{1,0:T(8,128)(2,1)S(1)} %get-tuple-element.158), channel_id=1, source_target_pairs={{0,2},{2,0},{4,6},{6,4},{8,10},{10,8},{12,14},{14,12},{16,18},{18,... | collective-permute-start | bytes 1179656 | tf_op jit(solution)/shard_map/ppermute | solution.py:553
  203.3 8.6 %collective-permute-start.12 = (bf16[2,2,2,16,768]{4,3,1,0,2:T(8,128)(2,1)S(1)}, bf16[2,2,2,16,768]{4,3,1,0,2:T(8,128)(2,1)S(1)}, u32[]{:S(2)}, u32[]{:S(2)}) collective-permute-start(bf16[2,2,2,16,768]{4,3,1,0,2:T(8,128)(2,1)S(1)} %bitcast.147), channel_id=1, source_target_pairs={{0,1},{1,0},{2,3},{3,2},{4,5},{5,4},{6,7},{7,6},{8,9},{9,8},{10,11... | collective-permute-start | bytes 589832 | tf_op jit(solution)/shard_map/ppermute | solution.py:553
  204.7 8.5 %collective-permute-start.22 = (bf16[2,2,16,2048]{3,2,1,0:T(8,128)(2,1)S(1)}, bf16[2,2,16,2048]{3,2,1,0:T(8,128)(2,1)S(1)}, u32[]{:S(2)}, u32[]{:S(2)}) collective-permute-start(bf16[2,2,16,2048]{3,2,1,0:T(8,128)(2,1)S(1)} %dynamic-slice_bitcast_fusion.3.refs_9_), channel_id=1, source_target_pairs={{0,4},{2,6},{4,0},{6,2},{8,12},{10,14},{12,8},{14,10},{16,20},{18,... | collective-permute-start | bytes 786440 | tf_op jit(solution)/shard_map/ppermute | solution.py:553
  213.8 7.0 %collective-permute-start.14 = (bf16[2,2,2,16,768]{4,3,1,0,2:T(8,128)(2,1)S(1)}, bf16[2,2,2,16,768]{4,3,1,0,2:T(8,128)(2,1)S(1)}, u32[]{:S(2)}, u32[]{:S(2)}) collective-permute-start(bf16[2,2,2,16,768]{4,3,1,0,2:T(8,128)(2,1)S(1)} %bitcast.148), channel_id=1, source_target_pairs={{0,1},{1,0},{2,3},{3,2},{4,5},{5,4},{6,7},{7,6},{8,9},{9,8},{10,11... | collective-permute-start | bytes 589832 | tf_op jit(solution)/shard_map/ppermute | solution.py:553
  220.8 6.2 %collective-permute-start.15 = (bf16[2,2,16,1536]{3,2,1,0:T(8,128)(2,1)S(1)}, bf16[2,2,16,1536]{3,2,1,0:T(8,128)(2,1)S(1)}, u32[]{:S(2)}, u32[]{:S(2)}) collective-permute-start(bf16[2,2,16,1536]{3,2,1,0:T(8,128)(2,1)S(1)} %fusion.14.refs_6_), channel_id=1, source_target_pairs={{0,4},{2,6},{4,0},{6,2},{8,12},{10,14},{12,8},{14,10},{16,20},{18,... | collective-permute-start | bytes 589832 | tf_op jit(solution)/shard_map/ppermute | solution.py:553
  222.5 8.9 %collective-permute-start.23 = (bf16[16,4736]{1,0:T(8,128)(2,1)S(1)}, bf16[16,4736]{1,0:T(8,128)(2,1)S(1)}, u32[]{:S(2)}, u32[]{:S(2)}) collective-permute-start(bf16[16,4736]{1,0:T(8,128)(2,1)S(1)} %get-tuple-element.189), channel_id=1, source_target_pairs={{0,8},{2,10},{4,12},{6,14},{8,0},{10,2},{12,4},{14,6},{16,24},{18,... | collective-permute-start | bytes 454664 | tf_op jit(solution)/shard_map/ppermute | solution.py:553
  224.1 15.8 %collective-permute-start.24 = (bf16[16,4736]{1,0:T(8,128)(2,1)S(1)}, bf16[16,4736]{1,0:T(8,128)(2,1)S(1)}, u32[]{:S(2)}, u32[]{:S(2)}) collective-permute-start(bf16[16,4736]{1,0:T(8,128)(2,1)S(1)} %get-tuple-element.188), channel_id=1, source_target_pairs={{0,16},{2,18},{4,20},{6,22},{8,24},{10,26},{12,28},{14,30},{16,0},... | collective-permute-start | bytes 454664 | tf_op jit(solution)/shard_map/ppermute | solution.py:553
  226.7 13.2 %collective-permute-start.25 = (bf16[16,4736]{1,0:T(8,128)(2,1)S(1)}, bf16[16,4736]{1,0:T(8,128)(2,1)S(1)}, u32[]{:S(2)}, u32[]{:S(2)}) collective-permute-start(bf16[16,4736]{1,0:T(8,128)(2,1)S(1)} %get-tuple-element.187), channel_id=1, source_target_pairs={{0,24},{2,26},{4,28},{6,30},{8,16},{10,18},{12,20},{14,22},{16,8},... | collective-permute-start | bytes 454664 | tf_op jit(solution)/shard_map/ppermute | solution.py:553
  227.1 17.3 %collective-permute-start.16 = (bf16[16,1536]{1,0:T(8,128)(2,1)S(1)}, bf16[16,1536]{1,0:T(8,128)(2,1)S(1)}, u32[]{:S(2)}, u32[]{:S(2)}) collective-permute-start(bf16[16,1536]{1,0:T(8,128)(2,1)S(1)} %get-tuple-element.206), channel_id=1, source_target_pairs={{0,8},{2,10},{4,12},{6,14},{8,0},{10,2},{12,4},{14,6},{16,24},{18,... | collective-permute-start | bytes 147464 | tf_op jit(solution)/shard_map/ppermute | solution.py:553
  228.8 17.0 %collective-permute-start.17 = (bf16[16,1536]{1,0:T(8,128)(2,1)S(1)}, bf16[16,1536]{1,0:T(8,128)(2,1)S(1)}, u32[]{:S(2)}, u32[]{:S(2)}) collective-permute-start(bf16[16,1536]{1,0:T(8,128)(2,1)S(1)} %get-tuple-element.208), channel_id=1, source_target_pairs={{0,16},{2,18},{4,20},{6,22},{8,24},{10,26},{12,28},{14,30},{16,0},... | collective-permute-start | bytes 147464 | tf_op jit(solution)/shard_map/ppermute | solution.py:553
  231.4 14.4 %collective-permute-start.18 = (bf16[16,1536]{1,0:T(8,128)(2,1)S(1)}, bf16[16,1536]{1,0:T(8,128)(2,1)S(1)}, u32[]{:S(2)}, u32[]{:S(2)}) collective-permute-start(bf16[16,1536]{1,0:T(8,128)(2,1)S(1)} %get-tuple-element.207), channel_id=1, source_target_pairs={{0,24},{2,26},{4,28},{6,30},{8,16},{10,18},{12,20},{14,22},{16,8},... | collective-permute-start | bytes 147464 | tf_op jit(solution)/shard_map/ppermute | solution.py:553
  240.0 8.9 %collective-permute-start.26 = (bf16[16,4736]{1,0:T(8,128)(2,1)S(1)}, bf16[16,4736]{1,0:T(8,128)(2,1)S(1)}, u32[]{:S(2)}, u32[]{:S(2)}) collective-permute-start(bf16[16,4736]{1,0:T(8,128)(2,1)S(1)} %add_convert_fusion.4), channel_id=1, source_target_pairs={{0,8},{2,10},{4,12},{6,14},{8,0},{10,2},{12,4},{14,6},{16,24},{18,... | collective-permute-start | bytes 454664 | tf_op jit(solution)/shard_map/ppermute | solution.py:553
  243.3 14.3 %collective-permute-start.27 = (bf16[16,4736]{1,0:T(8,128)(2,1)S(1)}, bf16[16,4736]{1,0:T(8,128)(2,1)S(1)}, u32[]{:S(2)}, u32[]{:S(2)}) collective-permute-start(bf16[16,4736]{1,0:T(8,128)(2,1)S(1)} %add_convert_fusion.4), channel_id=1, source_target_pairs={{0,16},{2,18},{4,20},{6,22},{8,24},{10,26},{12,28},{14,30},{16,0},... | collective-permute-start | bytes 454664 | tf_op jit(solution)/shard_map/ppermute | solution.py:553
  244.4 13.2 %collective-permute-start.28 = (bf16[16,4736]{1,0:T(8,128)(2,1)S(1)}, bf16[16,4736]{1,0:T(8,128)(2,1)S(1)}, u32[]{:S(2)}, u32[]{:S(2)}) collective-permute-start(bf16[16,4736]{1,0:T(8,128)(2,1)S(1)} %add_convert_fusion.4), channel_id=1, source_target_pairs={{0,24},{2,26},{4,28},{6,30},{8,16},{10,18},{12,20},{14,22},{16,8},... | collective-permute-start | bytes 454664 | tf_op jit(solution)/shard_map/ppermute | solution.py:553
  245.8 12.5 %collective-permute-start.19 = (bf16[16,1536]{1,0:T(8,128)(2,1)S(1)}, bf16[16,1536]{1,0:T(8,128)(2,1)S(1)}, u32[]{:S(2)}, u32[]{:S(2)}) collective-permute-start(bf16[16,1536]{1,0:T(8,128)(2,1)S(1)} %fusion.17), channel_id=1, source_target_pairs={{0,8},{2,10},{4,12},{6,14},{8,0},{10,2},{12,4},{14,6},{16,24},{18,... | collective-permute-start | bytes 147464 | tf_op jit(solution)/shard_map/ppermute | solution.py:553
  246.9 13.4 %collective-permute-start.20 = (bf16[16,1536]{1,0:T(8,128)(2,1)S(1)}, bf16[16,1536]{1,0:T(8,128)(2,1)S(1)}, u32[]{:S(2)}, u32[]{:S(2)}) collective-permute-start(bf16[16,1536]{1,0:T(8,128)(2,1)S(1)} %fusion.17), channel_id=1, source_target_pairs={{0,16},{2,18},{4,20},{6,22},{8,24},{10,26},{12,28},{14,30},{16,0},... | collective-permute-start | bytes 147464 | tf_op jit(solution)/shard_map/ppermute | solution.py:553
  248.9 11.4 %collective-permute-start.21 = (bf16[16,1536]{1,0:T(8,128)(2,1)S(1)}, bf16[16,1536]{1,0:T(8,128)(2,1)S(1)}, u32[]{:S(2)}, u32[]{:S(2)}) collective-permute-start(bf16[16,1536]{1,0:T(8,128)(2,1)S(1)} %fusion.17), channel_id=1, source_target_pairs={{0,24},{2,26},{4,28},{6,30},{8,16},{10,18},{12,20},{14,22},{16,8},... | collective-permute-start | bytes 147464 | tf_op jit(solution)/shard_map/ppermute | solution.py:553
  257.8 12.2 %collective-permute-start.29 = (bf16[2,2,1,16,4736]{4,3,1,2,0:T(8,128)(2,1)S(1)}, bf16[2,2,1,16,4736]{4,3,1,2,0:T(8,128)(2,1)S(1)}, u32[]{:S(2)}, u32[]{:S(2)}) collective-permute-start(bf16[2,2,1,16,4736]{4,3,1,2,0:T(8,128)(2,1)S(1)} %maximum_select_fusion.8), channel_id=1, source_target_pairs={{0,4},{2,6},{4,0},{6,2},{8,12},{10,14},{12,8},{14,10},{16,20},{18,... | collective-permute-start | bytes 1818632 | tf_op jit(solution)/shard_map/ppermute | solution.py:553
  270.3 5.7 %collective-permute-start.30 = (bf16[2,2,1,16,1536]{4,3,1,0,2:T(8,128)(2,1)S(1)}, bf16[2,2,1,16,1536]{4,3,1,0,2:T(8,128)(2,1)S(1)}, u32[]{:S(2)}, u32[]{:S(2)}) collective-permute-start(bf16[2,2,1,16,1536]{4,3,1,0,2:T(8,128)(2,1)S(1)} %bitcast.136), channel_id=1, source_target_pairs={{0,4},{2,6},{4,0},{6,2},{8,12},{10,14},{12,8},{14,10},{16,20},{18,... | collective-permute-start | bytes 589832 | tf_op jit(solution)/shard_map/ppermute | solution.py:553
  275.2 6.3 %collective-permute-start.32 = (bf16[128,4736]{1,0:T(8,128)(2,1)S(1)}, bf16[128,4736]{1,0:T(8,128)(2,1)S(1)}, u32[]{:S(2)}, u32[]{:S(2)}) collective-permute-start(bf16[128,4736]{1,0:T(8,128)(2,1)S(1)} %bitcast.114), channel_id=1, source_target_pairs={{0,2},{2,0},{4,6},{6,4},{8,10},{10,8},{12,14},{14,12},{16,18},{18,... | collective-permute-start | bytes 3637256 | tf_op jit(solution)/shard_map/ppermute | solution.py:553
  276.2 2.5 collective-permute-start.31
  (33 other events, 205.8 us)

commit v5 on v4

--- a/solution.py
+++ b/solution.py
@@ -859,8 +859,6 @@
         second.halve(*label)
     heads = join(first, second)
     heads.halve(*y_bit)
-    heads.settle()
-    feed.keep = copy_after(feed.keep, heads.value)
     feed.settle()
     feed.collect()
     (input_grad,) = call(

time: 291 us -> 284 us (0.976)
  starting transfers between devices: 43.3 us -> 39.3 us
    ppermute x33, starting transfers between devices: 43.3 us -> 39.3 us  [flip(): return lax.ppermute(value, axis, [(i, i ^ bit) for i in range(count)])]
    pallas_call x24 -> x23, Pallas kernels: 155 us -> 155 us  [call(): pl.pallas_call(run, out_shape=[jax.ShapeDtypeStruct(shape, dtype) for sha...]
  transfers between devices with their start and end apart: 33 -> 33, of which waited for: 15 -> 18; matrix products, arithmetic and copies ran while one was open for 4% -> 4% of each run, Pallas kernels for 19% -> 20%
where the time goes in v5:
time: 284 us; the launch traced here: 282 us
  Pallas kernels  155 us (55%)
  waiting for transfers between devices  53.1 us (19%)
  starting transfers between devices  39.3 us (14%)
  other arithmetic  16.7 us (6%)
  local copies, waits for them, and re-layouts  15.4 us (5%)
  between operations  3.13 us (1%)
    pallas_call x23, Pallas kernels, call(): pl.pallas_call(run, out_shape=[jax.ShapeDtypeStruct(shape, dtype) for sha...  155 us
    ppermute x33, waiting for transfers between devices, flip(): return lax.ppermute(value, axis, [(i, i ^ bit) for i in range(count)])  53.1 us
    ppermute x33, starting transfers between devices, flip(): return lax.ppermute(value, axis, [(i, i ^ bit) for i in range(count)])  39.3 us
    unnamed x64, local copies, waits for them, and re-layouts  6.96 us
  transfers between devices with their start and end apart: 33, of which 18 were waited for; matrix products, arithmetic and copies ran while one was open for 4% of the time, Pallas kernels for 20%

profile of v5, /device:TPU:0, one launch (start us, length us, event | category | flops | bytes accessed | tf_op | source)
XLA Modules:
  0.0 282.4 jit_solution(2260854365918587211)
XLA Ops:
  4.4 2.9 %collective-permute-start = (bf16[1,128,1536]{2,1,0:T(8,128)(2,1)}, bf16[1,128,1536]{2,1,0:T(8,128)(2,1)}, u32[]{:S(2)}, u32[]{:S(2)}) collective-permute-start(bf16[1,128,1536]{2,1,0:T(8,128)(2,1)} %pad_maximum_fusion.3), channel_id=1, source_target_pairs={{0,1},{1,0},{2,3},{3,2},{4,5},{5,4},{6,7},{7,6},{8,9},{9,8},{10,11... | collective-permute-start | bytes 1179656 | tf_op jit(solution)/shard_map/ppermute | solution.py:553
  13.2 3.5 %collective-permute-done = bf16[1,128,1536]{2,1,0:T(8,128)(2,1)} collective-permute-done((bf16[1,128,1536]{2,1,0:T(8,128)(2,1)}, bf16[1,128,1536]{2,1,0:T(8,128)(2,1)}, u32[]{:S(2)}, u32[]{:S(2)}) %collective-permute-start) | collective-permute-done | bytes 393248 | tf_op jit(solution)/shard_map/ppermute | solution.py:553
  21.1 8.7 %shard_map.239 = (bf16[768,512]{1,0:T(8,128)(2,1)S(1)}, bf16[3,256,1024]{2,1,0:T(8,128)(2,1)S(1)}, bf16[256,1024]{1,0:T(8,128)(2,1)S(1)}, f32[4,8,1024]{2,1,0:T(8,128)S(1)}) custom-call(bf16[512,1024]{1,0:T(8,128)(2,1)S(1)} %shard_map.238.refs_0_.refs_2_.refs_6_, bf16[512,1536]{1,0:T(8,128)(2,1)S(1)} %bitcast.125, f32[8,1024]{1,0:T(8,128)S(1)} %broadcast_in_dim.27.refs_2_.refs_4_), custom_call_target="tpu_custom_call" | custom-call | flops 10000000000 | bytes 30000000 | tf_op jit(solution)/shard_map/pallas_call | solution.py:537
  31.0 5.6 %collective-permute-done.2 = bf16[1,128,2688]{2,1,0:T(8,128)(2,1)S(1)} collective-permute-done((bf16[1,128,2688]{2,1,0:T(8,128)(2,1)S(1)}, bf16[1,128,2688]{2,1,0:T(8,128)(2,1)S(1)}, u32[]{:S(2)}, u32[]{:S(2)}) %collective-permute-start.2) | collective-permute-done | bytes 688160 | tf_op jit(solution)/shard_map/ppermute | solution.py:553
  38.7 8.7 %shard_map.240 = (bf16[768,512]{1,0:T(8,128)(2,1)S(1)}, bf16[3,256,1024]{2,1,0:T(8,128)(2,1)S(1)}, bf16[256,1024]{1,0:T(8,128)(2,1)S(1)}, f32[4,8,1024]{2,1,0:T(8,128)S(1)}) custom-call(bf16[512,1024]{1,0:T(8,128)(2,1)S(1)} %shard_map.238.refs_0_.refs_2_.refs_6_, bf16[512,1536]{1,0:T(8,128)(2,1)S(1)} %bitcast.126, f32[8,1024]{1,0:T(8,128)S(1)} %broadcast_in_dim.27.refs_2_.refs_4_), custom_call_target="tpu_custom_call" | custom-call | flops 10000000000 | bytes 30000000 | tf_op jit(solution)/shard_map/pallas_call | solution.py:537
  48.6 2.7 collective-permute-done.4
  52.6 8.0 %shard_map.241 = (bf16[512,1024]{1,0:T(8,128)(2,1)S(1)}, bf16[512,512]{1,0:T(8,128)(2,1)S(1)}, bf16[2048,512]{1,0:T(8,128)(2,1)S(1)}, f32[512,1024]{1,0:T(8,128)...) custom-call(bf16[256,1024]{1,0:T(8,128)(2,1)S(1)} %get-tuple-element, ...), custom_call_target="tpu_custom_call" | custom-call | flops 10000000000 | bytes 30000000 | tf_op jit(solution)/shard_map/pallas_call | solution.py:537
  62.6 3.4 %shard_map.242 = (bf16[2048,512]{1,0:T(8,128)(2,1)S(1)}, bf16[512,2048]{1,0:T(8,128)(2,1)S(1)}, f32[512,1024]{1,0:T(8,128)S(1)}, bf16[512,1024]{1,0:T(8,128)(2,1...) custom-call(f32[512,1024]{1,0:T(8,128)S(1)} %get-tuple-element.101.refs_0_, ...), custom_call_target="tpu_custom_call" | custom-call | flops 10000000000 | bytes 30000000 | tf_op jit(solution)/shard_map/pallas_call | solution.py:537
  66.0 21.6 %shard_map.244 = (bf16[3,256,1024]{2,1,0:T(8,128)(2,1)S(1)}, bf16[256,1024]{1,0:T(8,128)(2,1)S(1)}, f32[4,8,1024]{2,1,0:T(8,128)S(1)}) custom-call(bf16[512,1024]{1,0:T(8,128)(2,1)S(1)} %get-tuple-element.104.refs_0_.refs_5_, bf16[768,512]{1,0:T(8,128)(2,1)S(1)} %get-tuple-element.107.refs_1_, f32[8,1024]{1,0:T(8,128)S(1)} %broadcast_in_dim.27.refs_2_.refs_4_), custom_call_target="tpu_custom_call" | custom-call | flops 10000000000 | bytes 30000000 | tf_op jit(solution)/shard_map/pallas_call | solution.py:537
  87.6 8.8 %shard_map.243 = (bf16[3,256,1024]{2,1,0:T(8,128)(2,1)S(1)}, bf16[256,1024]{1,0:T(8,128)(2,1)S(1)}, f32[4,8,1024]{2,1,0:T(8,128)S(1)}) custom-call(bf16[512,1024]{1,0:T(8,128)(2,1)S(1)} %get-tuple-element.104.refs_0_.refs_5_, bf16[768,512]{1,0:T(8,128)(2,1)S(1)} %get-tuple-element.105.refs_1_, f32[8,1024]{1,0:T(8,128)S(1)} %broadcast_in_dim.27.refs_2_.refs_4_), custom_call_target="tpu_custom_call" | custom-call | flops 10000000000 | bytes 30000000 | tf_op jit(solution)/shard_map/pallas_call | solution.py:537
  96.4 22.5 %shard_map.245 = (bf16[512,1024]{1,0:T(8,128)(2,1)S(1)}, bf16[1024,512]{1,0:T(8,128)(2,1)}, bf16[2048,1024]{1,0:T(8,128)(2,1)S(1)}, bf16[2048,1024]{1,0:T(8,128)...) custom-call(bf16[256,1024]{1,0:T(8,128)(2,1)S(1)} %get-tuple-element, ...), custom_call_target="tpu_custom_call" | custom-call | flops 10000000000 | bytes 30000000 | tf_op jit(solution)/shard_map/pallas_call | solution.py:537
  119.0 5.1 %shard_map.246 = (bf16[2048,512]{1,0:T(8,128)(2,1)S(1)}, bf16[2048,512]{1,0:T(8,128)(2,1)S(1)}, bf16[512,512]{1,0:T(8,128)(2,1)S(1)}) custom-call(bf16[2048,1024]{1,0:T(8,128)(2,1)S(1)} %get-tuple-element.120.refs_0_, bf16[512,1024]{1,0:T(8,128)(2,1)S(1)} %get-tuple-element.121.refs_1_, bf16[2048,1024]{1,0:T(8,128)(2,1)S(1)} %get-tuple-element.122.refs_2_, ...), custom_call_target="tpu_custom_call" | custom-call | flops 10000000000 | bytes 30000000 | tf_op jit(solution)/shard_map/pallas_call | solution.py:537
  125.4 9.9 %shard_map.248 = (bf16[3,256,1024]{2,1,0:T(8,128)(2,1)S(1)}, bf16[512,768]{1,0:T(8,128)(2,1)S(1)}) custom-call(bf16[3,256,1024]{2,1,0:T(8,128)(2,1)S(1)} %copy-done.15, bf16[512,1024]{1,0:T(8,128)(2,1)S(1)} %get-tuple-element.117.refs_4_.refs_1_, bf16[512,1024]{1,0:T(8,128)(2,1)S(1)} %get-tuple-element.118.refs_2_, ...), custom_call_target="tpu_custom_call" | custom-call | flops 10000000000 | bytes 30000000 | tf_op jit(solution)/shard_map/pallas_call | solution.py:537
  135.2 9.9 %shard_map.247 = (bf16[3,256,1024]{2,1,0:T(8,128)(2,1)S(1)}, bf16[512,768]{1,0:T(8,128)(2,1)S(1)}) custom-call(bf16[3,256,1024]{2,1,0:T(8,128)(2,1)S(1)} %get-tuple-element.116.refs_0_, bf16[512,1024]{1,0:T(8,128)(2,1)S(1)} %get-tuple-element.117.refs_4_.refs_1_, bf16[512,1024]{1,0:T(8,128)(2,1)S(1)} %get-tuple-element.118.refs_2_, ...), custom_call_target="tpu_custom_call" | custom-call | flops 10000000000 | bytes 30000000 | tf_op jit(solution)/shard_map/pallas_call | solution.py:537
  147.0 9.7 %shard_map.250 = (f32[512,1024]{1,0:T(8,128)S(1)}, bf16[512,1024]{1,0:T(8,128)(2,1)S(1)}, bf16[2048,1024]{1,0:T(8,128)(2,1)S(1)}, bf16[512,1024]{1,0:T(8,128)(2,...) custom-call(f32[512,1024]{1,0:T(8,128)S(1)} %shard_map.249.refs_0_, ...), custom_call_target="tpu_custom_call", output_to_operand_aliasing={{2}: (5, {}), {5}: (8, {})} | custom-call | flops 10000000000 | bytes 30000000 | tf_op jit(solution)/shard_map/pallas_call | solution.py:537
  157.7 6.9 %shard_map.251 = (bf16[256,2688]{1,0:T(8,128)(2,1)S(1)}, bf16[256,2688]{1,0:T(8,128)(2,1)}) custom-call(s32[1]{0:T(128)} %bitcast.15.refs_0_.refs_5_, bf16[2048,1024]{1,0:T(8,128)(2,1)S(1)} %get-tuple-element.102.refs_1_, bf16[512,1024]{1,0:T(8,128)(2,1)S(1)} %get-tuple-element.144.refs_2_, bf16[2048,512]{1,0:T(8,128)(2,1)S(1)} %get-tuple-element.125.refs_6_.refs_3_, ...), custom_call_target="tpu_custom_call" | custom-call | flops 10000000000 | bytes 30000000 | tf_op jit(solution)/shard_map/pallas_call | solution.py:537
  165.0 3.1 %collective-permute-done.6 = bf16[256,2688]{1,0:T(8,128)(2,1)} collective-permute-done((bf16[256,2688]{1,0:T(8,128)(2,1)}, bf16[256,2688]{1,0:T(8,128)(2,1)}, u32[]{:S(2)}, u32[]{:S(2)}) %collective-permute-start.6) | collective-permute-done | bytes 1376288 | tf_op jit(solution)/shard_map/ppermute | solution.py:553
  173.1 4.6 %shard_map.252 = (bf16[256,2048]{1,0:T(8,128)(2,1)S(1)}, bf16[256,2048]{1,0:T(8,128)(2,1)S(1)}) custom-call(s32[1]{0:T(128)} %bitcast.15.refs_0_.refs_5_, bf16[512,1024]{1,0:T(8,128)(2,1)S(1)} %copy-done.26, bf16[2048,1024]{1,0:T(8,128)(2,1)S(1)} %copy-done.9, bf16[2048,512]{1,0:T(8,128)(2,1)S(1)} %copy-done.11, ...), custom_call_target="tpu_custom_call" | custom-call | flops 10000000000 | bytes 30000000 | tf_op jit(solution)/shard_map/pallas_call | solution.py:537
  178.0 4.3 %shard_map.253.refs_1_.refs_7_.refs_2_ = bf16[3,128,1024]{2,1,0:T(8,128)(2,1)S(1)} custom-call(bf16[3,256,1024]{2,1,0:T(8,128)(2,1)S(1)} %copy-done.24, bf16[512,1024]{1,0:T(8,128)(2,1)S(1)} %copy-done.20, bf16[512,1024]{1,0:T(8,128)(2,1)S(1)} %copy-done.13, f32[4,8,1024]{2,1,0:T(8,128)S(1)} %get-tuple-element.140.refs_3_, ...), custom_call_target="tpu_custom_call" | custom-call | flops 15000000512 | bytes 45000000 | tf_op jit(solution)/shard_map/pallas_call | solution.py:537
  182.4 5.5 %collective-permute-done.7 = bf16[2,2,2,16,2688]{4,3,2,1,0:T(8,128)(2,1)S(1)} collective-permute-done((bf16[2,2,2,16,2688]{4,3,2,1,0:T(8,128)(2,1)S(1)}, bf16[2,2,2,16,2688]{4,3,2,1,0:T(8,128)(2,1)S(1)}, u32[]{:S(2)}, u32[]{:S(2)}) %collective-permute-start.7) | collective-permute-done | bytes 688160 | tf_op jit(solution)/shard_map/ppermute | solution.py:553
  192.0 6.5 %shard_map.255 = (bf16[3,128,1024]{2,1,0:T(8,128)(2,1)S(1)}, bf16[256,768]{1,0:T(8,128)(2,1)S(1)}, bf16[256,768]{1,0:T(8,128)(2,1)S(1)}) custom-call(bf16[3,256,1024]{2,1,0:T(8,128)(2,1)S(1)} %copy-done.24, bf16[512,1024]{1,0:T(8,128)(2,1)S(1)} %copy-done.20, bf16[512,1024]{1,0:T(8,128)(2,1)S(1)} %copy-done.13, ...), custom_call_target="tpu_custom_call" | custom-call | flops 15000000512 | bytes 45000000 | tf_op jit(solution)/shard_map/pallas_call | solution.py:537
  198.6 4.3 %shard_map.256.refs_7_.refs_4_ = bf16[3,128,1024]{2,1,0:T(8,128)(2,1)S(1)} custom-call(bf16[3,256,1024]{2,1,0:T(8,128)(2,1)S(1)} %copy-done.22, bf16[512,1024]{1,0:T(8,128)(2,1)S(1)} %copy-done.20, bf16[512,1024]{1,0:T(8,128)(2,1)S(1)} %copy-done.13, f32[4,8,1024]{2,1,0:T(8,128)S(1)} %get-tuple-element.155.refs_3_, ...), custom_call_target="tpu_custom_call" | custom-call | flops 15000000512 | bytes 45000000 | tf_op jit(solution)/shard_map/pallas_call | solution.py:537
  205.3 6.5 %shard_map.258 = (bf16[3,128,1024]{2,1,0:T(8,128)(2,1)S(1)}, bf16[256,768]{1,0:T(8,128)(2,1)S(1)}, bf16[256,768]{1,0:T(8,128)(2,1)S(1)}) custom-call(bf16[3,256,1024]{2,1,0:T(8,128)(2,1)S(1)} %copy-done.22, bf16[512,1024]{1,0:T(8,128)(2,1)S(1)} %copy-done.20, bf16[512,1024]{1,0:T(8,128)(2,1)S(1)} %copy-done.13, ...), custom_call_target="tpu_custom_call" | custom-call | flops 15000000512 | bytes 45000000 | tf_op jit(solution)/shard_map/pallas_call | solution.py:537
  215.0 2.6 collective-permute-start.24
  220.5 8.5 %collective-permute-done.24 = bf16[16,4736]{1,0:T(8,128)(2,1)S(1)} collective-permute-done((bf16[16,4736]{1,0:T(8,128)(2,1)S(1)}, bf16[16,4736]{1,0:T(8,128)(2,1)S(1)}, u32[]{:S(2)}, u32[]{:S(2)}) %collective-permute-start.24) | collective-permute-done | bytes 151584 | tf_op jit(solution)/shard_map/ppermute | solution.py:553
  236.1 3.6 %collective-permute-done.15 = bf16[2,2,16,1536]{3,2,1,0:T(8,128)(2,1)S(1)} collective-permute-done((bf16[2,2,16,1536]{3,2,1,0:T(8,128)(2,1)S(1)}, bf16[2,2,16,1536]{3,2,1,0:T(8,128)(2,1)S(1)}, u32[]{:S(2)}, u32[]{:S(2)}) %collective-permute-start.15) | collective-permute-done | bytes 196640 | tf_op jit(solution)/shard_map/ppermute | solution.py:553
  246.0 3.6 %collective-permute-done.17 = bf16[16,1536]{1,0:T(8,128)(2,1)S(1)} collective-permute-done((bf16[16,1536]{1,0:T(8,128)(2,1)S(1)}, bf16[16,1536]{1,0:T(8,128)(2,1)S(1)}, u32[]{:S(2)}, u32[]{:S(2)}) %collective-permute-start.17) | collective-permute-done | bytes 49184 | tf_op jit(solution)/shard_map/ppermute | solution.py:553
  250.9 2.3 collective-permute-start.29
  258.7 2.3 collective-permute-done.21
  261.1 4.2 %collective-permute-done.29 = bf16[2,2,1,16,4736]{4,3,2,1,0:T(8,128)(2,1)S(1)} collective-permute-done((bf16[2,2,1,16,4736]{4,3,2,1,0:T(8,128)(2,1)S(1)}, bf16[2,2,1,16,4736]{4,3,2,1,0:T(8,128)(2,1)S(1)}, u32[]{:S(2)}, u32[]{:S(2)}) %collective-permute-start.29) | collective-permute-done | bytes 606240 | tf_op jit(solution)/shard_map/ppermute | solution.py:553
  267.2 3.3 %shard_map.259 = f32[1024,512]{1,0:T(8,128)} custom-call(bf16[512,1536]{1,0:T(8,128)(2,1)S(1)} %bitcast.128, f32[512,1024]{1,0:T(8,128)S(1)} %copy-done.7, bf16[3,128,1024]{2,1,0:T(8,128)(2,1)S(1)} %shard_map.253.refs_1_.refs_7_.refs_2_, bf16[3,128,1024]{2,1,0:T(8,128)(2,1)S(1)} %get-tuple-element.153.refs_5_.refs_1_.refs_3_, ...), custom_call_target="tpu_custom_call" | custom-call | flops 5000000000 | bytes 15000000 | tf_op jit(solution)/shard_map/pallas_call | solution.py:537
  271.4 2.6 collective-permute-done.31
  (209 shorter events, 73.8 us)
Async XLA Ops:
  4.4 12.4 %collective-permute-start = (bf16[1,128,1536]{2,1,0:T(8,128)(2,1)}, bf16[1,128,1536]{2,1,0:T(8,128)(2,1)}, u32[]{:S(2)}, u32[]{:S(2)}) collective-permute-start(bf16[1,128,1536]{2,1,0:T(8,128)(2,1)} %pad_maximum_fusion.3), channel_id=1, source_target_pairs={{0,1},{1,0},{2,3},{3,2},{4,5},{5,4},{6,7},{7,6},{8,9},{9,8},{10,11... | collective-permute-start | bytes 1179656 | tf_op jit(solution)/shard_map/ppermute | solution.py:553
  18.6 17.9 %collective-permute-start.2 = (bf16[1,128,2688]{2,1,0:T(8,128)(2,1)S(1)}, bf16[1,128,2688]{2,1,0:T(8,128)(2,1)S(1)}, u32[]{:S(2)}, u32[]{:S(2)}) collective-permute-start(bf16[1,128,2688]{2,1,0:T(8,128)(2,1)S(1)} %pad_maximum_fusion), channel_id=1, source_target_pairs={{0,1},{1,0},{2,3},{3,2},{4,5},{5,4},{6,7},{7,6},{8,9},{9,8},{10,11... | collective-permute-start | bytes 2064392 | tf_op jit(solution)/shard_map/ppermute | solution.py:553
  36.8 14.8 %collective-permute-start.3 = (bf16[2,128,2688]{2,1,0:T(8,128)(2,1)S(1)}, bf16[2,128,2688]{2,1,0:T(8,128)(2,1)S(1)}, u32[]{:S(2)}, u32[]{:S(2)}) collective-permute-start(bf16[2,128,2688]{2,1,0:T(8,128)(2,1)S(1)} %maximum_select_fusion.3), channel_id=1, source_target_pairs={{0,2},{2,0},{4,6},{6,4},{8,10},{10,8},{12,14},{14,12},{16,18},{18,... | collective-permute-start | bytes 4128776 | tf_op jit(solution)/shard_map/ppermute | solution.py:553
  36.9 14.4 %collective-permute-start.4 = (bf16[1,128,2048]{2,1,0:T(8,128)(2,1)S(1)}, bf16[1,128,2048]{2,1,0:T(8,128)(2,1)S(1)}, u32[]{:S(2)}, u32[]{:S(2)}) collective-permute-start(bf16[1,128,2048]{2,1,0:T(8,128)(2,1)S(1)} %pad_maximum_fusion.2), channel_id=1, source_target_pairs={{0,1},{1,0},{2,3},{3,2},{4,5},{5,4},{6,7},{7,6},{8,9},{9,8},{10,11... | collective-permute-start | bytes 1572872 | tf_op jit(solution)/shard_map/ppermute | solution.py:553
  51.5 10.1 %collective-permute-start.5 = (bf16[2,128,2048]{2,1,0:T(8,128)(2,1)S(1)}, bf16[2,128,2048]{2,1,0:T(8,128)(2,1)S(1)}, u32[]{:S(2)}, u32[]{:S(2)}) collective-permute-start(bf16[2,128,2048]{2,1,0:T(8,128)(2,1)S(1)} %maximum_select_fusion.5), channel_id=1, source_target_pairs={{0,2},{2,0},{4,6},{6,4},{8,10},{10,8},{12,14},{14,12},{16,18},{18,... | collective-permute-start | bytes 3145736 | tf_op jit(solution)/shard_map/ppermute | solution.py:553
  164.6 3.6 %collective-permute-start.6 = (bf16[256,2688]{1,0:T(8,128)(2,1)}, bf16[256,2688]{1,0:T(8,128)(2,1)}, u32[]{:S(2)}, u32[]{:S(2)}) collective-permute-start(bf16[256,2688]{1,0:T(8,128)(2,1)} %get-tuple-element.149), channel_id=1, source_target_pairs={{0,2},{2,0},{4,6},{6,4},{8,10},{10,8},{12,14},{14,12},{16,18},{18,... | collective-permute-start | bytes 4128776 | tf_op jit(solution)/shard_map/ppermute | solution.py:553
  170.1 17.8 %collective-permute-start.7 = (bf16[2,2,2,16,2688]{4,3,2,1,0:T(8,128)(2,1)S(1)}, bf16[2,2,2,16,2688]{4,3,2,1,0:T(8,128)(2,1)S(1)}, u32[]{:S(2)}, u32[]{:S(2)}) collective-permute-start(bf16[2,2,2,16,2688]{4,3,2,1,0:T(8,128)(2,1)S(1)} %get-tuple-element.167.refs_4_), channel_id=1, source_target_pairs={{0,1},{1,0},{2,3},{3,2},{4,5},{5,4},{6,7},{7,6},{8,9},{9,8},{10,11... | collective-permute-start | bytes 2064392 | tf_op jit(solution)/shard_map/ppermute | solution.py:553
  177.7 12.2 %collective-permute-start.8 = (bf16[256,2048]{1,0:T(8,128)(2,1)S(1)}, bf16[256,2048]{1,0:T(8,128)(2,1)S(1)}, u32[]{:S(2)}, u32[]{:S(2)}) collective-permute-start(bf16[256,2048]{1,0:T(8,128)(2,1)S(1)} %get-tuple-element.150.refs_5_), channel_id=1, source_target_pairs={{0,2},{2,0},{4,6},{6,4},{8,10},{10,8},{12,14},{14,12},{16,18},{18,... | collective-permute-start | bytes 3145736 | tf_op jit(solution)/shard_map/ppermute | solution.py:553
  188.1 14.9 %collective-permute-start.11 = (bf16[2,2,16,2688]{3,2,1,0:T(8,128)(2,1)S(1)}, bf16[2,2,16,2688]{3,2,1,0:T(8,128)(2,1)S(1)}, u32[]{:S(2)}, u32[]{:S(2)}) collective-permute-start(bf16[2,2,16,2688]{3,2,1,0:T(8,128)(2,1)S(1)} %get-tuple-element.185.refs_9_), channel_id=1, source_target_pairs={{0,4},{2,6},{4,0},{6,2},{8,12},{10,14},{12,8},{14,10},{16,20},{18,... | collective-permute-start | bytes 1032200 | tf_op jit(solution)/shard_map/ppermute | solution.py:553
  190.5 14.1 %collective-permute-start.9 = (bf16[2,2,2,16,2048]{4,3,1,0,2:T(8,128)(2,1)S(1)}, bf16[2,2,2,16,2048]{4,3,1,0,2:T(8,128)(2,1)S(1)}, u32[]{:S(2)}, u32[]{:S(2)}) collective-permute-start(bf16[2,2,2,16,2048]{4,3,1,0,2:T(8,128)(2,1)S(1)} %bitcast.148), channel_id=1, source_target_pairs={{0,1},{1,0},{2,3},{3,2},{4,5},{5,4},{6,7},{7,6},{8,9},{9,8},{10,11... | collective-permute-start | bytes 1572872 | tf_op jit(solution)/shard_map/ppermute | solution.py:553
  198.5 4.5 %collective-permute-start.10 = (bf16[256,768]{1,0:T(8,128)(2,1)S(1)}, bf16[256,768]{1,0:T(8,128)(2,1)S(1)}, u32[]{:S(2)}, u32[]{:S(2)}) collective-permute-start(bf16[256,768]{1,0:T(8,128)(2,1)S(1)} %get-tuple-element.158), channel_id=1, source_target_pairs={{0,2},{2,0},{4,6},{6,4},{8,10},{10,8},{12,14},{14,12},{16,18},{18,... | collective-permute-start | bytes 1179656 | tf_op jit(solution)/shard_map/ppermute | solution.py:553
  203.2 8.6 %collective-permute-start.12 = (bf16[2,2,2,16,768]{4,3,1,0,2:T(8,128)(2,1)S(1)}, bf16[2,2,2,16,768]{4,3,1,0,2:T(8,128)(2,1)S(1)}, u32[]{:S(2)}, u32[]{:S(2)}) collective-permute-start(bf16[2,2,2,16,768]{4,3,1,0,2:T(8,128)(2,1)S(1)} %bitcast.149), channel_id=1, source_target_pairs={{0,1},{1,0},{2,3},{3,2},{4,5},{5,4},{6,7},{7,6},{8,9},{9,8},{10,11... | collective-permute-start | bytes 589832 | tf_op jit(solution)/shard_map/ppermute | solution.py:553
  204.7 8.5 %collective-permute-start.22 = (bf16[2,2,16,2048]{3,2,1,0:T(8,128)(2,1)S(1)}, bf16[2,2,16,2048]{3,2,1,0:T(8,128)(2,1)S(1)}, u32[]{:S(2)}, u32[]{:S(2)}) collective-permute-start(bf16[2,2,16,2048]{3,2,1,0:T(8,128)(2,1)S(1)} %dynamic-slice_bitcast_fusion.3.refs_9_), channel_id=1, source_target_pairs={{0,4},{2,6},{4,0},{6,2},{8,12},{10,14},{12,8},{14,10},{16,20},{18,... | collective-permute-start | bytes 786440 | tf_op jit(solution)/shard_map/ppermute | solution.py:553
  211.8 6.0 %collective-permute-start.13 = (bf16[256,768]{1,0:T(8,128)(2,1)S(1)}, bf16[256,768]{1,0:T(8,128)(2,1)S(1)}, u32[]{:S(2)}, u32[]{:S(2)}) collective-permute-start(bf16[256,768]{1,0:T(8,128)(2,1)S(1)} %get-tuple-element.161), channel_id=1, source_target_pairs={{0,2},{2,0},{4,6},{6,4},{8,10},{10,8},{12,14},{14,12},{16,18},{18,... | collective-permute-start | bytes 1179656 | tf_op jit(solution)/shard_map/ppermute | solution.py:553
  213.4 7.2 %collective-permute-start.23 = (bf16[16,4736]{1,0:T(8,128)(2,1)S(1)}, bf16[16,4736]{1,0:T(8,128)(2,1)S(1)}, u32[]{:S(2)}, u32[]{:S(2)}) collective-permute-start(bf16[16,4736]{1,0:T(8,128)(2,1)S(1)} %get-tuple-element.186), channel_id=1, source_target_pairs={{0,8},{2,10},{4,12},{6,14},{8,0},{10,2},{12,4},{14,6},{16,24},{18,... | collective-permute-start | bytes 454664 | tf_op jit(solution)/shard_map/ppermute | solution.py:553
  215.0 14.0 %collective-permute-start.24 = (bf16[16,4736]{1,0:T(8,128)(2,1)S(1)}, bf16[16,4736]{1,0:T(8,128)(2,1)S(1)}, u32[]{:S(2)}, u32[]{:S(2)}) collective-permute-start(bf16[16,4736]{1,0:T(8,128)(2,1)S(1)} %get-tuple-element.188), channel_id=1, source_target_pairs={{0,16},{2,18},{4,20},{6,22},{8,24},{10,26},{12,28},{14,30},{16,0},... | collective-permute-start | bytes 454664 | tf_op jit(solution)/shard_map/ppermute | solution.py:553
  217.6 11.4 %collective-permute-start.25 = (bf16[16,4736]{1,0:T(8,128)(2,1)S(1)}, bf16[16,4736]{1,0:T(8,128)(2,1)S(1)}, u32[]{:S(2)}, u32[]{:S(2)}) collective-permute-start(bf16[16,4736]{1,0:T(8,128)(2,1)S(1)} %get-tuple-element.187), channel_id=1, source_target_pairs={{0,24},{2,26},{4,28},{6,30},{8,16},{10,18},{12,20},{14,22},{16,8},... | collective-permute-start | bytes 454664 | tf_op jit(solution)/shard_map/ppermute | solution.py:553
  218.0 15.9 %collective-permute-start.14 = (bf16[2,2,2,16,768]{4,3,1,0,2:T(8,128)(2,1)S(1)}, bf16[2,2,2,16,768]{4,3,1,0,2:T(8,128)(2,1)S(1)}, u32[]{:S(2)}, u32[]{:S(2)}) collective-permute-start(bf16[2,2,2,16,768]{4,3,1,0,2:T(8,128)(2,1)S(1)} %bitcast.150), channel_id=1, source_target_pairs={{0,1},{1,0},{2,3},{3,2},{4,5},{5,4},{6,7},{7,6},{8,9},{9,8},{10,11... | collective-permute-start | bytes 589832 | tf_op jit(solution)/shard_map/ppermute | solution.py:553
  229.1 6.9 %collective-permute-start.26 = (bf16[16,4736]{1,0:T(8,128)(2,1)S(1)}, bf16[16,4736]{1,0:T(8,128)(2,1)S(1)}, u32[]{:S(2)}, u32[]{:S(2)}) collective-permute-start(bf16[16,4736]{1,0:T(8,128)(2,1)S(1)} %fusion.12), channel_id=1, source_target_pairs={{0,8},{2,10},{4,12},{6,14},{8,0},{10,2},{12,4},{14,6},{16,24},{18,... | collective-permute-start | bytes 454664 | tf_op jit(solution)/shard_map/ppermute | solution.py:553
  231.4 14.4 %collective-permute-start.27 = (bf16[16,4736]{1,0:T(8,128)(2,1)S(1)}, bf16[16,4736]{1,0:T(8,128)(2,1)S(1)}, u32[]{:S(2)}, u32[]{:S(2)}) collective-permute-start(bf16[16,4736]{1,0:T(8,128)(2,1)S(1)} %fusion.12), channel_id=1, source_target_pairs={{0,16},{2,18},{4,20},{6,22},{8,24},{10,26},{12,28},{14,30},{16,0},... | collective-permute-start | bytes 454664 | tf_op jit(solution)/shard_map/ppermute | solution.py:553
  232.5 13.3 %collective-permute-start.28 = (bf16[16,4736]{1,0:T(8,128)(2,1)S(1)}, bf16[16,4736]{1,0:T(8,128)(2,1)S(1)}, u32[]{:S(2)}, u32[]{:S(2)}) collective-permute-start(bf16[16,4736]{1,0:T(8,128)(2,1)S(1)} %fusion.12), channel_id=1, source_target_pairs={{0,24},{2,26},{4,28},{6,30},{8,16},{10,18},{12,20},{14,22},{16,8},... | collective-permute-start | bytes 454664 | tf_op jit(solution)/shard_map/ppermute | solution.py:553
  233.9 5.7 %collective-permute-start.15 = (bf16[2,2,16,1536]{3,2,1,0:T(8,128)(2,1)S(1)}, bf16[2,2,16,1536]{3,2,1,0:T(8,128)(2,1)S(1)}, u32[]{:S(2)}, u32[]{:S(2)}) collective-permute-start(bf16[2,2,16,1536]{3,2,1,0:T(8,128)(2,1)S(1)} %fusion.17.refs_6_), channel_id=1, source_target_pairs={{0,4},{2,6},{4,0},{6,2},{8,12},{10,14},{12,8},{14,10},{16,20},{18,... | collective-permute-start | bytes 589832 | tf_op jit(solution)/shard_map/ppermute | solution.py:553
  239.8 6.2 %collective-permute-start.16 = (bf16[16,1536]{1,0:T(8,128)(2,1)S(1)}, bf16[16,1536]{1,0:T(8,128)(2,1)S(1)}, u32[]{:S(2)}, u32[]{:S(2)}) collective-permute-start(bf16[16,1536]{1,0:T(8,128)(2,1)S(1)} %get-tuple-element.205), channel_id=1, source_target_pairs={{0,8},{2,10},{4,12},{6,14},{8,0},{10,2},{12,4},{14,6},{16,24},{18,... | collective-permute-start | bytes 147464 | tf_op jit(solution)/shard_map/ppermute | solution.py:553
  240.8 8.8 %collective-permute-start.17 = (bf16[16,1536]{1,0:T(8,128)(2,1)S(1)}, bf16[16,1536]{1,0:T(8,128)(2,1)S(1)}, u32[]{:S(2)}, u32[]{:S(2)}) collective-permute-start(bf16[16,1536]{1,0:T(8,128)(2,1)S(1)} %get-tuple-element.207), channel_id=1, source_target_pairs={{0,16},{2,18},{4,20},{6,22},{8,24},{10,26},{12,28},{14,30},{16,0},... | collective-permute-start | bytes 147464 | tf_op jit(solution)/shard_map/ppermute | solution.py:553
  242.8 6.8 %collective-permute-start.18 = (bf16[16,1536]{1,0:T(8,128)(2,1)S(1)}, bf16[16,1536]{1,0:T(8,128)(2,1)S(1)}, u32[]{:S(2)}, u32[]{:S(2)}) collective-permute-start(bf16[16,1536]{1,0:T(8,128)(2,1)S(1)} %get-tuple-element.206), channel_id=1, source_target_pairs={{0,24},{2,26},{4,28},{6,30},{8,16},{10,18},{12,20},{14,22},{16,8},... | collective-permute-start | bytes 147464 | tf_op jit(solution)/shard_map/ppermute | solution.py:553
  249.6 6.9 %collective-permute-start.19 = (bf16[16,1536]{1,0:T(8,128)(2,1)S(1)}, bf16[16,1536]{1,0:T(8,128)(2,1)S(1)}, u32[]{:S(2)}, u32[]{:S(2)}) collective-permute-start(bf16[16,1536]{1,0:T(8,128)(2,1)S(1)} %fusion.20), channel_id=1, source_target_pairs={{0,8},{2,10},{4,12},{6,14},{8,0},{10,2},{12,4},{14,6},{16,24},{18,... | collective-permute-start | bytes 147464 | tf_op jit(solution)/shard_map/ppermute | solution.py:553
  250.9 14.3 %collective-permute-start.29 = (bf16[2,2,1,16,4736]{4,3,2,1,0:T(8,128)(2,1)S(1)}, bf16[2,2,1,16,4736]{4,3,2,1,0:T(8,128)(2,1)S(1)}, u32[]{:S(2)}, u32[]{:S(2)}) collective-permute-start(bf16[2,2,1,16,4736]{4,3,2,1,0:T(8,128)(2,1)S(1)} %maximum_select_fusion.8), channel_id=1, source_target_pairs={{0,4},{2,6},{4,0},{6,2},{8,12},{10,14},{12,8},{14,10},{16,20},{18,... | collective-permute-start | bytes 1818632 | tf_op jit(solution)/shard_map/ppermute | solution.py:553
  253.2 5.5 %collective-permute-start.20 = (bf16[16,1536]{1,0:T(8,128)(2,1)S(1)}, bf16[16,1536]{1,0:T(8,128)(2,1)S(1)}, u32[]{:S(2)}, u32[]{:S(2)}) collective-permute-start(bf16[16,1536]{1,0:T(8,128)(2,1)S(1)} %fusion.20), channel_id=1, source_target_pairs={{0,16},{2,18},{4,20},{6,22},{8,24},{10,26},{12,28},{14,30},{16,0},... | collective-permute-start | bytes 147464 | tf_op jit(solution)/shard_map/ppermute | solution.py:553
  255.1 5.9 %collective-permute-start.21 = (bf16[16,1536]{1,0:T(8,128)(2,1)S(1)}, bf16[16,1536]{1,0:T(8,128)(2,1)S(1)}, u32[]{:S(2)}, u32[]{:S(2)}) collective-permute-start(bf16[16,1536]{1,0:T(8,128)(2,1)S(1)} %fusion.20), channel_id=1, source_target_pairs={{0,24},{2,26},{4,28},{6,30},{8,16},{10,18},{12,20},{14,22},{16,8},... | collective-permute-start | bytes 147464 | tf_op jit(solution)/shard_map/ppermute | solution.py:553
  265.4 5.7 %collective-permute-start.30 = (bf16[2,2,1,16,1536]{4,3,1,0,2:T(8,128)(2,1)S(1)}, bf16[2,2,1,16,1536]{4,3,1,0,2:T(8,128)(2,1)S(1)}, u32[]{:S(2)}, u32[]{:S(2)}) collective-permute-start(bf16[2,2,1,16,1536]{4,3,1,0,2:T(8,128)(2,1)S(1)} %bitcast.135), channel_id=1, source_target_pairs={{0,4},{2,6},{4,0},{6,2},{8,12},{10,14},{12,8},{14,10},{16,20},{18,... | collective-permute-start | bytes 589832 | tf_op jit(solution)/shard_map/ppermute | solution.py:553
  270.6 6.3 %collective-permute-start.32 = (bf16[128,4736]{1,0:T(8,128)(2,1)S(1)}, bf16[128,4736]{1,0:T(8,128)(2,1)S(1)}, u32[]{:S(2)}, u32[]{:S(2)}) collective-permute-start(bf16[128,4736]{1,0:T(8,128)(2,1)S(1)} %bitcast.115), channel_id=1, source_target_pairs={{0,2},{2,0},{4,6},{6,4},{8,10},{10,8},{12,14},{14,12},{16,18},{18,... | collective-permute-start | bytes 3637256 | tf_op jit(solution)/shard_map/ppermute | solution.py:553
  271.3 2.8 collective-permute-start.31
  (33 other events, 206.5 us)
